TPU v7x, 32 devices: a whole 2x2x4 slice. The times are simulated.
32 devices in a mesh: run: 2 (over x), blk: 4 (over y, core), grp: 4 (over z).
Axes of the slice: x: 2, y: 2, z: 4, core: 2. Of those that a mesh axis runs over, the one named last changes fastest.
Arguments:
- a_gate: bfloat16 [7168, 4096], P('blk', ('run', 'grp')), may hold values from -6 to 6
- a_up: bfloat16 [7168, 4096], P('blk', ('run', 'grp')), may hold values from -6 to 6
- a_down: bfloat16 [7168, 4096], P('blk', ('run', 'grp')), may hold values from -6 to 6
- b_gate: bfloat16 [14336, 4096], P(('run', 'grp'), 'blk'), may hold values from -6 to 6
- b_up: bfloat16 [14336, 4096], P(('run', 'grp'), 'blk'), may hold values from -6 to 6
- b_down: bfloat16 [14336, 4096], P(('run', 'grp'), 'blk'), may hold values from -6 to 6
Outputs:
- cost: float32 [7168, 14336], P('blk', ('run', 'grp'))
All inputs are finite; a program needn't handle non-finite values.
Results may differ from a plain program's by a relative error of at most 0.0003.
Values may be sent and summed in bfloat16 or wider, within the bound.
No kernel may reach another device: no remote copies, remote signals or barrier semaphores. Data moves between devices by JAX's collectives and lax.ppermute only.
A program may use at most 192 MiB of HBM per device.

v0:
```python
import math

import jax
import jax.numpy as jnp
from jax import lax
from jax.sharding import PartitionSpec as P


def pair_term(left, right):
    return lax.dot_general(
        left, right, (((1,), (1,)), ((), ())), preferred_element_type=jnp.float32
    )


def add_piece(total, whole, piece):
    return total + pair_term(whole, piece)


def local(a_gate, a_up, a_down, b_gate, b_up, b_down):
    a_full = (
        lax.all_gather(a_gate, ("run", "grp"), axis=1, tiled=True),
        lax.all_gather(a_up, ("run", "grp"), axis=1, tiled=True),
        lax.all_gather(a_down, ("run", "grp"), axis=1, tiled=True),
    )
    width = a_full[0].shape[1]
    empty = jnp.zeros((a_gate.shape[0], b_gate.shape[0]), jnp.float32)
    total = add_piece(empty, a_full[0], lax.all_gather(b_gate, "blk", axis=1, tiled=True))
    total = add_piece(total, a_full[1], lax.all_gather(b_up, "blk", axis=1, tiled=True))
    total = add_piece(total, a_full[2], lax.all_gather(b_down, "blk", axis=1, tiled=True))
    return total * (1.0 / math.sqrt(3.0 * width))


def solution(mesh):
    placed = (
        P("blk", ("run", "grp")),
        P("blk", ("run", "grp")),
        P("blk", ("run", "grp")),
        P(("run", "grp"), "blk"),
        P(("run", "grp"), "blk"),
        P(("run", "grp"), "blk"),
    )
    return jax.shard_map(
        local, mesh=mesh, in_specs=placed, out_specs=P("blk", ("run", "grp")), check_vma=False
    )
```

profile of v0, /device:TPU:0, one launch (start us, length us, event | category | flops | bytes accessed | tf_op | source)
XLA Modules:
  0.0 949.3 jit_solution(16626155114051708869)
XLA Ops:
  6.5 0.0 all-gather.9.cloned.1.call-start
  6.5 0.7 all-gather.9.cloned.1.call-update
  7.3 0.0 all-gather.7.cloned.1.call-start
  7.3 0.7 all-gather.7.cloned.1.call-update
  8.0 0.0 all-gather.13.cloned.1.call-start
  8.1 0.7 all-gather.13.cloned.1.call-update
  8.7 0.0 all-gather.11.cloned.1.call-start
  8.8 0.5 all-gather.11.cloned.1.call-update
  9.3 0.0 all-gather.17.cloned.1.call-start
  9.4 0.5 all-gather.17.cloned.1.call-update
  9.9 0.0 all-gather.15.cloned.1.call-start
  9.9 0.5 all-gather.15.cloned.1.call-update
  10.5 95.2 %all-gather.9.cloned.1.call-done = bf16[1792,4096]{1,0:T(8,128)(2,1)} async-done(((bf16[1792,1024]{1,0:T(8,128)(2,1)}), bf16[1792,4096]{1,0:T(8,128)(2,1)}) %all-gather.9.cloned.1.call-update) | async-done | bytes 14680080 | tf_op jit(solution)/shard_map/all_gather | solution.py:27
  105.7 204.2 %all-gather.7.cloned.1.call-done = bf16[1792,4096]{1,0:T(8,128)(2,1)} async-done(((bf16[1792,512]{1,0:T(8,128)(2,1)}), bf16[1792,4096]{1,0:T(8,128)(2,1)}) %all-gather.7.cloned.1.call-update) | async-done | bytes 14680080 | tf_op jit(solution)/shard_map/all_gather | solution.py:21
  309.9 35.7 %fusion = f32[1792,1792]{1,0:T(8,128)} fusion(bf16[1792,4096]{1,0:T(8,128)(2,1)} %all-gather.7.cloned.1.call-done, bf16[1792,4096]{1,0:T(8,128)(2,1)} %all-gather.9.cloned.1.call-done), kind=kOutput, calls=%fused_computation.1 | convolution fusion | flops 26306674688 | bytes 42205184 | tf_op jit(solution)/shard_map/dot_general | solution.py:10
  345.5 58.1 %all-gather.13.cloned.1.call-done = bf16[1792,4096]{1,0:T(8,128)(2,1)} async-done(((bf16[1792,1024]{1,0:T(8,128)(2,1)}), bf16[1792,4096]{1,0:T(8,128)(2,1)}) %all-gather.13.cloned.1.call-update) | async-done | bytes 14680080 | tf_op jit(solution)/shard_map/all_gather | solution.py:28
  403.7 204.1 %all-gather.11.cloned.1.call-done = bf16[1792,4096]{1,0:T(8,128)(2,1)} async-done(((bf16[1792,512]{1,0:T(8,128)(2,1)}), bf16[1792,4096]{1,0:T(8,128)(2,1)}) %all-gather.11.cloned.1.call-update) | async-done | bytes 14680080 | tf_op jit(solution)/shard_map/all_gather | solution.py:22
  607.7 35.8 %fusion.1 = f32[1792,1792]{1,0:T(8,128)} fusion(bf16[1792,4096]{1,0:T(8,128)(2,1)} %all-gather.11.cloned.1.call-done, bf16[1792,4096]{1,0:T(8,128)(2,1)} %all-gather.13.cloned.1.call-done), kind=kOutput, calls=%fused_computation.2 | convolution fusion | flops 26306674688 | bytes 42205184 | tf_op jit(solution)/shard_map/dot_general | solution.py:10
  643.5 57.9 %all-gather.17.cloned.1.call-done = bf16[1792,4096]{1,0:T(8,128)(2,1)} async-done(((bf16[1792,1024]{1,0:T(8,128)(2,1)}), bf16[1792,4096]{1,0:T(8,128)(2,1)}) %all-gather.17.cloned.1.call-update) | async-done | bytes 14680080 | tf_op jit(solution)/shard_map/all_gather | solution.py:29
  701.4 204.1 %all-gather.15.cloned.1.call-done = bf16[1792,4096]{1,0:T(8,128)(2,1)} async-done(((bf16[1792,512]{1,0:T(8,128)(2,1)}), bf16[1792,4096]{1,0:T(8,128)(2,1)}) %all-gather.15.cloned.1.call-update) | async-done | bytes 14680080 | tf_op jit(solution)/shard_map/all_gather | solution.py:23
  905.4 37.0 %add_multiply_fusion = f32[1792,1792]{1,0:T(8,128)} fusion(f32[1792,1792]{1,0:T(8,128)} %fusion, f32[1792,1792]{1,0:T(8,128)} %fusion.1, bf16[1792,4096]{1,0:T(8,128)(2,1)} %all-gather.15.cloned.1.call-done, bf16[1792,4096]{1,0:T(8,128)(2,1)} %all-gather.17.cloned.1.call-done), kind=kOutput, calls=%fused_computation | convolution fusion | flops 26316308480 | bytes 67895296 | tf_op jit(solution)/shard_map/dot_general | solution.py:10
Async XLA Ops:
  6.5 99.1 %all-gather.9.cloned.1.call-start = ((), (), s32[]{:S(2)}) async-start(), calls=%async_computation.1 | async-start | bytes 18350080 | tf_op jit(solution)/shard_map/all_gather | solution.py:27
  7.3 302.6 %all-gather.7.cloned.1.call-start = ((), (), s32[]{:S(2)}) async-start(), calls=%async_computation | async-start | bytes 16515072 | tf_op jit(solution)/shard_map/all_gather | solution.py:21
  8.0 395.7 %all-gather.13.cloned.1.call-start = ((), (), s32[]{:S(2)}) async-start(), calls=%async_computation.3 | async-start | bytes 18350080 | tf_op jit(solution)/shard_map/all_gather | solution.py:28
  8.7 599.0 %all-gather.11.cloned.1.call-start = ((), (), s32[]{:S(2)}) async-start(), calls=%async_computation.2 | async-start | bytes 16515072 | tf_op jit(solution)/shard_map/all_gather | solution.py:22
  9.3 692.1 %all-gather.17.cloned.1.call-start = ((), (), s32[]{:S(2)}) async-start(), calls=%async_computation.5 | async-start | bytes 18350080 | tf_op jit(solution)/shard_map/all_gather | solution.py:29
  9.9 895.5 %all-gather.15.cloned.1.call-start = ((), (), s32[]{:S(2)}) async-start(), calls=%async_computation.4 | async-start | bytes 16515072 | tf_op jit(solution)/shard_map/all_gather | solution.py:23
Sparse Core Ops, SparseCore 0:
  8.9 96.7 all-gather.8
  107.7 202.1 all-gather.6
  311.4 92.1 all-gather.12
  405.5 202.1 all-gather.10
  609.1 92.1 all-gather.16
  703.2 202.1 all-gather.14
where the time goes:
time: 949 us
  waiting for transfers between devices  827 us (87%)
  matrix products  108 us (11%)
  between operations  13.5 us (1%)
    all_gather x1, waiting for transfers between devices, local(): lax.all_gather(a_gate, ('run', 'grp'), axis=1, tiled=True)  204 us
    all_gather x1, waiting for transfers between devices, local(): lax.all_gather(a_up, ('run', 'grp'), axis=1, tiled=True)  204 us
    all_gather x1, waiting for transfers between devices, local(): lax.all_gather(a_down, ('run', 'grp'), axis=1, tiled=True)  204 us
    dot_general x3, matrix products, pair_term(): lax.dot_general(left, right, (((1,), (1,)), ((), ())), preferred_element_...  108 us
    all_gather x1, waiting for transfers between devices, local(): lax.all_gather(b_gate, 'blk', axis=1, tiled=True)  95.2 us
    all_gather x1, waiting for transfers between devices, local(): lax.all_gather(b_up, 'blk', axis=1, tiled=True)  58.1 us
    all_gather x1, waiting for transfers between devices, local(): lax.all_gather(b_down, 'blk', axis=1, tiled=True)  57.9 us
  transfers between devices with their start and end apart: 6, of which 6 were waited for; matrix products, arithmetic and copies ran while one was open for 8% of the time, Pallas kernels for 0%

commit v1 on v0

v1 whole, which is shorter than its diff:
```python
import functools
import math

import jax
import jax.numpy as jnp
from jax import lax
from jax.experimental import pallas as pl
from jax.experimental.pallas import tpu as pltpu
from jax.sharding import PartitionSpec as P


def ring_order(n):
    return list(range(0, n, 2)) + list(range(1, n, 2))[::-1]


def ring_step(value, order, axis):
    n = len(order)
    return lax.ppermute(value, axis, [(order[i], order[(i + 1) % n]) for i in range(n)])


def shift(value, by, n, axis):
    return lax.ppermute(value, axis, [(i, (i + by) % n) for i in range(n)])


def tile(extent, most):
    return max(t for t in range(128, most + 1, 128) if extent % t == 0)


def add_terms_body(count, first, scale, cols_ref, *refs):
    lefts, rights = refs[:count], refs[count : 2 * count]
    out = refs[-1]
    total = None if first else refs[2 * count][...]
    for left, right in zip(lefts, rights):
        term = lax.dot_general(
            left[...], right[...], (((1,), (1,)), ((), ())), preferred_element_type=jnp.float32
        )
        total = term if total is None else total + term
    out[...] = total if scale is None else total * scale


def add_terms(total, pieces, scale=None):
    rows, across = pieces[0][0].shape[0], pieces[0][1].shape[0]
    tm, tn = tile(rows, 896), tile(across, 896)
    count, first = len(pieces), total is None
    in_specs = [
        pl.BlockSpec((tm, a.shape[1]), lambda i, j, cols: (i, 0)) for a, _, _ in pieces
    ] + [
        pl.BlockSpec((tn, a.shape[1]), functools.partial(lambda p, i, j, cols: (j, cols[p]), p))
        for p, (a, _, _) in enumerate(pieces)
    ]
    place = pl.BlockSpec((tm, tn), lambda i, j, cols: (i, j))
    operands = [a for a, _, _ in pieces] + [b for _, b, _ in pieces]
    if not first:
        in_specs.append(place)
        operands.append(total)
    deep = sum(a.shape[1] for a, _, _ in pieces)
    return pl.pallas_call(
        functools.partial(add_terms_body, count, first, scale),
        grid_spec=pltpu.PrefetchScalarGridSpec(
            num_scalar_prefetch=1,
            grid=(rows // tm, across // tn),
            in_specs=in_specs,
            out_specs=place,
        ),
        out_shape=jax.ShapeDtypeStruct((rows, across), jnp.float32),
        input_output_aliases={} if first else {2 * count + 1: 0},
        compiler_params=pltpu.CompilerParams(vmem_limit_bytes=48 * 1024 * 1024),
        cost_estimate=pl.CostEstimate(
            flops=2 * rows * across * deep,
            bytes_accessed=2 * deep * (rows + across) + (4 if first else 8) * rows * across,
            transcendentals=0,
        ),
    )(jnp.stack([c for _, _, c in pieces]), *operands)


def make_local(runs, grps):
    order = ring_order(grps)
    place = [order.index(i) for i in range(grps)]
    came_from = [[order[(place[g] - s) % grps] for g in range(grps)] for s in range(grps)]

    def local(a_gate, a_up, a_down, b_gate, b_up, b_down):
        depth = a_gate.shape[1]
        width = depth * runs * grps
        half = depth // 2
        run = lax.axis_index("run")
        grp = lax.axis_index("grp")
        b_full = [lax.all_gather(b, "blk", axis=1, tiled=True) for b in (b_gate, b_up, b_down)]

        def block(r, s):
            return lax.rem(run - r + runs, runs) * grps + jnp.array(came_from[s], jnp.int32)[grp]

        def ring_first(piece):
            got = []
            held = piece
            for s in range(grps):
                got.append([(held, 0, s)])
                for r in range(1, runs):
                    got[-1].append((shift(held, r, runs, "run"), r, s))
                if s < grps - 1:
                    held = ring_step(held, order, "grp")
            return got

        def run_first(piece):
            held = [piece] + [shift(piece, r, runs, "run") for r in range(1, runs)]
            got = []
            for s in range(grps):
                got.append([(h, r, s) for r, h in enumerate(held)])
                if s < grps - 1:
                    held = [ring_step(h, order, "grp") for h in held]
            return got

        gate, up = ring_first(a_gate), ring_first(a_up)
        low, high = ring_first(a_down[:, :half]), run_first(a_down[:, half:])
        calls = [[(v, b_full[0], block(r, s)) for v, r, s in g] for g in gate]
        calls += [[(v, b_full[1], block(r, s)) for v, r, s in g] for g in up]
        calls += [
            [(v, b_full[2], 2 * block(r, s)) for v, r, s in g]
            + [(v, b_full[2], 2 * block(r, s) + 1) for v, r, s in h]
            for g, h in zip(low, high)
        ]
        total = None
        for i, pieces in enumerate(calls):
            last = i == len(calls) - 1
            total = add_terms(total, pieces, 1.0 / math.sqrt(3.0 * width) if last else None)
        return total

    return local


def solution(mesh):
    placed = (
        P("blk", ("run", "grp")),
        P("blk", ("run", "grp")),
        P("blk", ("run", "grp")),
        P(("run", "grp"), "blk"),
        P(("run", "grp"), "blk"),
        P(("run", "grp"), "blk"),
    )
    local = make_local(mesh.shape["run"], mesh.shape["grp"])
    return jax.shard_map(
        local, mesh=mesh, in_specs=placed, out_specs=P("blk", ("run", "grp")), check_vma=False
    )
```

time: 949 us -> 502 us (0.53)
  waiting for transfers between devices: 827 us -> 228 us
  Pallas kernels: 0 us -> 200 us
  matrix products: 108 us -> 0 us
  starting transfers between devices: 0.19 us -> 44.7 us
  local copies, waits for them, and re-layouts: 0 us -> 11.1 us
    all_gather x6 -> x3, waiting for transfers between devices: 824 us -> 0.01 us  [local(): lax.all_gather(b, 'blk', axis=1, tiled=True)]
    ppermute x0 -> x28, waiting for transfers between devices: none -> 226 us  [the longest x15 146 us: ring_step(): lax.ppermute(value, axis, [(order[i], order[(i + 1) % n]) for i in range(...]
    pallas_call x0 -> x12, Pallas kernels: none -> 200 us  [add_terms(): pl.pallas_call(functools.partial(add_terms_body, count, first, scale), gr...]
    dot_general x3 -> x0, matrix products: 108 us -> none  [pair_term(): lax.dot_general(left, right, (((1,), (1,)), ((), ())), preferred_element_...]
    ppermute x0 -> x28, starting transfers between devices: none -> 44.6 us  [the longest x15 28.5 us: ring_step(): lax.ppermute(value, axis, [(order[i], order[(i + 1) % n]) for i in range(...]
  transfers between devices with their start and end apart: 6 -> 31, of which waited for: 6 -> 12; matrix products, arithmetic and copies ran while one was open for 8% -> 1% of each run, Pallas kernels for 0% -> 36%
where the time goes in v1:
time: 502 us
  waiting for transfers between devices  228 us (45%)
  Pallas kernels  200 us (40%)
  starting transfers between devices  44.7 us (9%)
  between operations  17.2 us (3%)
  local copies, waits for them, and re-layouts  11.1 us (2%)
    pallas_call x12, Pallas kernels, add_terms(): pl.pallas_call(functools.partial(add_terms_body, count, first, scale), gr...  200 us
    ppermute x15, waiting for transfers between devices, ring_step(): lax.ppermute(value, axis, [(order[i], order[(i + 1) % n]) for i in range(...  146 us
    ppermute x13, waiting for transfers between devices, shift(): return lax.ppermute(value, axis, [(i, (i + by) % n) for i in range(n)])  80.1 us
    ppermute x15, starting transfers between devices, ring_step(): lax.ppermute(value, axis, [(order[i], order[(i + 1) % n]) for i in range(...  28.5 us
    ppermute x13, starting transfers between devices, shift(): return lax.ppermute(value, axis, [(i, (i + by) % n) for i in range(n)])  16.1 us
  transfers between devices with their start and end apart: 31, of which 12 were waited for; matrix products, arithmetic and copies ran while one was open for 1% of the time, Pallas kernels for 36%

profile of v1, /device:TPU:0, one launch (start us, length us, event | category | flops | bytes accessed | tf_op | source)
XLA Modules:
  0.0 502.1 jit_solution(8372132600090962198)
XLA Ops:
  8.8 4.1 collective-permute-start.21
  12.9 39.6 %collective-permute-done.21.refs_0_ = bf16[1792,512]{1,0:T(8,128)(2,1)S(1)} collective-permute-done((bf16[1792,512]{1,0:T(8,128)(2,1)}, bf16[1792,512]{1,0:T(8,128)(2,1)S(1)}, u32[]{:S(2)}, u32[]{:S(2)}) %collective-permute-start.21) | collective-permute-done | bytes 1835040 | tf_op jit(solution)/shard_map/ppermute | solution.py:18
  57.9 38.3 %collective-permute-done.22.refs_0_ = bf16[1792,512]{1,0:T(8,128)(2,1)} collective-permute-done((bf16[1792,512]{1,0:T(8,128)(2,1)S(1)}, bf16[1792,512]{1,0:T(8,128)(2,1)}, u32[]{:S(2)}, u32[]{:S(2)}) %collective-permute-start.22) | collective-permute-done | bytes 1835040 | tf_op jit(solution)/shard_map/ppermute | solution.py:18
  96.2 3.5 collective-permute-start.23
  103.2 32.4 %collective-permute-done.14.refs_0_ = bf16[1792,512]{1,0:T(8,128)(2,1)} collective-permute-done((bf16[1792,512]{1,0:T(8,128)(2,1)S(1)}, bf16[1792,512]{1,0:T(8,128)(2,1)}, u32[]{:S(2)}, u32[]{:S(2)}) %collective-permute-start.14) | collective-permute-done | bytes 1835040 | tf_op jit(solution)/shard_map/ppermute | solution.py:18
  147.2 27.8 %collective-permute-done.23.refs_0_ = bf16[1792,512]{1,0:T(8,128)(2,1)} collective-permute-done((bf16[1792,512]{1,0:T(8,128)(2,1)}, bf16[1792,512]{1,0:T(8,128)(2,1)}, u32[]{:S(2)}, u32[]{:S(2)}) %collective-permute-start.23) | collective-permute-done | bytes 1835040 | tf_op jit(solution)/shard_map/ppermute | solution.py:18
  176.5 14.4 %shard_map.352.refs_4_ = f32[1792,1792]{1,0:T(8,128)} custom-call(s32[2]{0:T(128)S(1)} %pad_add_fusion.7.cols_ref, bf16[1792,512]{1,0:T(8,128)(2,1)} %refs_0_.2, bf16[1792,512]{1,0:T(8,128)(2,1)} %collective-permute-done.27.refs_1_, bf16[1792,4096]{1,0:T(8,128)(2,1)} %all-gather.8.cloned.1.call-done.refs_2_.refs_3_, ...), custom_call_target="tpu_custom_call" | custom-call | flops 6576668672 | bytes 20185088 | tf_op jit(solution)/shard_map/pallas_call | solution.py:57
  190.9 14.7 %collective-permute-done.7.refs_3_ = bf16[1792,256]{1,0:T(8,128)(2,1)S(1)} collective-permute-done((bf16[1792,256]{1,0:T(8,128)(2,1)S(1)}, bf16[1792,256]{1,0:T(8,128)(2,1)S(1)}, u32[]{:S(2)}, u32[]{:S(2)}) %collective-permute-start.7) | collective-permute-done | bytes 917536 | tf_op jit(solution)/shard_map/ppermute | solution.py:22
  207.6 4.6 collective-permute-done.15.refs_0_
  215.6 17.7 %shard_map.353.refs_4_ = f32[1792,1792]{1,0:T(8,128)} custom-call(s32[2]{0:T(128)S(1)} %pad_add_fusion.6.cols_ref, bf16[1792,512]{1,0:T(8,128)(2,1)S(1)} %copy-done.4, bf16[1792,512]{1,0:T(8,128)(2,1)} %collective-permute-done.26.refs_1_, bf16[1792,4096]{1,0:T(8,128)(2,1)} %all-gather.8.cloned.1.call-done.refs_2_.refs_3_, ...), custom_call_target="tpu_custom_call", output_to_operand_aliasing={{}: (5, {})} | custom-call | flops 6576668672 | bytes 33030144 | tf_op jit(solution)/shard_map/pallas_call | solution.py:57
  233.3 17.0 %shard_map.354.refs_4_ = f32[1792,1792]{1,0:T(8,128)} custom-call(s32[2]{0:T(128)S(1)} %pad_add_fusion.5.cols_ref, bf16[1792,512]{1,0:T(8,128)(2,1)} %collective-permute-done.22.refs_0_, bf16[1792,512]{1,0:T(8,128)(2,1)} %collective-permute-done.25.refs_1_, ...), custom_call_target="tpu_custom_call", output_to_operand_aliasing={{}: (5, {})} | custom-call | flops 6576668672 | bytes 33030144 | tf_op jit(solution)/shard_map/pallas_call | solution.py:57
  252.2 17.2 %shard_map.355.refs_4_ = f32[1792,1792]{1,0:T(8,128)} custom-call(s32[2]{0:T(128)S(1)} %pad_add_fusion.4.cols_ref, bf16[1792,512]{1,0:T(8,128)(2,1)} %collective-permute-done.23.refs_0_, bf16[1792,512]{1,0:T(8,128)(2,1)} %collective-permute-done.24.refs_1_, ...), custom_call_target="tpu_custom_call", output_to_operand_aliasing={{}: (5, {})} | custom-call | flops 6576668672 | bytes 33030144 | tf_op jit(solution)/shard_map/pallas_call | solution.py:57
  269.4 3.5 collective-permute-done.refs_0_
  276.4 7.8 %collective-permute-done.20.refs_1_ = bf16[1792,512]{1,0:T(8,128)(2,1)S(1)} collective-permute-done((bf16[1792,512]{1,0:T(8,128)(2,1)S(1)}, bf16[1792,512]{1,0:T(8,128)(2,1)S(1)}, u32[]{:S(2)}, u32[]{:S(2)}) %collective-permute-start.20) | collective-permute-done | bytes 1835040 | tf_op jit(solution)/shard_map/ppermute | solution.py:22
  285.4 38.1 %collective-permute-done.19.refs_1_ = bf16[1792,512]{1,0:T(8,128)(2,1)S(1)} collective-permute-done((bf16[1792,512]{1,0:T(8,128)(2,1)}, bf16[1792,512]{1,0:T(8,128)(2,1)S(1)}, u32[]{:S(2)}, u32[]{:S(2)}) %collective-permute-start.19) | collective-permute-done | bytes 1835040 | tf_op jit(solution)/shard_map/ppermute | solution.py:22
  329.3 15.9 %shard_map.356.refs_4_ = f32[1792,1792]{1,0:T(8,128)} custom-call(s32[2]{0:T(128)S(1)} %pad_add_fusion.7.cols_ref, bf16[1792,512]{1,0:T(8,128)(2,1)S(1)} %copy-done.2, bf16[1792,512]{1,0:T(8,128)(2,1)S(1)} %copy-done.6, bf16[1792,4096]{1,0:T(8,128)(2,1)} %all-gather.6.cloned.1.call-done.refs_2_.refs_3_, ...), custom_call_target="tpu_custom_call", output_to_operand_aliasing={{}: (5, {})} | custom-call | flops 6576668672 | bytes 33030144 | tf_op jit(solution)/shard_map/pallas_call | solution.py:57
  345.2 16.5 %shard_map.357.refs_4_ = f32[1792,1792]{1,0:T(8,128)} custom-call(s32[2]{0:T(128)S(1)} %pad_add_fusion.6.cols_ref, bf16[1792,512]{1,0:T(8,128)(2,1)} %collective-permute-done.14.refs_0_, bf16[1792,512]{1,0:T(8,128)(2,1)S(1)} %copy-done.8, bf16[1792,4096]{1,0:T(8,128)(2,1)} %all-gather.6.cloned.1.call-done.refs_2_.refs_3_, ...), custom_call_target="tpu_custom_call", output_to_operand_aliasing={{}: (5, {})} | custom-call | flops 6576668672 | bytes 33030144 | tf_op jit(solution)/shard_map/pallas_call | solution.py:57
  367.1 17.0 %shard_map.358.refs_4_ = f32[1792,1792]{1,0:T(8,128)} custom-call(s32[2]{0:T(128)S(1)} %pad_add_fusion.5.cols_ref, bf16[1792,512]{1,0:T(8,128)(2,1)} %collective-permute-done.15.refs_0_, bf16[1792,512]{1,0:T(8,128)(2,1)} %collective-permute-done.18.refs_1_, ...), custom_call_target="tpu_custom_call", output_to_operand_aliasing={{}: (5, {})} | custom-call | flops 6576668672 | bytes 33030144 | tf_op jit(solution)/shard_map/pallas_call | solution.py:57
  384.1 18.2 %collective-permute-done.17.refs_1_ = bf16[1792,512]{1,0:T(8,128)(2,1)} collective-permute-done((bf16[1792,512]{1,0:T(8,128)(2,1)}, bf16[1792,512]{1,0:T(8,128)(2,1)}, u32[]{:S(2)}, u32[]{:S(2)}) %collective-permute-start.17) | collective-permute-done | bytes 1835040 | tf_op jit(solution)/shard_map/ppermute | solution.py:22
  403.8 17.0 %shard_map.359.refs_8_ = f32[1792,1792]{1,0:T(8,128)} custom-call(s32[2]{0:T(128)S(1)} %pad_add_fusion.4.cols_ref, bf16[1792,512]{1,0:T(8,128)(2,1)} %collective-permute-done.16.refs_0_, bf16[1792,512]{1,0:T(8,128)(2,1)} %collective-permute-done.17.refs_1_, ...), custom_call_target="tpu_custom_call", output_to_operand_aliasing={{}: (5, {})} | custom-call | flops 6576668672 | bytes 33030144 | tf_op jit(solution)/shard_map/pallas_call | solution.py:57
  427.8 16.0 %shard_map.360.refs_8_ = f32[1792,1792]{1,0:T(8,128)} custom-call(s32[4]{0:T(128)S(1)} %pad_add_fusion.3.cols_ref, bf16[1792,256]{1,0:T(8,128)(2,1)S(1)} %get-tuple-element.6.refs_0_, bf16[1792,256]{1,0:T(8,128)(2,1)S(1)} %copy-done.10, bf16[1792,256]{1,0:T(8,128)(2,1)S(1)} %get-tuple-element.5.refs_2_, ...), custom_call_target="tpu_custom_call", output_to_operand_aliasing={{}: (9, {})} | custom-call | flops 6576668672 | bytes 33030144 | tf_op jit(solution)/shard_map/pallas_call | solution.py:57
  443.8 17.1 %shard_map.361.refs_8_ = f32[1792,1792]{1,0:T(8,128)} custom-call(s32[4]{0:T(128)S(1)} %pad_add_fusion.2.cols_ref, bf16[1792,256]{1,0:T(8,128)(2,1)} %collective-permute-done.refs_0_, bf16[1792,256]{1,0:T(8,128)(2,1)} %collective-permute-done.12.refs_1_, bf16[1792,256]{1,0:T(8,128)(2,1)} %collective-permute-done.4.refs_2_, ...), custom_call_target="tpu_custom_call", output_to_operand_aliasing={{}: (9, {})} | custom-call | flops 6576668672 | bytes 33030144 | tf_op jit(solution)/shard_map/pallas_call | solution.py:57
  461.3 17.1 %shard_map.362.refs_8_ = f32[1792,1792]{1,0:T(8,128)} custom-call(s32[4]{0:T(128)S(1)} %pad_add_fusion.1.cols_ref, bf16[1792,256]{1,0:T(8,128)(2,1)} %collective-permute-done.1.refs_0_, bf16[1792,256]{1,0:T(8,128)(2,1)} %collective-permute-done.11.refs_1_, bf16[1792,256]{1,0:T(8,128)(2,1)} %collective-permute-done.5.refs_2_, ...), custom_call_target="tpu_custom_call", output_to_operand_aliasing={{}: (9, {})} | custom-call | flops 6576668672 | bytes 33030144 | tf_op jit(solution)/shard_map/pallas_call | solution.py:57
  478.4 17.1 %shard_map.363 = f32[1792,1792]{1,0:T(8,128)} custom-call(s32[4]{0:T(128)S(1)} %pad_add_fusion.cols_ref, bf16[1792,256]{1,0:T(8,128)(2,1)} %collective-permute-done.2.refs_0_, bf16[1792,256]{1,0:T(8,128)(2,1)} %collective-permute-done.3.refs_1_, bf16[1792,256]{1,0:T(8,128)(2,1)} %collective-permute-done.6.refs_2_, ...), custom_call_target="tpu_custom_call", output_to_operand_aliasing={{}: (9, {})} | custom-call | flops 6576668672 | bytes 33030144 | tf_op jit(solution)/shard_map/pallas_call | solution.py:57
  (93 shorter events, 52.3 us)
Async XLA Ops:
  6.5 169.9 %all-gather.8.cloned.1.call-start = ((), (), s32[]{:S(2)}) async-start(), calls=%async_computation.2 | async-start | bytes 18350080 | tf_op jit(solution)/shard_map/all_gather | solution.py:87
  7.3 319.0 %all-gather.6.cloned.1.call-start = ((), (), s32[]{:S(2)}) async-start(), calls=%async_computation.1 | async-start | bytes 18350080 | tf_op jit(solution)/shard_map/all_gather | solution.py:87
  8.1 418.6 %all-gather.4.cloned.1.call-start = ((), (), s32[]{:S(2)}) async-start(), calls=%async_computation | async-start | bytes 18350080 | tf_op jit(solution)/shard_map/all_gather | solution.py:87
  55.7 79.8 %collective-permute-start.14 = (bf16[1792,512]{1,0:T(8,128)(2,1)S(1)}, bf16[1792,512]{1,0:T(8,128)(2,1)}, u32[]{:S(2)}, u32[]{:S(2)}) collective-permute-start(bf16[1792,512]{1,0:T(8,128)(2,1)S(1)} %copy-done), channel_id=1, source_target_pairs={{0,2},{2,3},{3,1},{1,0},{4,6},{6,7},{7,5},{5,4},{8,10},{10,11},{11... | collective-permute-start | bytes 5505032 | tf_op jit(solution)/shard_map/ppermute | solution.py:18
  56.4 90.0 %collective-permute-start.27 = (bf16[1792,512]{1,0:T(8,128)(2,1)}, bf16[1792,512]{1,0:T(8,128)(2,1)}, u32[]{:S(2)}, u32[]{:S(2)}) collective-permute-start(bf16[1792,512]{1,0:T(8,128)(2,1)} %refs_0_.2), channel_id=1, source_target_pairs={{0,16},{16,0},{1,17},{17,1},{2,18},{18,2},{3,19},{19,3},{4,20},{20... | collective-permute-start | bytes 5505032 | tf_op jit(solution)/shard_map/ppermute | solution.py:22
  96.2 78.8 %collective-permute-start.23 = (bf16[1792,512]{1,0:T(8,128)(2,1)}, bf16[1792,512]{1,0:T(8,128)(2,1)}, u32[]{:S(2)}, u32[]{:S(2)}) collective-permute-start(bf16[1792,512]{1,0:T(8,128)(2,1)} %collective-permute-done.22.refs_0_), channel_id=1, source_target_pairs={{0,2},{2,3},{3,1},{1,0},{4,6},{6,7},{7,5},{5,4},{8,10},{10,11},{11... | collective-permute-start | bytes 5505032 | tf_op jit(solution)/shard_map/ppermute | solution.py:18
  101.7 105.4 %collective-permute-start.26 = (bf16[1792,512]{1,0:T(8,128)(2,1)}, bf16[1792,512]{1,0:T(8,128)(2,1)}, u32[]{:S(2)}, u32[]{:S(2)}) collective-permute-start(bf16[1792,512]{1,0:T(8,128)(2,1)} %copy-done.3), channel_id=1, source_target_pairs={{0,16},{16,0},{1,17},{17,1},{2,18},{18,2},{3,19},{19,3},{4,20},{20... | collective-permute-start | bytes 5505032 | tf_op jit(solution)/shard_map/ppermute | solution.py:22
  135.5 76.7 %collective-permute-start.15 = (bf16[1792,512]{1,0:T(8,128)(2,1)}, bf16[1792,512]{1,0:T(8,128)(2,1)}, u32[]{:S(2)}, u32[]{:S(2)}) collective-permute-start(bf16[1792,512]{1,0:T(8,128)(2,1)} %collective-permute-done.14.refs_0_), channel_id=1, source_target_pairs={{0,2},{2,3},{3,1},{1,0},{4,6},{6,7},{7,5},{5,4},{8,10},{10,11},{11... | collective-permute-start | bytes 5505032 | tf_op jit(solution)/shard_map/ppermute | solution.py:18
  142.7 90.6 %collective-permute-start.25 = (bf16[1792,512]{1,0:T(8,128)(2,1)}, bf16[1792,512]{1,0:T(8,128)(2,1)}, u32[]{:S(2)}, u32[]{:S(2)}) collective-permute-start(bf16[1792,512]{1,0:T(8,128)(2,1)} %collective-permute-done.22.refs_0_), channel_id=1, source_target_pairs={{0,16},{16,0},{1,17},{17,1},{2,18},{18,2},{3,19},{19,3},{4,20},{20... | collective-permute-start | bytes 5505032 | tf_op jit(solution)/shard_map/ppermute | solution.py:22
  146.4 59.2 %collective-permute-start.7 = (bf16[1792,256]{1,0:T(8,128)(2,1)S(1)}, bf16[1792,256]{1,0:T(8,128)(2,1)S(1)}, u32[]{:S(2)}, u32[]{:S(2)}) collective-permute-start(bf16[1792,256]{1,0:T(8,128)(2,1)S(1)} %get-tuple-element.5.refs_2_), channel_id=1, source_target_pairs={{0,16},{16,0},{1,17},{17,1},{2,18},{18,2},{3,19},{19,3},{4,20},{20... | collective-permute-start | bytes 2752520 | tf_op jit(solution)/shard_map/ppermute | solution.py:22
  175.0 75.4 %collective-permute-start.24 = (bf16[1792,512]{1,0:T(8,128)(2,1)}, bf16[1792,512]{1,0:T(8,128)(2,1)}, u32[]{:S(2)}, u32[]{:S(2)}) collective-permute-start(bf16[1792,512]{1,0:T(8,128)(2,1)} %collective-permute-done.23.refs_0_), channel_id=1, source_target_pairs={{0,16},{16,0},{1,17},{17,1},{2,18},{18,2},{3,19},{19,3},{4,20},{20... | collective-permute-start | bytes 5505032 | tf_op jit(solution)/shard_map/ppermute | solution.py:22
  205.6 78.6 %collective-permute-start.20 = (bf16[1792,512]{1,0:T(8,128)(2,1)S(1)}, bf16[1792,512]{1,0:T(8,128)(2,1)S(1)}, u32[]{:S(2)}, u32[]{:S(2)}) collective-permute-start(bf16[1792,512]{1,0:T(8,128)(2,1)S(1)} %copy-done.1), channel_id=1, source_target_pairs={{0,16},{16,0},{1,17},{17,1},{2,18},{18,2},{3,19},{19,3},{4,20},{20... | collective-permute-start | bytes 5505032 | tf_op jit(solution)/shard_map/ppermute | solution.py:22
  207.1 116.5 %collective-permute-start.19 = (bf16[1792,512]{1,0:T(8,128)(2,1)}, bf16[1792,512]{1,0:T(8,128)(2,1)S(1)}, u32[]{:S(2)}, u32[]{:S(2)}) collective-permute-start(bf16[1792,512]{1,0:T(8,128)(2,1)} %collective-permute-done.14.refs_0_), channel_id=1, source_target_pairs={{0,16},{16,0},{1,17},{17,1},{2,18},{18,2},{3,19},{19,3},{4,20},{20... | collective-permute-start | bytes 5505032 | tf_op jit(solution)/shard_map/ppermute | solution.py:22
  212.2 112.5 %collective-permute-start.16 = (bf16[1792,512]{1,0:T(8,128)(2,1)}, bf16[1792,512]{1,0:T(8,128)(2,1)}, u32[]{:S(2)}, u32[]{:S(2)}) collective-permute-start(bf16[1792,512]{1,0:T(8,128)(2,1)} %collective-permute-done.15.refs_0_), channel_id=1, source_target_pairs={{0,2},{2,3},{3,1},{1,0},{4,6},{6,7},{7,5},{5,4},{8,10},{10,11},{11... | collective-permute-start | bytes 5505032 | tf_op jit(solution)/shard_map/ppermute | solution.py:18
  250.4 113.7 %collective-permute-start.18 = (bf16[1792,512]{1,0:T(8,128)(2,1)}, bf16[1792,512]{1,0:T(8,128)(2,1)}, u32[]{:S(2)}, u32[]{:S(2)}) collective-permute-start(bf16[1792,512]{1,0:T(8,128)(2,1)} %collective-permute-done.15.refs_0_), channel_id=1, source_target_pairs={{0,16},{16,0},{1,17},{17,1},{2,18},{18,2},{3,19},{19,3},{4,20},{20... | collective-permute-start | bytes 5505032 | tf_op jit(solution)/shard_map/ppermute | solution.py:22
  273.0 88.7 %collective-permute-start.4 = (bf16[1792,256]{1,0:T(8,128)(2,1)S(1)}, bf16[1792,256]{1,0:T(8,128)(2,1)}, u32[]{:S(2)}, u32[]{:S(2)}) collective-permute-start(bf16[1792,256]{1,0:T(8,128)(2,1)S(1)} %get-tuple-element.5.refs_2_), channel_id=1, source_target_pairs={{0,2},{2,3},{3,1},{1,0},{4,6},{6,7},{7,5},{5,4},{8,10},{10,11},{11... | collective-permute-start | bytes 2752520 | tf_op jit(solution)/shard_map/ppermute | solution.py:18
  285.4 76.8 %collective-permute-start.8 = (bf16[1792,256]{1,0:T(8,128)(2,1)S(1)}, bf16[1792,256]{1,0:T(8,128)(2,1)}, u32[]{:S(2)}, u32[]{:S(2)}) collective-permute-start(bf16[1792,256]{1,0:T(8,128)(2,1)S(1)} %collective-permute-done.7.refs_3_), channel_id=1, source_target_pairs={{0,2},{2,3},{3,1},{1,0},{4,6},{6,7},{7,5},{5,4},{8,10},{10,11},{11... | collective-permute-start | bytes 2752520 | tf_op jit(solution)/shard_map/ppermute | solution.py:18
  324.8 77.5 %collective-permute-start.17 = (bf16[1792,512]{1,0:T(8,128)(2,1)}, bf16[1792,512]{1,0:T(8,128)(2,1)}, u32[]{:S(2)}, u32[]{:S(2)}) collective-permute-start(bf16[1792,512]{1,0:T(8,128)(2,1)} %collective-permute-done.16.refs_0_), channel_id=1, source_target_pairs={{0,16},{16,0},{1,17},{17,1},{2,18},{18,2},{3,19},{19,3},{4,20},{20... | collective-permute-start | bytes 5505032 | tf_op jit(solution)/shard_map/ppermute | solution.py:22
  361.7 60.2 %collective-permute-start.13 = (bf16[1792,256]{1,0:T(8,128)(2,1)S(1)}, bf16[1792,256]{1,0:T(8,128)(2,1)S(1)}, u32[]{:S(2)}, u32[]{:S(2)}) collective-permute-start(bf16[1792,256]{1,0:T(8,128)(2,1)S(1)} %get-tuple-element.6.refs_0_), channel_id=1, source_target_pairs={{0,16},{16,0},{1,17},{17,1},{2,18},{18,2},{3,19},{19,3},{4,20},{20... | collective-permute-start | bytes 2752520 | tf_op jit(solution)/shard_map/ppermute | solution.py:22
  362.2 62.1 %collective-permute-start.5 = (bf16[1792,256]{1,0:T(8,128)(2,1)}, bf16[1792,256]{1,0:T(8,128)(2,1)}, u32[]{:S(2)}, u32[]{:S(2)}) collective-permute-start(bf16[1792,256]{1,0:T(8,128)(2,1)} %collective-permute-done.4.refs_2_), channel_id=1, source_target_pairs={{0,2},{2,3},{3,1},{1,0},{4,6},{6,7},{7,5},{5,4},{8,10},{10,11},{11... | collective-permute-start | bytes 2752520 | tf_op jit(solution)/shard_map/ppermute | solution.py:18
  364.0 60.9 %collective-permute-start.9 = (bf16[1792,256]{1,0:T(8,128)(2,1)}, bf16[1792,256]{1,0:T(8,128)(2,1)}, u32[]{:S(2)}, u32[]{:S(2)}) collective-permute-start(bf16[1792,256]{1,0:T(8,128)(2,1)} %collective-permute-done.8.refs_3_), channel_id=1, source_target_pairs={{0,2},{2,3},{3,1},{1,0},{4,6},{6,7},{7,5},{5,4},{8,10},{10,11},{11... | collective-permute-start | bytes 2752520 | tf_op jit(solution)/shard_map/ppermute | solution.py:18
  364.0 60.3 %collective-permute-start.2 = (bf16[1792,256]{1,0:T(8,128)(2,1)}, bf16[1792,256]{1,0:T(8,128)(2,1)}, u32[]{:S(2)}, u32[]{:S(2)}) collective-permute-start(bf16[1792,256]{1,0:T(8,128)(2,1)} %collective-permute-done.1.refs_0_), channel_id=1, source_target_pairs={{0,2},{2,3},{3,1},{1,0},{4,6},{6,7},{7,5},{5,4},{8,10},{10,11},{11... | collective-permute-start | bytes 2752520 | tf_op jit(solution)/shard_map/ppermute | solution.py:18
  424.3 54.1 %collective-permute-start.6 = (bf16[1792,256]{1,0:T(8,128)(2,1)}, bf16[1792,256]{1,0:T(8,128)(2,1)}, u32[]{:S(2)}, u32[]{:S(2)}) collective-permute-start(bf16[1792,256]{1,0:T(8,128)(2,1)} %collective-permute-done.5.refs_2_), channel_id=1, source_target_pairs={{0,2},{2,3},{3,1},{1,0},{4,6},{6,7},{7,5},{5,4},{8,10},{10,11},{11... | collective-permute-start | bytes 2752520 | tf_op jit(solution)/shard_map/ppermute | solution.py:18
  424.3 54.1 %collective-permute-start.3 = (bf16[1792,256]{1,0:T(8,128)(2,1)}, bf16[1792,256]{1,0:T(8,128)(2,1)}, u32[]{:S(2)}, u32[]{:S(2)}) collective-permute-start(bf16[1792,256]{1,0:T(8,128)(2,1)} %collective-permute-done.2.refs_0_), channel_id=1, source_target_pairs={{0,16},{16,0},{1,17},{17,1},{2,18},{18,2},{3,19},{19,3},{4,20},{20... | collective-permute-start | bytes 2752520 | tf_op jit(solution)/shard_map/ppermute | solution.py:22
  (21 other events, 804.5 us)
Sparse Core Ops, SparseCore 0:
  8.9 96.7 all-gather.7
  107.2 94.0 all-gather.5
  202.8 94.0 all-gather.3

commit v2 on v0

v2 whole, which is shorter than its diff:
```python
import functools
import math

import jax
import jax.numpy as jnp
from jax import lax
from jax.experimental import pallas as pl
from jax.experimental.pallas import tpu as pltpu
from jax.sharding import PartitionSpec as P


def cycle_of(runs, grps):
    rows = [[r * grps + g for g in range(grps)] for r in range(runs)]
    return [i for r, row in enumerate(rows) for i in (row if r % 2 == 0 else row[::-1])]


def pass_on(value, cycle, way):
    n = len(cycle)
    pairs = [(cycle[i], cycle[(i + way) % n]) for i in range(n)]
    return lax.ppermute(value, ("run", "grp"), pairs)


def tile(extent, most):
    return max(t for t in range(128, most + 1, 128) if extent % t == 0)


def add_terms_body(count, first, scale, blocks_ref, *refs):
    lefts, rights = refs[:count], refs[count : 2 * count]
    out, mark = refs[-2:]
    mark[...] = jnp.zeros_like(mark)
    total = None if first else refs[2 * count][...]
    for left, right in zip(lefts, rights):
        term = lax.dot_general(
            left[...], right[...], (((1,), (1,)), ((), ())), preferred_element_type=jnp.float32
        )
        total = term if total is None else total + term
    out[...] = total if scale is None else total * scale


def add_terms(total, blocks, pieces, scale=None):
    rows, across = pieces[0][0].shape[0], pieces[0][1].shape[0]
    tm = tile(rows, 256)
    count, first = len(pieces), total is None

    def columns(step, parts, part, i, blocks):
        return 0, blocks[step] * parts + part

    in_specs = [pl.BlockSpec((tm, p[0].shape[1]), lambda i, blocks: (i, 0)) for p in pieces]
    in_specs += [
        pl.BlockSpec((across, p[0].shape[1]), functools.partial(columns, *p[2:])) for p in pieces
    ]
    place = pl.BlockSpec((tm, across), lambda i, blocks: (i, 0))
    operands = [p[0] for p in pieces] + [p[1] for p in pieces]
    if not first:
        in_specs.append(place)
        operands.append(total)
    deep = sum(p[0].shape[1] for p in pieces)
    return pl.pallas_call(
        functools.partial(add_terms_body, count, first, scale),
        grid_spec=pltpu.PrefetchScalarGridSpec(
            num_scalar_prefetch=1,
            grid=(rows // tm,),
            in_specs=in_specs,
            out_specs=[place, pl.BlockSpec((8, 128), lambda i, blocks: (0, 0))],
        ),
        out_shape=[
            jax.ShapeDtypeStruct((rows, across), jnp.float32),
            jax.ShapeDtypeStruct((8, 128), jnp.float32),
        ],
        input_output_aliases={} if first else {2 * count + 1: 0},
        compiler_params=pltpu.CompilerParams(vmem_limit_bytes=60 * 1024 * 1024),
        cost_estimate=pl.CostEstimate(
            flops=2 * rows * across * deep,
            bytes_accessed=2 * deep * (rows + across) + (4 if first else 8) * rows * across,
            transcendentals=0,
        ),
    )(blocks, *operands)


def make_local(runs, grps):
    cycle = cycle_of(runs, grps)
    n = len(cycle)
    source = [[cycle[(cycle.index(d) - s) % n] for s in range(n)] for d in range(n)]

    def local(a_gate, a_up, a_down, b_gate, b_up, b_down):
        depth = a_gate.shape[1]
        half = depth // 2
        here = lax.axis_index(("run", "grp"))
        blocks = jnp.array(source, jnp.int32)[here]
        b_full = [lax.all_gather(b, "blk", axis=1, tiled=True) for b in (b_gate, b_up, b_down)]

        lanes = [
            [(a_gate, 0, 1, 0), (a_down[:, :half], 2, 2, 0)],
            [(a_up, 1, 1, 0), (a_down[:, half:], 2, 2, 1)],
        ]
        rounds = n // 2
        waiting = [(a_gate, b_full[0], 0, 1, 0)]
        late = [(a_up, b_full[1], 0, 1, 0)]
        total, marks = None, [None]
        held = [None, None]
        for stage in range(2 * rounds):
            phase, s = stage // rounds, stage % rounds + 1
            if stage == rounds:
                waiting.append((a_down, b_full[2], 0, 1, 0))
            arrived = []
            for lane in range(2):
                a, tensor, parts, part = lanes[lane][phase]
                ahead, back = (a, a) if s == 1 else held[lane]
                if s == 1 and phase:
                    ahead, back, _ = lax.optimization_barrier((ahead, back, held[lane]))
                if stage > 1:
                    ahead, back, _ = lax.optimization_barrier((ahead, back, marks[stage - 1]))
                b = b_full[tensor]
                if 2 * s < n:
                    held[lane] = pass_on(ahead, cycle, 1), pass_on(back, cycle, -1)
                    arrived += [
                        (held[lane][0], b, s, parts, part),
                        (held[lane][1], b, n - s, parts, part),
                    ]
                elif parts == 1:
                    held[lane] = pass_on(ahead[:, :half], cycle, 1), pass_on(back[:, half:], cycle, -1)
                    arrived += [(held[lane][0], b, s, 2, 0), (held[lane][1], b, s, 2, 1)]
                else:
                    last_one = pass_on(back, cycle, -1) if part else pass_on(ahead, cycle, 1)
                    arrived += [(last_one, b, s, parts, part)]
            if phase == 0 and s < 3 and s < rounds:
                waiting += arrived[:2]
                late += arrived[2:]
            else:
                waiting += arrived[:2] + late + arrived[2:]
                late = []
            while waiting:
                call, deep = [], 0
                while waiting and deep + waiting[0][0].shape[1] <= 4 * depth:
                    deep += waiting[0][0].shape[1]
                    call.append(waiting.pop(0))
                last = stage == 2 * rounds - 1 and not waiting
                scale = 1.0 / math.sqrt(3.0 * depth * n) if last else None
                total, mark = add_terms(total, blocks, call, scale)
            marks.append(mark)
        return total

    return local


def solution(mesh):
    placed = (
        P("blk", ("run", "grp")),
        P("blk", ("run", "grp")),
        P("blk", ("run", "grp")),
        P(("run", "grp"), "blk"),
        P(("run", "grp"), "blk"),
        P(("run", "grp"), "blk"),
    )
    local = make_local(mesh.shape["run"], mesh.shape["grp"])
    return jax.shard_map(
        local, mesh=mesh, in_specs=placed, out_specs=P("blk", ("run", "grp")), check_vma=False
    )
```

time: 949 us -> 486 us (0.51)
  waiting for transfers between devices: 827 us -> 238 us
  Pallas kernels: 0 us -> 186 us
  matrix products: 108 us -> 0 us
  starting transfers between devices: 0.19 us -> 33.7 us
  local copies, waits for them, and re-layouts: 0 us -> 12.9 us
    all_gather x6 -> x3, waiting for transfers between devices: 824 us -> 8.04 us  [local(): lax.all_gather(b, 'blk', axis=1, tiled=True)]
    ppermute x0 -> x30, waiting for transfers between devices: none -> 228 us  [pass_on(): return lax.ppermute(value, ('run', 'grp'), pairs)]
    pallas_call x0 -> x10, Pallas kernels: none -> 186 us  [add_terms(): pl.pallas_call(functools.partial(add_terms_body, count, first, scale), gr...]
    dot_general x3 -> x0, matrix products: 108 us -> none  [pair_term(): lax.dot_general(left, right, (((1,), (1,)), ((), ())), preferred_element_...]
    ppermute x0 -> x30, starting transfers between devices: none -> 33.6 us  [pass_on(): return lax.ppermute(value, ('run', 'grp'), pairs)]
    slice x0 -> x5, local copies, waits for them, and re-layouts: none -> 10.4 us  [the longest x2 4.55 us: local(): ahead[:, :half]]
  transfers between devices with their start and end apart: 6 -> 33, of which waited for: 6 -> 17; matrix products, arithmetic and copies ran while one was open for 8% -> 2% of each run, Pallas kernels for 0% -> 35%
where the time goes in v2:
time: 486 us; the launch traced here: 484 us
  waiting for transfers between devices  238 us (49%)
  Pallas kernels  186 us (38%)
  starting transfers between devices  33.7 us (7%)
  between operations  13.2 us (3%)
  local copies, waits for them, and re-layouts  12.9 us (3%)
    ppermute x30, waiting for transfers between devices, pass_on(): return lax.ppermute(value, ('run', 'grp'), pairs)  228 us
    pallas_call x10, Pallas kernels, add_terms(): pl.pallas_call(functools.partial(add_terms_body, count, first, scale), gr...  186 us
    ppermute x30, starting transfers between devices, pass_on(): return lax.ppermute(value, ('run', 'grp'), pairs)  33.6 us
  transfers between devices with their start and end apart: 33, of which 17 were waited for; matrix products, arithmetic and copies ran while one was open for 2% of the time, Pallas kernels for 35%

profile of v2, /device:TPU:0, one launch (start us, length us, event | category | flops | bytes accessed | tf_op | source)
XLA Modules:
  0.0 483.9 jit_solution(703326157025836911)
XLA Ops:
  8.8 3.0 collective-permute-start.10
  13.9 39.1 %collective-permute-done.10.refs_0_ = bf16[1792,512]{1,0:T(8,128)(2,1)} collective-permute-done((bf16[1792,512]{1,0:T(8,128)(2,1)}, bf16[1792,512]{1,0:T(8,128)(2,1)}, u32[]{:S(2)}, u32[]{:S(2)}) %collective-permute-start.10) | collective-permute-done | bytes 1835040 | tf_op jit(solution)/shard_map/ppermute | solution.py:20
  55.1 39.2 %collective-permute-done.refs_1_ = bf16[1792,512]{1,0:T(8,128)(2,1)} collective-permute-done((bf16[1792,512]{1,0:T(8,128)(2,1)S(1)}, bf16[1792,512]{1,0:T(8,128)(2,1)}, u32[]{:S(2)}, u32[]{:S(2)}) %collective-permute-start) | collective-permute-done | bytes 1835040 | tf_op jit(solution)/shard_map/ppermute | solution.py:20
  97.6 8.0 %all-gather.4.cloned.1.call-done.refs_3_.refs_4_.refs_5_.refs_2_ = bf16[1792,4096]{1,0:T(8,128)(2,1)} async-done(((bf16[1792,1024]{1,0:T(8,128)(2,1)}), bf16[1792,4096]{1,0:T(8,128)(2,1)}) %all-gather.4.cloned.1.call-update) | async-done | bytes 14680080 | tf_op jit(solution)/shard_map/all_gather | solution.py:90
  105.7 16.8 %shard_map.73 = (f32[1792,1792]{1,0:T(8,128)}, f32[8,128]{1,0:T(8,128)}) custom-call(s32[8]{0:T(128)} %dynamic-slice_bitcast_fusion.blocks_ref, bf16[1792,512]{1,0:T(8,128)(2,1)} %refs_0_.2, bf16[1792,512]{1,0:T(8,128)(2,1)} %collective-permute-done.refs_1_, bf16[1792,512]{1,0:T(8,128)(2,1)} %collective-permute-done.2.refs_2_, ...), custom_call_target="tpu_custom_call" | custom-call | flops 9865003008 | bytes 23855104 | tf_op jit(solution)/shard_map/pallas_call | solution.py:58
  122.5 9.1 %collective-permute-done.11.refs_2_ = bf16[1792,512]{1,0:T(8,128)(2,1)} collective-permute-done((bf16[1792,512]{1,0:T(8,128)(2,1)}, bf16[1792,512]{1,0:T(8,128)(2,1)}, u32[]{:S(2)}, u32[]{:S(2)}) %collective-permute-start.11) | collective-permute-done | bytes 1835040 | tf_op jit(solution)/shard_map/ppermute | solution.py:20
  135.7 37.3 %collective-permute-done.1.refs_0_ = bf16[1792,512]{1,0:T(8,128)(2,1)} collective-permute-done((bf16[1792,512]{1,0:T(8,128)(2,1)}, bf16[1792,512]{1,0:T(8,128)(2,1)}, u32[]{:S(2)}, u32[]{:S(2)}) %collective-permute-start.1) | collective-permute-done | bytes 1835040 | tf_op jit(solution)/shard_map/ppermute | solution.py:20
  176.4 18.0 %shard_map.74 = (f32[1792,1792]{1,0:T(8,128)}, f32[8,128]{1,0:T(8,128)}) custom-call(s32[8]{0:T(128)} %dynamic-slice_bitcast_fusion.blocks_ref, bf16[1792,512]{1,0:T(8,128)(2,1)} %collective-permute-done.1.refs_0_, bf16[1792,512]{1,0:T(8,128)(2,1)} %collective-permute-done.3.refs_1_, ...), custom_call_target="tpu_custom_call", output_to_operand_aliasing={{0}: (5, {})} | custom-call | flops 6576668672 | bytes 33030144 | tf_op jit(solution)/shard_map/pallas_call | solution.py:58
  194.4 15.9 %collective-permute-done.12.refs_0_ = bf16[1792,512]{1,0:T(8,128)(2,1)} collective-permute-done((bf16[1792,512]{1,0:T(8,128)(2,1)}, bf16[1792,512]{1,0:T(8,128)(2,1)}, u32[]{:S(2)}, u32[]{:S(2)}) %collective-permute-start.12) | collective-permute-done | bytes 1835040 | tf_op jit(solution)/shard_map/ppermute | solution.py:20
  212.3 2.4 slice.21
  214.8 2.3 slice.22
  219.0 32.6 %collective-permute-done.4.refs_0_ = bf16[1792,512]{1,0:T(8,128)(2,1)} collective-permute-done((bf16[1792,512]{1,0:T(8,128)(2,1)}, bf16[1792,512]{1,0:T(8,128)(2,1)}, u32[]{:S(2)}, u32[]{:S(2)}) %collective-permute-start.4) | collective-permute-done | bytes 1835040 | tf_op jit(solution)/shard_map/ppermute | solution.py:20
  258.0 22.2 %shard_map.75 = (f32[1792,1792]{1,0:T(8,128)}, f32[8,128]{1,0:T(8,128)}) custom-call(s32[8]{0:T(128)} %dynamic-slice_bitcast_fusion.blocks_ref, bf16[1792,512]{1,0:T(8,128)(2,1)} %collective-permute-done.4.refs_0_, bf16[1792,512]{1,0:T(8,128)(2,1)} %collective-permute-done.5.refs_1_, bf16[1792,512]{1,0:T(8,128)(2,1)} %refs_2_.1, ...), custom_call_target="tpu_custom_call", output_to_operand_aliasing={{0}: (9, {})} | custom-call | flops 13153337344 | bytes 40370176 | tf_op jit(solution)/shard_map/pallas_call | solution.py:58
  280.2 22.1 %shard_map.76 = (f32[1792,1792]{1,0:T(8,128)}, f32[8,128]{1,0:T(8,128)}) custom-call(s32[8]{0:T(128)} %dynamic-slice_bitcast_fusion.blocks_ref, bf16[1792,512]{1,0:T(8,128)(2,1)} %collective-permute-done.10.refs_0_, bf16[1792,512]{1,0:T(8,128)(2,1)} %collective-permute-done.9.refs_1_, ...), custom_call_target="tpu_custom_call", output_to_operand_aliasing={{0}: (9, {})} | custom-call | flops 13153337344 | bytes 40370176 | tf_op jit(solution)/shard_map/pallas_call | solution.py:58
  302.2 15.5 %shard_map.77 = (f32[1792,1792]{1,0:T(8,128)}, f32[8,128]{1,0:T(8,128)}) custom-call(s32[8]{0:T(128)} %dynamic-slice_bitcast_fusion.blocks_ref, bf16[1792,512]{1,0:T(8,128)(2,1)} %collective-permute-done.12.refs_0_, bf16[1792,4096]{1,0:T(8,128)(2,1)} %all-gather.6.cloned.1.call-done.refs_6_.refs_7_.refs_4_.refs_5_.refs_1_, ...), custom_call_target="tpu_custom_call", output_to_operand_aliasing={{0}: (3, {})} | custom-call | flops 3288334336 | bytes 29360128 | tf_op jit(solution)/shard_map/pallas_call | solution.py:58
  322.0 18.7 %shard_map.78 = (f32[1792,1792]{1,0:T(8,128)}, f32[8,128]{1,0:T(8,128)}) custom-call(s32[8]{0:T(128)} %dynamic-slice_bitcast_fusion.blocks_ref, bf16[1792,256]{1,0:T(8,128)(2,1)} %copy-done.4, bf16[1792,256]{1,0:T(8,128)(2,1)} %collective-permute-done.7.refs_1_, bf16[1792,256]{1,0:T(8,128)(2,1)} %copy-done.2, ...), custom_call_target="tpu_custom_call", output_to_operand_aliasing={{0}: (9, {})} | custom-call | flops 6576668672 | bytes 33030144 | tf_op jit(solution)/shard_map/pallas_call | solution.py:58
  343.6 17.6 %collective-permute-done.14.refs_1_ = bf16[1792,256]{1,0:T(8,128)(2,1)} collective-permute-done((bf16[1792,256]{1,0:T(8,128)(2,1)}, bf16[1792,256]{1,0:T(8,128)(2,1)}, u32[]{:S(2)}, u32[]{:S(2)}) %collective-permute-start.14) | collective-permute-done | bytes 917536 | tf_op jit(solution)/shard_map/ppermute | solution.py:20
  363.2 19.3 %shard_map.79 = (f32[1792,1792]{1,0:T(8,128)}, f32[8,128]{1,0:T(8,128)}) custom-call(s32[8]{0:T(128)} %dynamic-slice_bitcast_fusion.blocks_ref, bf16[1792,512]{1,0:T(8,128)(2,1)} %refs_0_.3, bf16[1792,256]{1,0:T(8,128)(2,1)} %collective-permute-done.14.refs_1_, bf16[1792,256]{1,0:T(8,128)(2,1)} %collective-permute-done.15.refs_2_, ...), custom_call_target="tpu_custom_call", output_to_operand_aliasing={{0}: (11, {})} | custom-call | flops 9865003008 | bytes 36700160 | tf_op jit(solution)/shard_map/pallas_call | solution.py:58
  384.6 15.7 %collective-permute-done.18.refs_0_ = bf16[1792,256]{1,0:T(8,128)(2,1)S(1)} collective-permute-done((bf16[1792,256]{1,0:T(8,128)(2,1)}, bf16[1792,256]{1,0:T(8,128)(2,1)S(1)}, u32[]{:S(2)}, u32[]{:S(2)}) %collective-permute-start.18) | collective-permute-done | bytes 917536 | tf_op jit(solution)/shard_map/ppermute | solution.py:20
  402.6 18.7 %shard_map.80 = (f32[1792,1792]{1,0:T(8,128)}, f32[8,128]{1,0:T(8,128)}) custom-call(s32[8]{0:T(128)} %dynamic-slice_bitcast_fusion.blocks_ref, bf16[1792,256]{1,0:T(8,128)(2,1)} %copy-done.7, bf16[1792,256]{1,0:T(8,128)(2,1)} %collective-permute-done.19.refs_1_, bf16[1792,256]{1,0:T(8,128)(2,1)} %copy-done.5, ...), custom_call_target="tpu_custom_call", output_to_operand_aliasing={{0}: (9, {})} | custom-call | flops 6576668672 | bytes 33030144 | tf_op jit(solution)/shard_map/pallas_call | solution.py:58
  423.3 12.5 %collective-permute-done.22.refs_0_ = bf16[1792,256]{1,0:T(8,128)(2,1)} collective-permute-done((bf16[1792,256]{1,0:T(8,128)(2,1)S(1)}, bf16[1792,256]{1,0:T(8,128)(2,1)}, u32[]{:S(2)}, u32[]{:S(2)}) %collective-permute-start.22) | collective-permute-done | bytes 917536 | tf_op jit(solution)/shard_map/ppermute | solution.py:20
  435.7 4.1 collective-permute-done.23.refs_1_
  441.7 18.7 %shard_map.81 = (f32[1792,1792]{1,0:T(8,128)}, f32[8,128]{1,0:T(8,128)}) custom-call(s32[8]{0:T(128)} %dynamic-slice_bitcast_fusion.blocks_ref, bf16[1792,256]{1,0:T(8,128)(2,1)} %collective-permute-done.22.refs_0_, bf16[1792,256]{1,0:T(8,128)(2,1)} %collective-permute-done.23.refs_1_, ...), custom_call_target="tpu_custom_call", output_to_operand_aliasing={{0}: (9, {})} | custom-call | flops 6576668672 | bytes 33030144 | tf_op jit(solution)/shard_map/pallas_call | solution.py:58
  461.6 15.7 %shard_map.82 = (f32[1792,1792]{1,0:T(8,128)}, f32[8,128]{1,0:T(8,128)}) custom-call(s32[8]{0:T(128)} %dynamic-slice_bitcast_fusion.blocks_ref, bf16[1792,256]{1,0:T(8,128)(2,1)} %copy-done.9, bf16[1792,256]{1,0:T(8,128)(2,1)} %copy-done.8, ...), custom_call_target="tpu_custom_call", output_to_operand_aliasing={{0}: (5, {})} | custom-call | flops 3288334336 | bytes 29360128 | tf_op jit(solution)/shard_map/pallas_call | solution.py:58
  (81 shorter events, 46.2 us)
Async XLA Ops:
  6.5 99.1 %all-gather.4.cloned.1.call-start = ((), (), s32[]{:S(2)}) async-start(), calls=%async_computation | async-start | bytes 18350080 | tf_op jit(solution)/shard_map/all_gather | solution.py:90
  7.3 250.7 %all-gather.6.cloned.1.call-start = ((), (), s32[]{:S(2)}) async-start(), calls=%async_computation.1 | async-start | bytes 18350080 | tf_op jit(solution)/shard_map/all_gather | solution.py:90
  8.0 355.2 %all-gather.8.cloned.1.call-start = ((), (), s32[]{:S(2)}) async-start(), calls=%async_computation.2 | async-start | bytes 18350080 | tf_op jit(solution)/shard_map/all_gather | solution.py:90
  8.8 44.2 %collective-permute-start.10 = (bf16[1792,512]{1,0:T(8,128)(2,1)}, bf16[1792,512]{1,0:T(8,128)(2,1)}, u32[]{:S(2)}, u32[]{:S(2)}) collective-permute-start(bf16[1792,512]{1,0:T(8,128)(2,1)} %refs_2_.1), channel_id=1, source_target_pairs={{0,16},{1,0},{2,1},{3,2},{19,3},{18,19},{17,18},{16,17},{4,20},{5,... | collective-permute-start | bytes 5505032 | tf_op jit(solution)/shard_map/ppermute | solution.py:20
  11.7 43.3 %collective-permute-start.8 = (bf16[1792,512]{1,0:T(8,128)(2,1)}, bf16[1792,512]{1,0:T(8,128)(2,1)}, u32[]{:S(2)}, u32[]{:S(2)}) collective-permute-start(bf16[1792,512]{1,0:T(8,128)(2,1)} %refs_2_.1), channel_id=1, source_target_pairs={{0,1},{1,2},{2,3},{3,19},{19,18},{18,17},{17,16},{16,0},{4,5},{5,6... | collective-permute-start | bytes 5505032 | tf_op jit(solution)/shard_map/ppermute | solution.py:20
  11.9 82.4 %collective-permute-start = (bf16[1792,512]{1,0:T(8,128)(2,1)S(1)}, bf16[1792,512]{1,0:T(8,128)(2,1)}, u32[]{:S(2)}, u32[]{:S(2)}) collective-permute-start(bf16[1792,512]{1,0:T(8,128)(2,1)S(1)} %copy-done.1), channel_id=1, source_target_pairs={{0,1},{1,2},{2,3},{3,19},{19,18},{18,17},{17,16},{16,0},{4,5},{5,6... | collective-permute-start | bytes 5505032 | tf_op jit(solution)/shard_map/ppermute | solution.py:20
  13.9 80.6 %collective-permute-start.2 = (bf16[1792,512]{1,0:T(8,128)(2,1)S(1)}, bf16[1792,512]{1,0:T(8,128)(2,1)}, u32[]{:S(2)}, u32[]{:S(2)}) collective-permute-start(bf16[1792,512]{1,0:T(8,128)(2,1)S(1)} %copy-done.1), channel_id=1, source_target_pairs={{0,16},{1,0},{2,1},{3,2},{19,3},{18,19},{17,18},{16,17},{4,20},{5,... | collective-permute-start | bytes 5505032 | tf_op jit(solution)/shard_map/ppermute | solution.py:20
  53.0 78.6 %collective-permute-start.11 = (bf16[1792,512]{1,0:T(8,128)(2,1)}, bf16[1792,512]{1,0:T(8,128)(2,1)}, u32[]{:S(2)}, u32[]{:S(2)}) collective-permute-start(bf16[1792,512]{1,0:T(8,128)(2,1)} %collective-permute-done.10.refs_0_), channel_id=1, source_target_pairs={{0,16},{1,0},{2,1},{3,2},{19,3},{18,19},{17,18},{16,17},{4,20},{5,... | collective-permute-start | bytes 5505032 | tf_op jit(solution)/shard_map/ppermute | solution.py:20
  55.0 78.6 %collective-permute-start.9 = (bf16[1792,512]{1,0:T(8,128)(2,1)}, bf16[1792,512]{1,0:T(8,128)(2,1)}, u32[]{:S(2)}, u32[]{:S(2)}) collective-permute-start(bf16[1792,512]{1,0:T(8,128)(2,1)} %collective-permute-done.8.refs_3_), channel_id=1, source_target_pairs={{0,1},{1,2},{2,3},{3,19},{19,18},{18,17},{17,16},{16,0},{4,5},{5,6... | collective-permute-start | bytes 5505032 | tf_op jit(solution)/shard_map/ppermute | solution.py:20
  94.3 78.6 %collective-permute-start.1 = (bf16[1792,512]{1,0:T(8,128)(2,1)}, bf16[1792,512]{1,0:T(8,128)(2,1)}, u32[]{:S(2)}, u32[]{:S(2)}) collective-permute-start(bf16[1792,512]{1,0:T(8,128)(2,1)} %collective-permute-done.refs_1_), channel_id=1, source_target_pairs={{0,1},{1,2},{2,3},{3,19},{19,18},{18,17},{17,16},{16,0},{4,5},{5,6... | collective-permute-start | bytes 5505032 | tf_op jit(solution)/shard_map/ppermute | solution.py:20
  94.4 78.5 %collective-permute-start.3 = (bf16[1792,512]{1,0:T(8,128)(2,1)}, bf16[1792,512]{1,0:T(8,128)(2,1)}, u32[]{:S(2)}, u32[]{:S(2)}) collective-permute-start(bf16[1792,512]{1,0:T(8,128)(2,1)} %collective-permute-done.2.refs_2_), channel_id=1, source_target_pairs={{0,16},{1,0},{2,1},{3,2},{19,3},{18,19},{17,18},{16,17},{4,20},{5,... | collective-permute-start | bytes 5505032 | tf_op jit(solution)/shard_map/ppermute | solution.py:20
  133.6 76.6 %collective-permute-start.12 = (bf16[1792,512]{1,0:T(8,128)(2,1)}, bf16[1792,512]{1,0:T(8,128)(2,1)}, u32[]{:S(2)}, u32[]{:S(2)}) collective-permute-start(bf16[1792,512]{1,0:T(8,128)(2,1)} %collective-permute-done.11.refs_2_), channel_id=1, source_target_pairs={{0,16},{1,0},{2,1},{3,2},{19,3},{18,19},{17,18},{16,17},{4,20},{5,... | collective-permute-start | bytes 5505032 | tf_op jit(solution)/shard_map/ppermute | solution.py:20
  135.2 77.1 %collective-permute-start.13 = (bf16[1792,512]{1,0:T(8,128)(2,1)}, bf16[1792,512]{1,0:T(8,128)(2,1)}, u32[]{:S(2)}, u32[]{:S(2)}) collective-permute-start(bf16[1792,512]{1,0:T(8,128)(2,1)} %collective-permute-done.9.refs_1_), channel_id=1, source_target_pairs={{0,1},{1,2},{2,3},{3,19},{19,18},{18,17},{17,16},{16,0},{4,5},{5,6... | collective-permute-start | bytes 5505032 | tf_op jit(solution)/shard_map/ppermute | solution.py:20
  173.0 78.6 %collective-permute-start.4 = (bf16[1792,512]{1,0:T(8,128)(2,1)}, bf16[1792,512]{1,0:T(8,128)(2,1)}, u32[]{:S(2)}, u32[]{:S(2)}) collective-permute-start(bf16[1792,512]{1,0:T(8,128)(2,1)} %collective-permute-done.1.refs_0_), channel_id=1, source_target_pairs={{0,1},{1,2},{2,3},{3,19},{19,18},{18,17},{17,16},{16,0},{4,5},{5,6... | collective-permute-start | bytes 5505032 | tf_op jit(solution)/shard_map/ppermute | solution.py:20
  173.1 78.5 %collective-permute-start.5 = (bf16[1792,512]{1,0:T(8,128)(2,1)}, bf16[1792,512]{1,0:T(8,128)(2,1)}, u32[]{:S(2)}, u32[]{:S(2)}) collective-permute-start(bf16[1792,512]{1,0:T(8,128)(2,1)} %collective-permute-done.3.refs_1_), channel_id=1, source_target_pairs={{0,16},{1,0},{2,1},{3,2},{19,3},{18,19},{17,18},{16,17},{4,20},{5,... | collective-permute-start | bytes 5505032 | tf_op jit(solution)/shard_map/ppermute | solution.py:20
  214.7 103.1 %collective-permute-start.16 = (bf16[1792,256]{1,0:T(8,128)(2,1)}, bf16[1792,256]{1,0:T(8,128)(2,1)S(1)}, u32[]{:S(2)}, u32[]{:S(2)}) collective-permute-start(bf16[1792,256]{1,0:T(8,128)(2,1)} %slice.21), channel_id=1, source_target_pairs={{0,1},{1,2},{2,3},{3,19},{19,18},{18,17},{17,16},{16,0},{4,5},{5,6... | collective-permute-start | bytes 2752520 | tf_op jit(solution)/shard_map/ppermute | solution.py:20
  217.1 100.7 %collective-permute-start.17 = (bf16[1792,256]{1,0:T(8,128)(2,1)}, bf16[1792,256]{1,0:T(8,128)(2,1)S(1)}, u32[]{:S(2)}, u32[]{:S(2)}) collective-permute-start(bf16[1792,256]{1,0:T(8,128)(2,1)} %slice.22), channel_id=1, source_target_pairs={{0,16},{1,0},{2,1},{3,2},{19,3},{18,19},{17,18},{16,17},{4,20},{5,... | collective-permute-start | bytes 2752520 | tf_op jit(solution)/shard_map/ppermute | solution.py:20
  253.8 66.1 %collective-permute-start.6 = (bf16[1792,256]{1,0:T(8,128)(2,1)}, bf16[1792,256]{1,0:T(8,128)(2,1)S(1)}, u32[]{:S(2)}, u32[]{:S(2)}) collective-permute-start(bf16[1792,256]{1,0:T(8,128)(2,1)} %slice.19), channel_id=1, source_target_pairs={{0,1},{1,2},{2,3},{3,19},{19,18},{18,17},{17,16},{16,0},{4,5},{5,6... | collective-permute-start | bytes 2752520 | tf_op jit(solution)/shard_map/ppermute | solution.py:20
  256.1 63.8 %collective-permute-start.7 = (bf16[1792,256]{1,0:T(8,128)(2,1)}, bf16[1792,256]{1,0:T(8,128)(2,1)}, u32[]{:S(2)}, u32[]{:S(2)}) collective-permute-start(bf16[1792,256]{1,0:T(8,128)(2,1)} %slice.20), channel_id=1, source_target_pairs={{0,16},{1,0},{2,1},{3,2},{19,3},{18,19},{17,18},{16,17},{4,20},{5,... | collective-permute-start | bytes 2752520 | tf_op jit(solution)/shard_map/ppermute | solution.py:20
  319.9 41.2 %collective-permute-start.14 = (bf16[1792,256]{1,0:T(8,128)(2,1)}, bf16[1792,256]{1,0:T(8,128)(2,1)}, u32[]{:S(2)}, u32[]{:S(2)}) collective-permute-start(bf16[1792,256]{1,0:T(8,128)(2,1)} %get-tuple-element.63), channel_id=1, source_target_pairs={{0,1},{1,2},{2,3},{3,19},{19,18},{18,17},{17,16},{16,0},{4,5},{5,6... | collective-permute-start | bytes 2752520 | tf_op jit(solution)/shard_map/ppermute | solution.py:20
  320.0 41.2 %collective-permute-start.15 = (bf16[1792,256]{1,0:T(8,128)(2,1)}, bf16[1792,256]{1,0:T(8,128)(2,1)}, u32[]{:S(2)}, u32[]{:S(2)}) collective-permute-start(bf16[1792,256]{1,0:T(8,128)(2,1)} %get-tuple-element.63), channel_id=1, source_target_pairs={{0,16},{1,0},{2,1},{3,2},{19,3},{18,19},{17,18},{16,17},{4,20},{5,... | collective-permute-start | bytes 2752520 | tf_op jit(solution)/shard_map/ppermute | solution.py:20
  341.5 41.0 %collective-permute-start.24 = (bf16[1792,256]{1,0:T(8,128)(2,1)}, bf16[1792,256]{1,0:T(8,128)(2,1)S(1)}, u32[]{:S(2)}, u32[]{:S(2)}) collective-permute-start(bf16[1792,256]{1,0:T(8,128)(2,1)} %collective-permute-done.20.refs_3_), channel_id=1, source_target_pairs={{0,1},{1,2},{2,3},{3,19},{19,18},{18,17},{17,16},{16,0},{4,5},{5,6... | collective-permute-start | bytes 2752520 | tf_op jit(solution)/shard_map/ppermute | solution.py:20
  361.2 39.1 %collective-permute-start.18 = (bf16[1792,256]{1,0:T(8,128)(2,1)}, bf16[1792,256]{1,0:T(8,128)(2,1)S(1)}, u32[]{:S(2)}, u32[]{:S(2)}) collective-permute-start(bf16[1792,256]{1,0:T(8,128)(2,1)} %collective-permute-done.14.refs_1_), channel_id=1, source_target_pairs={{0,1},{1,2},{2,3},{3,19},{19,18},{18,17},{17,16},{16,0},{4,5},{5,6... | collective-permute-start | bytes 2752520 | tf_op jit(solution)/shard_map/ppermute | solution.py:20
  421.3 39.1 %collective-permute-start.29 = (bf16[1792,256]{1,0:T(8,128)(2,1)}, bf16[1792,256]{1,0:T(8,128)(2,1)S(1)}, u32[]{:S(2)}, u32[]{:S(2)}) collective-permute-start(bf16[1792,256]{1,0:T(8,128)(2,1)} %collective-permute-done.28.refs_3_), channel_id=1, source_target_pairs={{0,16},{1,0},{2,1},{3,2},{19,3},{18,19},{17,18},{16,17},{4,20},{5,... | collective-permute-start | bytes 2752520 | tf_op jit(solution)/shard_map/ppermute | solution.py:20
  (19 other events, 429.4 us)
Sparse Core Ops, SparseCore 0:
  8.9 96.7 all-gather.3
  107.2 94.0 all-gather.5
  202.8 94.0 all-gather.7

commit v3 on v2

--- a/solution.py
+++ b/solution.py
@@ -24,54 +24,68 @@
     return max(t for t in range(128, most + 1, 128) if extent % t == 0)
 
 
-def add_terms_body(count, first, scale, blocks_ref, *refs):
-    lefts, rights = refs[:count], refs[count : 2 * count]
+def add_terms_body(columns, first, scale, tm, blocks_ref, *refs):
+    count = len(columns)
+    sources = refs[: 2 * count]
+    total = None if first else refs[2 * count]
     out, mark = refs[-2:]
     mark[...] = jnp.zeros_like(mark)
-    total = None if first else refs[2 * count][...]
-    for left, right in zip(lefts, rights):
-        term = lax.dot_general(
-            left[...], right[...], (((1,), (1,)), ((), ())), preferred_element_type=jnp.float32
-        )
-        total = term if total is None else total + term
-    out[...] = total if scale is None else total * scale
+    rows = sources[0].shape[0]
+    across = sources[count].shape[0]
+
+    def step(*tiles):
+        lefts, rights = tiles[:count], tiles[count : 2 * count]
+        here = pl.ds(pl.multiple_of(pl.program_id(0) * tm, tm), tm)
+        result = None if first else total[here, :]
+        for left, right in zip(lefts, rights):
+            term = lax.dot_general(
+                left[...], right[...], (((1,), (1,)), ((), ())), preferred_element_type=jnp.float32
+            )
+            result = term if result is None else result + term
+        if scale is None:
+            out[here, :] = result
+        else:
+            tiles[-1][...] = result * scale
+
+    def place(wide, which, parts, part):
+        return pl.BlockSpec((across, wide), lambda i: (0, blocks_ref[which] * parts + part))
+
+    specs = [pl.BlockSpec((tm, wide), lambda i: (i, 0)) for wide, *_ in columns]
+    specs += [place(*c) for c in columns]
+    result_specs = [] if scale is None else [pl.BlockSpec((tm, across), lambda i: (i, 0))]
+    results = [] if scale is None else [out]
+    pltpu.emit_pipeline(step, grid=(rows // tm,), in_specs=specs, out_specs=result_specs)(
+        *sources, *results
+    )
 
 
 def add_terms(total, blocks, pieces, scale=None):
     rows, across = pieces[0][0].shape[0], pieces[0][1].shape[0]
-    tm = tile(rows, 256)
-    count, first = len(pieces), total is None
-
-    def columns(step, parts, part, i, blocks):
-        return 0, blocks[step] * parts + part
-
-    in_specs = [pl.BlockSpec((tm, p[0].shape[1]), lambda i, blocks: (i, 0)) for p in pieces]
-    in_specs += [
-        pl.BlockSpec((across, p[0].shape[1]), functools.partial(columns, *p[2:])) for p in pieces
-    ]
-    place = pl.BlockSpec((tm, across), lambda i, blocks: (i, 0))
+    first, last = total is None, scale is not None
+    columns = [(p[0].shape[1],) + tuple(p[2:]) for p in pieces]
     operands = [p[0] for p in pieces] + [p[1] for p in pieces]
+    in_specs = [pl.BlockSpec(memory_space=pl.ANY)] * len(operands)
     if not first:
-        in_specs.append(place)
-        operands.append(total)
-    deep = sum(p[0].shape[1] for p in pieces)
+        operands.append(pltpu.with_memory_space_constraint(total, pltpu.VMEM))
+        in_specs.append(pl.BlockSpec(memory_space=pltpu.VMEM))
+    deep = sum(c[0] for c in columns)
+    if last:
+        shape = jax.ShapeDtypeStruct((rows, across), jnp.float32)
+    else:
+        shape = pltpu.VMEM((rows, across), jnp.float32)
     return pl.pallas_call(
-        functools.partial(add_terms_body, count, first, scale),
-        grid_spec=pltpu.PrefetchScalarGridSpec(
-            num_scalar_prefetch=1,
-            grid=(rows // tm,),
-            in_specs=in_specs,
-            out_specs=[place, pl.BlockSpec((8, 128), lambda i, blocks: (0, 0))],
-        ),
-        out_shape=[
-            jax.ShapeDtypeStruct((rows, across), jnp.float32),
-            jax.ShapeDtypeStruct((8, 128), jnp.float32),
+        functools.partial(add_terms_body, columns, first, scale, tile(rows, 256)),
+        in_specs=[pl.BlockSpec(memory_space=pltpu.SMEM)] + in_specs,
+        out_specs=[
+            pl.BlockSpec(memory_space=pl.ANY if last else pltpu.VMEM),
+            pl.BlockSpec(memory_space=pltpu.VMEM),
         ],
-        input_output_aliases={} if first else {2 * count + 1: 0},
-        compiler_params=pltpu.CompilerParams(vmem_limit_bytes=60 * 1024 * 1024),
+        out_shape=[shape, jax.ShapeDtypeStruct((8, 128), jnp.float32)],
+        input_output_aliases={} if first or last else {len(operands): 0},
+        compiler_params=pltpu.CompilerParams(vmem_limit_bytes=44 * 1024 * 1024),
         cost_estimate=pl.CostEstimate(
             flops=2 * rows * across * deep,
-            bytes_accessed=2 * deep * (rows + across) + (4 if first else 8) * rows * across,
+            bytes_accessed=2 * deep * (rows + across),
             transcendentals=0,
         ),
     )(blocks, *operands)
@@ -123,7 +137,7 @@
                 else:
                     last_one = pass_on(back, cycle, -1) if part else pass_on(ahead, cycle, 1)
                     arrived += [(last_one, b, s, parts, part)]
-            if phase == 0 and s < 3 and s < rounds:
+            if phase == 0 and s < 2 and s < rounds:
                 waiting += arrived[:2]
                 late += arrived[2:]
             else:

time: 486 us -> 448 us (0.922)
  Pallas kernels: 186 us -> 135 us
  local copies, waits for them, and re-layouts: 12.9 us -> 29.8 us
    pallas_call x10 -> x9, Pallas kernels: 186 us -> 135 us  [add_terms(): pl.pallas_call(functools.partial(add_terms_body, columns, first, scale, t...]
    ppermute x30, waiting for transfers between devices: 228 us -> 200 us  [pass_on(): return lax.ppermute(value, ('run', 'grp'), pairs)]
    all_gather x3, waiting for transfers between devices: 8.04 us -> 34.8 us  [local(): lax.all_gather(b, 'blk', axis=1, tiled=True)]
    unnamed x20 -> x38, local copies, waits for them, and re-layouts: 1.23 us -> 20.6 us
  transfers between devices with their start and end apart: 33 -> 33, of which waited for: 17 -> 23; matrix products, arithmetic and copies ran while one was open for 2% -> 2% of each run, Pallas kernels for 35% -> 28%
where the time goes in v3:
time: 448 us; the launch traced here: 447 us
  waiting for transfers between devices  237 us (53%)
  Pallas kernels  135 us (30%)
  starting transfers between devices  31.8 us (7%)
  local copies, waits for them, and re-layouts  29.8 us (7%)
  between operations  13.3 us (3%)
    ppermute x30, waiting for transfers between devices, pass_on(): return lax.ppermute(value, ('run', 'grp'), pairs)  200 us
    pallas_call x9, Pallas kernels, add_terms(): pl.pallas_call(functools.partial(add_terms_body, columns, first, scale, t...  135 us
    all_gather x3, waiting for transfers between devices, local(): lax.all_gather(b, 'blk', axis=1, tiled=True)  34.8 us
    ppermute x30, starting transfers between devices, pass_on(): return lax.ppermute(value, ('run', 'grp'), pairs)  31.7 us
    unnamed x38, local copies, waits for them, and re-layouts  20.6 us
  transfers between devices with their start and end apart: 33, of which 23 were waited for; matrix products, arithmetic and copies ran while one was open for 2% of the time, Pallas kernels for 28%

profile of v3, /device:TPU:0, one launch (start us, length us, event | category | flops | bytes accessed | tf_op | source)
XLA Modules:
  0.0 447.2 jit_solution(8353619844088184311)
XLA Ops:
  13.9 39.0 %collective-permute-done.7.refs_3_ = bf16[1792,512]{1,0:T(8,128)(2,1)} collective-permute-done((bf16[1792,512]{1,0:T(8,128)(2,1)}, bf16[1792,512]{1,0:T(8,128)(2,1)}, u32[]{:S(2)}, u32[]{:S(2)}) %collective-permute-start.7) | collective-permute-done | bytes 1835040 | tf_op jit(solution)/shard_map/ppermute | solution.py:20
  55.1 37.1 %collective-permute-done.refs_1_ = bf16[1792,512]{1,0:T(8,128)(2,1)} collective-permute-done((bf16[1792,512]{1,0:T(8,128)(2,1)}, bf16[1792,512]{1,0:T(8,128)(2,1)}, u32[]{:S(2)}, u32[]{:S(2)}) %collective-permute-start) | collective-permute-done | bytes 1835040 | tf_op jit(solution)/shard_map/ppermute | solution.py:20
  97.1 8.6 %all-gather.4.cloned.1.call-done.refs_3_.refs_4_.refs_5_ = bf16[1792,4096]{1,0:T(8,128)(2,1)} async-done(((bf16[1792,1024]{1,0:T(8,128)(2,1)}), bf16[1792,4096]{1,0:T(8,128)(2,1)}) %all-gather.4.cloned.1.call-update) | async-done | bytes 14680080 | tf_op jit(solution)/shard_map/all_gather | solution.py:104
  105.7 15.2 %shard_map.73 = (f32[1792,1792]{1,0:T(8,128)S(1)}, f32[8,128]{1,0:T(8,128)}) custom-call(s32[8]{0:T(128)} %dynamic-slice_bitcast_fusion.blocks_ref, bf16[1792,512]{1,0:T(8,128)(2,1)} %refs_0_.2, bf16[1792,512]{1,0:T(8,128)(2,1)} %collective-permute-done.refs_1_, bf16[1792,512]{1,0:T(8,128)(2,1)} %collective-permute-done.2.refs_2_, ...), custom_call_target="tpu_custom_call" | custom-call | flops 9865003008 | bytes 11010048 | tf_op jit(solution)/shard_map/pallas_call | solution.py:76
  120.9 5.4 %copy-done = f32[1792,1792]{1,0:T(8,128)} copy-done((f32[1792,1792]{1,0:T(8,128)}, f32[1792,1792]{1,0:T(8,128)S(1)}, u32[]{:S(2)}) %copy-start) | copy-done | bytes 12845080
  126.3 5.2 %collective-permute-done.8.refs_1_ = bf16[1792,512]{1,0:T(8,128)(2,1)} collective-permute-done((bf16[1792,512]{1,0:T(8,128)(2,1)}, bf16[1792,512]{1,0:T(8,128)(2,1)}, u32[]{:S(2)}, u32[]{:S(2)}) %collective-permute-start.8) | collective-permute-done | bytes 1835040 | tf_op jit(solution)/shard_map/ppermute | solution.py:20
  135.8 35.1 %collective-permute-done.1.refs_0_ = bf16[1792,512]{1,0:T(8,128)(2,1)} collective-permute-done((bf16[1792,512]{1,0:T(8,128)(2,1)}, bf16[1792,512]{1,0:T(8,128)(2,1)}, u32[]{:S(2)}, u32[]{:S(2)}) %collective-permute-start.1) | collective-permute-done | bytes 1835040 | tf_op jit(solution)/shard_map/ppermute | solution.py:20
  175.1 26.2 %all-gather.6.cloned.1.call-done.refs_6_.refs_7_.refs_3_.refs_4_.refs_5_ = bf16[1792,4096]{1,0:T(8,128)(2,1)} async-done(((bf16[1792,1024]{1,0:T(8,128)(2,1)}), bf16[1792,4096]{1,0:T(8,128)(2,1)}) %all-gather.6.cloned.1.call-update) | async-done | bytes 14680080 | tf_op jit(solution)/shard_map/all_gather | solution.py:104
  201.3 4.6 %copy-done.1 = f32[1792,1792]{1,0:T(8,128)S(1)} copy-done((f32[1792,1792]{1,0:T(8,128)S(1)}, f32[1792,1792]{1,0:T(8,128)}, u32[]{:S(2)}) %copy-start.1) | copy-done | bytes 12845080
  205.9 20.6 %shard_map.74 = (f32[1792,1792]{1,0:T(8,128)S(1)}, f32[8,128]{1,0:T(8,128)}) custom-call(s32[8]{0:T(128)} %dynamic-slice_bitcast_fusion.blocks_ref, bf16[1792,512]{1,0:T(8,128)(2,1)} %collective-permute-done.1.refs_0_, bf16[1792,512]{1,0:T(8,128)(2,1)} %collective-permute-done.3.refs_1_, bf16[1792,512]{1,0:T(8,128)(2,1)} %refs_2_.1, ...), custom_call_target="tpu_custom_call", output_to_operand_aliasing={{0}: (9, {})} | custom-call | flops 13153337344 | bytes 14680064 | tf_op jit(solution)/shard_map/pallas_call | solution.py:76
  226.6 15.9 %shard_map.75 = (f32[1792,1792]{1,0:T(8,128)S(1)}, f32[8,128]{1,0:T(8,128)}) custom-call(s32[8]{0:T(128)} %dynamic-slice_bitcast_fusion.blocks_ref, bf16[1792,512]{1,0:T(8,128)(2,1)} %collective-permute-done.6.refs_0_, bf16[1792,512]{1,0:T(8,128)(2,1)} %collective-permute-done.8.refs_1_, ...), custom_call_target="tpu_custom_call", output_to_operand_aliasing={{0}: (7, {})} | custom-call | flops 9865003008 | bytes 11010048 | tf_op jit(solution)/shard_map/pallas_call | solution.py:76
  257.7 19.9 %shard_map.76 = (f32[1792,1792]{1,0:T(8,128)S(1)}, f32[8,128]{1,0:T(8,128)}) custom-call(s32[8]{0:T(128)} %dynamic-slice_bitcast_fusion.blocks_ref, bf16[1792,512]{1,0:T(8,128)(2,1)} %collective-permute-done.4.refs_0_, bf16[1792,512]{1,0:T(8,128)(2,1)} %collective-permute-done.5.refs_1_, ...), custom_call_target="tpu_custom_call", output_to_operand_aliasing={{0}: (9, {})} | custom-call | flops 13153337344 | bytes 14680064 | tf_op jit(solution)/shard_map/pallas_call | solution.py:76
  279.7 9.0 %collective-permute-done.10.refs_0_ = bf16[1792,256]{1,0:T(8,128)(2,1)S(1)} collective-permute-done((bf16[1792,256]{1,0:T(8,128)(2,1)}, bf16[1792,256]{1,0:T(8,128)(2,1)S(1)}, u32[]{:S(2)}, u32[]{:S(2)}) %collective-permute-start.10) | collective-permute-done | bytes 917536 | tf_op jit(solution)/shard_map/ppermute | solution.py:20
  292.6 12.1 %shard_map.77 = (f32[1792,1792]{1,0:T(8,128)S(1)}, f32[8,128]{1,0:T(8,128)}) custom-call(s32[8]{0:T(128)} %dynamic-slice_bitcast_fusion.blocks_ref, bf16[1792,256]{1,0:T(8,128)(2,1)} %copy-done.11, bf16[1792,256]{1,0:T(8,128)(2,1)} %copy-done.14, bf16[1792,256]{1,0:T(8,128)(2,1)} %copy-done.6, ...), custom_call_target="tpu_custom_call", output_to_operand_aliasing={{0}: (9, {})} | custom-call | flops 6576668672 | bytes 7340032 | tf_op jit(solution)/shard_map/pallas_call | solution.py:76
  304.7 4.9 %copy-done.2 = f32[1792,1792]{1,0:T(8,128)} copy-done((f32[1792,1792]{1,0:T(8,128)}, f32[1792,1792]{1,0:T(8,128)S(1)}, u32[]{:S(2)}) %copy-start.2) | copy-done | bytes 12845080
  312.3 15.8 %collective-permute-done.14.refs_1_ = bf16[1792,256]{1,0:T(8,128)(2,1)S(1)} collective-permute-done((bf16[1792,256]{1,0:T(8,128)(2,1)}, bf16[1792,256]{1,0:T(8,128)(2,1)S(1)}, u32[]{:S(2)}, u32[]{:S(2)}) %collective-permute-start.14) | collective-permute-done | bytes 917536 | tf_op jit(solution)/shard_map/ppermute | solution.py:20
  332.0 4.6 %copy-done.3 = f32[1792,1792]{1,0:T(8,128)S(1)} copy-done((f32[1792,1792]{1,0:T(8,128)S(1)}, f32[1792,1792]{1,0:T(8,128)}, u32[]{:S(2)}) %copy-start.3) | copy-done | bytes 12845080
  336.7 16.2 %shard_map.78 = (f32[1792,1792]{1,0:T(8,128)S(1)}, f32[8,128]{1,0:T(8,128)}) custom-call(s32[8]{0:T(128)} %dynamic-slice_bitcast_fusion.blocks_ref, bf16[1792,512]{1,0:T(8,128)(2,1)} %refs_0_.3, bf16[1792,256]{1,0:T(8,128)(2,1)} %copy-done.9, bf16[1792,256]{1,0:T(8,128)(2,1)} %collective-permute-done.15.refs_2_, ...), custom_call_target="tpu_custom_call", output_to_operand_aliasing={{0}: (11, {})} | custom-call | flops 9865003008 | bytes 11010048 | tf_op jit(solution)/shard_map/pallas_call | solution.py:76
  355.0 12.5 %collective-permute-done.18.refs_0_ = bf16[1792,256]{1,0:T(8,128)(2,1)} collective-permute-done((bf16[1792,256]{1,0:T(8,128)(2,1)S(1)}, bf16[1792,256]{1,0:T(8,128)(2,1)}, u32[]{:S(2)}, u32[]{:S(2)}) %collective-permute-start.18) | collective-permute-done | bytes 917536 | tf_op jit(solution)/shard_map/ppermute | solution.py:20
  371.3 12.1 %shard_map.79 = (f32[1792,1792]{1,0:T(8,128)S(1)}, f32[8,128]{1,0:T(8,128)}) custom-call(s32[8]{0:T(128)} %dynamic-slice_bitcast_fusion.blocks_ref, bf16[1792,256]{1,0:T(8,128)(2,1)} %collective-permute-done.18.refs_0_, bf16[1792,256]{1,0:T(8,128)(2,1)} %collective-permute-done.19.refs_1_, ...), custom_call_target="tpu_custom_call", output_to_operand_aliasing={{0}: (9, {})} | custom-call | flops 6576668672 | bytes 7340032 | tf_op jit(solution)/shard_map/pallas_call | solution.py:76
  389.2 16.7 %collective-permute-done.22.refs_0_ = bf16[1792,256]{1,0:T(8,128)(2,1)S(1)} collective-permute-done((bf16[1792,256]{1,0:T(8,128)(2,1)}, bf16[1792,256]{1,0:T(8,128)(2,1)S(1)}, u32[]{:S(2)}, u32[]{:S(2)}) %collective-permute-start.22) | collective-permute-done | bytes 917536 | tf_op jit(solution)/shard_map/ppermute | solution.py:20
  410.2 12.1 %shard_map.80 = (f32[1792,1792]{1,0:T(8,128)S(1)}, f32[8,128]{1,0:T(8,128)}) custom-call(s32[8]{0:T(128)} %dynamic-slice_bitcast_fusion.blocks_ref, bf16[1792,256]{1,0:T(8,128)(2,1)} %copy-done.15, bf16[1792,256]{1,0:T(8,128)(2,1)} %copy-done.16, bf16[1792,256]{1,0:T(8,128)(2,1)} %copy-done.12, ...), custom_call_target="tpu_custom_call", output_to_operand_aliasing={{0}: (9, {})} | custom-call | flops 6576668672 | bytes 7340032 | tf_op jit(solution)/shard_map/pallas_call | solution.py:76
  422.3 4.7 %collective-permute-done.29.refs_1_ = bf16[1792,256]{1,0:T(8,128)(2,1)S(1)} collective-permute-done((bf16[1792,256]{1,0:T(8,128)(2,1)S(1)}, bf16[1792,256]{1,0:T(8,128)(2,1)S(1)}, u32[]{:S(2)}, u32[]{:S(2)}) %collective-permute-start.29) | collective-permute-done | bytes 917536 | tf_op jit(solution)/shard_map/ppermute | solution.py:20
  429.6 11.1 %shard_map.81 = (f32[1792,1792]{1,0:T(8,128)}, f32[8,128]{1,0:T(8,128)}) custom-call(s32[8]{0:T(128)} %dynamic-slice_bitcast_fusion.blocks_ref, bf16[1792,256]{1,0:T(8,128)(2,1)} %copy-done.18, bf16[1792,256]{1,0:T(8,128)(2,1)} %copy-done.17, bf16[1792,4096]{1,0:T(8,128)(2,1)} %all-gather.8.cloned.1.call-done.refs_5_.refs_6_.refs_7_.refs_8_.refs_9_.refs_4_.refs_2_.refs_3_, ...), custom_call_target="tpu_custom_call" | custom-call | flops 3288334336 | bytes 3670016 | tf_op jit(solution)/shard_map/pallas_call | solution.py:76
  (98 shorter events, 68.9 us)
Async XLA Ops:
  6.5 99.1 %all-gather.4.cloned.1.call-start = ((), (), s32[]{:S(2)}) async-start(), calls=%async_computation | async-start | bytes 18350080 | tf_op jit(solution)/shard_map/all_gather | solution.py:104
  7.3 194.0 %all-gather.6.cloned.1.call-start = ((), (), s32[]{:S(2)}) async-start(), calls=%async_computation.1 | async-start | bytes 18350080 | tf_op jit(solution)/shard_map/all_gather | solution.py:104
  8.0 324.0 %all-gather.8.cloned.1.call-start = ((), (), s32[]{:S(2)}) async-start(), calls=%async_computation.2 | async-start | bytes 18350080 | tf_op jit(solution)/shard_map/all_gather | solution.py:104
  8.8 44.1 %collective-permute-start.7 = (bf16[1792,512]{1,0:T(8,128)(2,1)}, bf16[1792,512]{1,0:T(8,128)(2,1)}, u32[]{:S(2)}, u32[]{:S(2)}) collective-permute-start(bf16[1792,512]{1,0:T(8,128)(2,1)} %refs_2_.1), channel_id=1, source_target_pairs={{0,1},{1,2},{2,3},{3,19},{19,18},{18,17},{17,16},{16,0},{4,5},{5,6... | collective-permute-start | bytes 5505032 | tf_op jit(solution)/shard_map/ppermute | solution.py:20
  11.8 43.3 %collective-permute-start.6 = (bf16[1792,512]{1,0:T(8,128)(2,1)}, bf16[1792,512]{1,0:T(8,128)(2,1)}, u32[]{:S(2)}, u32[]{:S(2)}) collective-permute-start(bf16[1792,512]{1,0:T(8,128)(2,1)} %refs_2_.1), channel_id=1, source_target_pairs={{0,16},{1,0},{2,1},{3,2},{19,3},{18,19},{17,18},{16,17},{4,20},{5,... | collective-permute-start | bytes 5505032 | tf_op jit(solution)/shard_map/ppermute | solution.py:20
  11.8 80.4 %collective-permute-start = (bf16[1792,512]{1,0:T(8,128)(2,1)}, bf16[1792,512]{1,0:T(8,128)(2,1)}, u32[]{:S(2)}, u32[]{:S(2)}) collective-permute-start(bf16[1792,512]{1,0:T(8,128)(2,1)} %refs_0_.2), channel_id=1, source_target_pairs={{0,1},{1,2},{2,3},{3,19},{19,18},{18,17},{17,16},{16,0},{4,5},{5,6... | collective-permute-start | bytes 5505032 | tf_op jit(solution)/shard_map/ppermute | solution.py:20
  13.9 80.5 %collective-permute-start.2 = (bf16[1792,512]{1,0:T(8,128)(2,1)}, bf16[1792,512]{1,0:T(8,128)(2,1)}, u32[]{:S(2)}, u32[]{:S(2)}) collective-permute-start(bf16[1792,512]{1,0:T(8,128)(2,1)} %refs_0_.2), channel_id=1, source_target_pairs={{0,16},{1,0},{2,1},{3,2},{19,3},{18,19},{17,18},{16,17},{4,20},{5,... | collective-permute-start | bytes 5505032 | tf_op jit(solution)/shard_map/ppermute | solution.py:20
  52.9 78.6 %collective-permute-start.8 = (bf16[1792,512]{1,0:T(8,128)(2,1)}, bf16[1792,512]{1,0:T(8,128)(2,1)}, u32[]{:S(2)}, u32[]{:S(2)}) collective-permute-start(bf16[1792,512]{1,0:T(8,128)(2,1)} %collective-permute-done.7.refs_3_), channel_id=1, source_target_pairs={{0,1},{1,2},{2,3},{3,19},{19,18},{18,17},{17,16},{16,0},{4,5},{5,6... | collective-permute-start | bytes 5505032 | tf_op jit(solution)/shard_map/ppermute | solution.py:20
  55.1 78.6 %collective-permute-start.9 = (bf16[1792,512]{1,0:T(8,128)(2,1)}, bf16[1792,512]{1,0:T(8,128)(2,1)}, u32[]{:S(2)}, u32[]{:S(2)}) collective-permute-start(bf16[1792,512]{1,0:T(8,128)(2,1)} %collective-permute-done.6.refs_0_), channel_id=1, source_target_pairs={{0,16},{1,0},{2,1},{3,2},{19,3},{18,19},{17,18},{16,17},{4,20},{5,... | collective-permute-start | bytes 5505032 | tf_op jit(solution)/shard_map/ppermute | solution.py:20
  92.2 78.6 %collective-permute-start.1 = (bf16[1792,512]{1,0:T(8,128)(2,1)}, bf16[1792,512]{1,0:T(8,128)(2,1)}, u32[]{:S(2)}, u32[]{:S(2)}) collective-permute-start(bf16[1792,512]{1,0:T(8,128)(2,1)} %collective-permute-done.refs_1_), channel_id=1, source_target_pairs={{0,1},{1,2},{2,3},{3,19},{19,18},{18,17},{17,16},{16,0},{4,5},{5,6... | collective-permute-start | bytes 5505032 | tf_op jit(solution)/shard_map/ppermute | solution.py:20
  94.4 78.6 %collective-permute-start.3 = (bf16[1792,512]{1,0:T(8,128)(2,1)}, bf16[1792,512]{1,0:T(8,128)(2,1)}, u32[]{:S(2)}, u32[]{:S(2)}) collective-permute-start(bf16[1792,512]{1,0:T(8,128)(2,1)} %collective-permute-done.2.refs_2_), channel_id=1, source_target_pairs={{0,16},{1,0},{2,1},{3,2},{19,3},{18,19},{17,18},{16,17},{4,20},{5,... | collective-permute-start | bytes 5505032 | tf_op jit(solution)/shard_map/ppermute | solution.py:20
  133.7 108.8 %collective-permute-start.12 = (bf16[1792,512]{1,0:T(8,128)(2,1)}, bf16[1792,512]{1,0:T(8,128)(2,1)S(1)}, u32[]{:S(2)}, u32[]{:S(2)}) collective-permute-start(bf16[1792,512]{1,0:T(8,128)(2,1)} %collective-permute-done.8.refs_1_), channel_id=1, source_target_pairs={{0,1},{1,2},{2,3},{3,19},{19,18},{18,17},{17,16},{16,0},{4,5},{5,6... | collective-permute-start | bytes 5505032 | tf_op jit(solution)/shard_map/ppermute | solution.py:20
  135.3 107.2 %collective-permute-start.13 = (bf16[1792,512]{1,0:T(8,128)(2,1)}, bf16[1792,512]{1,0:T(8,128)(2,1)}, u32[]{:S(2)}, u32[]{:S(2)}) collective-permute-start(bf16[1792,512]{1,0:T(8,128)(2,1)} %collective-permute-done.9.refs_2_), channel_id=1, source_target_pairs={{0,16},{1,0},{2,1},{3,2},{19,3},{18,19},{17,18},{16,17},{4,20},{5,... | collective-permute-start | bytes 5505032 | tf_op jit(solution)/shard_map/ppermute | solution.py:20
  173.1 76.5 %collective-permute-start.4 = (bf16[1792,512]{1,0:T(8,128)(2,1)}, bf16[1792,512]{1,0:T(8,128)(2,1)}, u32[]{:S(2)}, u32[]{:S(2)}) collective-permute-start(bf16[1792,512]{1,0:T(8,128)(2,1)} %collective-permute-done.1.refs_0_), channel_id=1, source_target_pairs={{0,1},{1,2},{2,3},{3,19},{19,18},{18,17},{17,16},{16,0},{4,5},{5,6... | collective-permute-start | bytes 5505032 | tf_op jit(solution)/shard_map/ppermute | solution.py:20
  174.6 76.7 %collective-permute-start.5 = (bf16[1792,512]{1,0:T(8,128)(2,1)}, bf16[1792,512]{1,0:T(8,128)(2,1)}, u32[]{:S(2)}, u32[]{:S(2)}) collective-permute-start(bf16[1792,512]{1,0:T(8,128)(2,1)} %collective-permute-done.3.refs_1_), channel_id=1, source_target_pairs={{0,16},{1,0},{2,1},{3,2},{19,3},{18,19},{17,18},{16,17},{4,20},{5,... | collective-permute-start | bytes 5505032 | tf_op jit(solution)/shard_map/ppermute | solution.py:20
  290.6 37.5 %collective-permute-start.14 = (bf16[1792,256]{1,0:T(8,128)(2,1)}, bf16[1792,256]{1,0:T(8,128)(2,1)S(1)}, u32[]{:S(2)}, u32[]{:S(2)}) collective-permute-start(bf16[1792,256]{1,0:T(8,128)(2,1)} %get-tuple-element.61), channel_id=1, source_target_pairs={{0,1},{1,2},{2,3},{3,19},{19,18},{18,17},{17,16},{16,0},{4,5},{5,6... | collective-permute-start | bytes 2752520 | tf_op jit(solution)/shard_map/ppermute | solution.py:20
  292.2 37.8 %collective-permute-start.15 = (bf16[1792,256]{1,0:T(8,128)(2,1)}, bf16[1792,256]{1,0:T(8,128)(2,1)}, u32[]{:S(2)}, u32[]{:S(2)}) collective-permute-start(bf16[1792,256]{1,0:T(8,128)(2,1)} %get-tuple-element.61), channel_id=1, source_target_pairs={{0,16},{1,0},{2,1},{3,2},{19,3},{18,19},{17,18},{16,17},{4,20},{5,... | collective-permute-start | bytes 2752520 | tf_op jit(solution)/shard_map/ppermute | solution.py:20
  310.2 42.7 %collective-permute-start.24 = (bf16[1792,256]{1,0:T(8,128)(2,1)S(1)}, bf16[1792,256]{1,0:T(8,128)(2,1)}, u32[]{:S(2)}, u32[]{:S(2)}) collective-permute-start(bf16[1792,256]{1,0:T(8,128)(2,1)S(1)} %collective-permute-done.20.refs_3_), channel_id=1, source_target_pairs={{0,1},{1,2},{2,3},{3,19},{19,18},{18,17},{17,16},{16,0},{4,5},{5,6... | collective-permute-start | bytes 2752520 | tf_op jit(solution)/shard_map/ppermute | solution.py:20
  311.9 41.0 %collective-permute-start.25 = (bf16[1792,256]{1,0:T(8,128)(2,1)S(1)}, bf16[1792,256]{1,0:T(8,128)(2,1)}, u32[]{:S(2)}, u32[]{:S(2)}) collective-permute-start(bf16[1792,256]{1,0:T(8,128)(2,1)S(1)} %collective-permute-done.21.refs_4_), channel_id=1, source_target_pairs={{0,16},{1,0},{2,1},{3,2},{19,3},{18,19},{17,18},{16,17},{4,20},{5,... | collective-permute-start | bytes 2752520 | tf_op jit(solution)/shard_map/ppermute | solution.py:20
  330.0 37.5 %collective-permute-start.18 = (bf16[1792,256]{1,0:T(8,128)(2,1)S(1)}, bf16[1792,256]{1,0:T(8,128)(2,1)}, u32[]{:S(2)}, u32[]{:S(2)}) collective-permute-start(bf16[1792,256]{1,0:T(8,128)(2,1)S(1)} %collective-permute-done.14.refs_1_), channel_id=1, source_target_pairs={{0,1},{1,2},{2,3},{3,19},{19,18},{18,17},{17,16},{16,0},{4,5},{5,6... | collective-permute-start | bytes 2752520 | tf_op jit(solution)/shard_map/ppermute | solution.py:20
  331.7 37.7 %collective-permute-start.19 = (bf16[1792,256]{1,0:T(8,128)(2,1)}, bf16[1792,256]{1,0:T(8,128)(2,1)}, u32[]{:S(2)}, u32[]{:S(2)}) collective-permute-start(bf16[1792,256]{1,0:T(8,128)(2,1)} %collective-permute-done.15.refs_2_), channel_id=1, source_target_pairs={{0,16},{1,0},{2,1},{3,2},{19,3},{18,19},{17,18},{16,17},{4,20},{5,... | collective-permute-start | bytes 2752520 | tf_op jit(solution)/shard_map/ppermute | solution.py:20
  369.3 36.6 %collective-permute-start.22 = (bf16[1792,256]{1,0:T(8,128)(2,1)}, bf16[1792,256]{1,0:T(8,128)(2,1)S(1)}, u32[]{:S(2)}, u32[]{:S(2)}) collective-permute-start(bf16[1792,256]{1,0:T(8,128)(2,1)} %collective-permute-done.18.refs_0_), channel_id=1, source_target_pairs={{0,1},{1,2},{2,3},{3,19},{19,18},{18,17},{17,16},{16,0},{4,5},{5,6... | collective-permute-start | bytes 2752520 | tf_op jit(solution)/shard_map/ppermute | solution.py:20
  371.0 37.6 %collective-permute-start.23 = (bf16[1792,256]{1,0:T(8,128)(2,1)}, bf16[1792,256]{1,0:T(8,128)(2,1)S(1)}, u32[]{:S(2)}, u32[]{:S(2)}) collective-permute-start(bf16[1792,256]{1,0:T(8,128)(2,1)} %collective-permute-done.19.refs_1_), channel_id=1, source_target_pairs={{0,16},{1,0},{2,1},{3,2},{19,3},{18,19},{17,18},{16,17},{4,20},{5,... | collective-permute-start | bytes 2752520 | tf_op jit(solution)/shard_map/ppermute | solution.py:20
  388.9 38.2 %collective-permute-start.29 = (bf16[1792,256]{1,0:T(8,128)(2,1)S(1)}, bf16[1792,256]{1,0:T(8,128)(2,1)S(1)}, u32[]{:S(2)}, u32[]{:S(2)}) collective-permute-start(bf16[1792,256]{1,0:T(8,128)(2,1)S(1)} %collective-permute-done.28.refs_3_), channel_id=1, source_target_pairs={{0,16},{1,0},{2,1},{3,2},{19,3},{18,19},{17,18},{16,17},{4,20},{5,... | collective-permute-start | bytes 2752520 | tf_op jit(solution)/shard_map/ppermute | solution.py:20
  (28 other events, 534.1 us)
Sparse Core Ops, SparseCore 0:
  8.9 96.7 all-gather.3
  107.2 94.0 all-gather.5
  202.8 94.0 all-gather.7

commit v4 on v3

v4 whole, which is shorter than its diff:
```python
import functools
import math

import jax
import jax.numpy as jnp
from jax import lax
from jax.experimental import pallas as pl
from jax.experimental.pallas import tpu as pltpu
from jax.sharding import PartitionSpec as P


def cycle_of(runs, grps):
    rows = [[r * grps + g for g in range(grps)] for r in range(runs)]
    return [i for r, row in enumerate(rows) for i in (row if r % 2 == 0 else row[::-1])]


def pass_on(value, cycle, way):
    n = len(cycle)
    pairs = [(cycle[i], cycle[(i + way) % n]) for i in range(n)]
    return lax.ppermute(value, ("run", "grp"), pairs)


def tile(extent, most):
    return max(t for t in range(16, most + 1, 16) if extent % t == 0)


def add_terms_body(groups, first, scale, blocks_ref, *refs):
    count = sum(len(columns) for _, _, columns in groups)
    mark = refs[-1]
    out = refs[-2]
    mark[...] = jnp.zeros_like(mark)
    total = None if first else refs[2 * count]
    across = refs[count].shape[0]

    def add_group(row0, rows, columns, lefts, rights):
        tm = tile(rows, 256)

        def step(*tiles):
            here = pl.ds(pl.multiple_of(row0 + pl.program_id(0) * tm, 16), tm)
            result = None if first else total[here, :]
            for left, right in zip(tiles[: len(columns)], tiles[len(columns) : 2 * len(columns)]):
                term = lax.dot_general(
                    left[...], right[...], (((1,), (1,)), ((), ())),
                    preferred_element_type=jnp.float32,
                )
                result = term if result is None else result + term
            if scale is None:
                out[here, :] = result
            else:
                tiles[-1][...] = result * scale

        def left_place(wide, start):
            return pl.BlockSpec((tm, wide), lambda i: (i + start // tm, 0))

        def right_place(wide, which, parts, part):
            return pl.BlockSpec((across, wide), lambda i: (0, blocks_ref[which] * parts + part))

        specs = [left_place(c[0], c[-1]) for c in columns]
        specs += [right_place(*c[:-1]) for c in columns]
        result_specs, results = [], []
        if scale is not None:
            result_specs = [pl.BlockSpec((tm, across), lambda i: (i + row0 // tm, 0))]
            results = [out]
        pltpu.emit_pipeline(step, grid=(rows // tm,), in_specs=specs, out_specs=result_specs)(
            *lefts, *rights, *results
        )

    at = 0
    for row0, rows, columns in groups:
        end = at + len(columns)
        add_group(row0, rows, columns, refs[at:end], refs[count + at : count + end])
        at = end


def add_terms(total, blocks, groups, scale=None, result=None):
    pieces = [p for _, _, members in groups for p in members]
    shape = pieces[0][1].shape[0] if total is None else total.shape
    first, last = total is None, scale is not None
    if first:
        shape = (groups[0][1], pieces[0][1].shape[0])
    rows, across = shape
    plan = [(row0, n, [(p[0].shape[1],) + tuple(p[2:]) for p in m]) for row0, n, m in groups]
    operands = [p[0] for p in pieces] + [p[1] for p in pieces]
    in_specs = [pl.BlockSpec(memory_space=pl.ANY)] * len(operands)
    aliases = {}
    if not first:
        operands.append(pltpu.with_memory_space_constraint(total, pltpu.VMEM))
        in_specs.append(pl.BlockSpec(memory_space=pltpu.VMEM))
        aliases = {} if last else {len(operands): 0}
    if result is not None:
        operands.append(result)
        in_specs.append(pl.BlockSpec(memory_space=pl.ANY))
        aliases = {len(operands): 0}
    work = sum(n * p[0].shape[1] for _, n, m in groups for p in m)
    return pl.pallas_call(
        functools.partial(add_terms_body, plan, first, scale),
        in_specs=[pl.BlockSpec(memory_space=pltpu.SMEM)] + in_specs,
        out_specs=[
            pl.BlockSpec(memory_space=pl.ANY if last else pltpu.VMEM),
            pl.BlockSpec(memory_space=pltpu.VMEM),
        ],
        out_shape=[
            jax.ShapeDtypeStruct(shape, jnp.float32) if last else pltpu.VMEM(shape, jnp.float32),
            jax.ShapeDtypeStruct((8, 128), jnp.float32),
        ],
        input_output_aliases=aliases,
        compiler_params=pltpu.CompilerParams(vmem_limit_bytes=44 * 1024 * 1024),
        cost_estimate=pl.CostEstimate(
            flops=2 * work * across, bytes_accessed=4 * work, transcendentals=0
        ),
    )(blocks, *operands)


def make_local(runs, grps):
    cycle = cycle_of(runs, grps)
    n = len(cycle)
    source = [[cycle[(cycle.index(d) - s) % n] for s in range(n)] for d in range(n)]

    def local(a_gate, a_up, a_down, b_gate, b_up, b_down):
        depth = a_gate.shape[1]
        half = depth // 2
        here = lax.axis_index(("run", "grp"))
        blocks = jnp.array(source, jnp.int32)[here]
        b_full = [lax.all_gather(b, "blk", axis=1, tiled=True) for b in (b_gate, b_up, b_down)]

        lanes = [
            [(a_gate, 0, 1, 0), (a_down[:, :half], 2, 2, 0)],
            [(a_up, 1, 1, 0), (a_down[:, half:], 2, 2, 1)],
        ]
        rounds = n // 2
        waiting = [(a_gate, b_full[0], 0, 1, 0)]
        late = [(a_up, b_full[1], 0, 1, 0)]
        rows = a_gate.shape[0]
        cut = rows // 4 * 3
        bands = [(0, cut), (cut, rows)]

        def by_bands(pieces):
            return [
                (start, end - start, [
                    (p[0][k],) + p[1:] + (0,) if isinstance(p[0], list) else p + (start,)
                    for p in pieces
                ])
                for k, (start, end) in enumerate(bands)
            ]

        total, marks = None, [None]
        held = [None, None]
        for stage in range(2 * rounds):
            phase, s = stage // rounds, stage % rounds + 1
            if stage == rounds:
                waiting.append((a_down, b_full[2], 0, 1, 0))
            arrived = []
            for lane in range(2):
                a, tensor, parts, part = lanes[lane][phase]
                ahead, back = (a, a) if s == 1 else held[lane]
                if s == 1 and phase:
                    ahead, back, _ = lax.optimization_barrier((ahead, back, held[lane]))
                if stage > 1:
                    ahead, back, _ = lax.optimization_barrier((ahead, back, marks[stage - 1]))
                b = b_full[tensor]
                way = -1 if part else 1
                if phase and n - 4 < 2 * s < n and n % 2 == 0:
                    onward, other = (back, ahead) if part else (ahead, back)
                    onward = [pass_on(onward[start:end], cycle, way) for start, end in bands]
                    other = pass_on(other, cycle, -way)
                    held[lane] = (other, onward) if part else (onward, other)
                    arrived += [
                        (held[lane][0], b, s, parts, part),
                        (held[lane][1], b, n - s, parts, part),
                    ]
                elif 2 * s < n:
                    held[lane] = pass_on(ahead, cycle, 1), pass_on(back, cycle, -1)
                    arrived += [
                        (held[lane][0], b, s, parts, part),
                        (held[lane][1], b, n - s, parts, part),
                    ]
                elif parts == 1:
                    held[lane] = pass_on(ahead[:, :half], cycle, 1), pass_on(back[:, half:], cycle, -1)
                    arrived += [(held[lane][0], b, s, 2, 0), (held[lane][1], b, s, 2, 1)]
                else:
                    last_ones = [pass_on(v, cycle, way) for v in (back if part else ahead)]
                    arrived += [(last_ones, b, s, parts, part)]
            if phase == 0 and s < 2 and s < rounds:
                waiting += arrived[:2]
                late += arrived[2:]
            else:
                waiting += arrived[:2] + late + arrived[2:]
                late = []
            if stage == 2 * rounds - 1:
                break
            if any(isinstance(p[0], list) for p in waiting):
                total, mark = add_terms(total, blocks, by_bands(waiting))
                waiting = []
            while waiting:
                call, deep = [], 0
                while waiting and deep + waiting[0][0].shape[1] <= 4 * depth:
                    deep += waiting[0][0].shape[1]
                    call.append(waiting.pop(0))
                call = [piece + (0,) for piece in call]
                total, mark = add_terms(total, blocks, [(0, rows, call)])
            marks.append(mark)
        scale = 1.0 / math.sqrt(3.0 * depth * n)
        result = None
        for group in by_bands(waiting):
            result, _ = add_terms(total, blocks, [group], scale, result)
        return result

    return local


def solution(mesh):
    placed = (
        P("blk", ("run", "grp")),
        P("blk", ("run", "grp")),
        P("blk", ("run", "grp")),
        P(("run", "grp"), "blk"),
        P(("run", "grp"), "blk"),
        P(("run", "grp"), "blk"),
    )
    local = make_local(mesh.shape["run"], mesh.shape["grp"])
    return jax.shard_map(
        local, mesh=mesh, in_specs=placed, out_specs=P("blk", ("run", "grp")), check_vma=False
    )
```

time: 448 us -> 456 us (1.018)
  waiting for transfers between devices: 237 us -> 227 us
  Pallas kernels: 135 us -> 144 us
  starting transfers between devices: 31.8 us -> 38.2 us
    ppermute x30 -> x34, waiting for transfers between devices: 200 us -> 190 us  [pass_on(): return lax.ppermute(value, ('run', 'grp'), pairs)]
    pallas_call x9 -> x10, Pallas kernels: 135 us -> 144 us  [add_terms(): pl.pallas_call(functools.partial(add_terms_body, plan, first, scale), in_...]
    ppermute x30 -> x34, starting transfers between devices: 31.7 us -> 38.1 us  [pass_on(): return lax.ppermute(value, ('run', 'grp'), pairs)]
    unnamed x38 -> x46, local copies, waits for them, and re-layouts: 20.6 us -> 22.2 us
  transfers between devices with their start and end apart: 33 -> 37, of which waited for: 23 -> 18; matrix products, arithmetic and copies ran while one was open for 2% -> 2% of each run, Pallas kernels for 28% -> 30%
where the time goes in v4:
time: 456 us; the launch traced here: 455 us
  waiting for transfers between devices  227 us (50%)
  Pallas kernels  144 us (32%)
  starting transfers between devices  38.2 us (8%)
  local copies, waits for them, and re-layouts  33.1 us (7%)
  between operations  13.4 us (3%)
    ppermute x34, waiting for transfers between devices, pass_on(): return lax.ppermute(value, ('run', 'grp'), pairs)  190 us
    pallas_call x10, Pallas kernels, add_terms(): pl.pallas_call(functools.partial(add_terms_body, plan, first, scale), in_...  144 us
    ppermute x34, starting transfers between devices, pass_on(): return lax.ppermute(value, ('run', 'grp'), pairs)  38.1 us
    all_gather x3, waiting for transfers between devices, local(): lax.all_gather(b, 'blk', axis=1, tiled=True)  35.1 us
    unnamed x46, local copies, waits for them, and re-layouts  22.2 us
  transfers between devices with their start and end apart: 37, of which 18 were waited for; matrix products, arithmetic and copies ran while one was open for 2% of the time, Pallas kernels for 30%

profile of v4, /device:TPU:0, one launch (start us, length us, event | category | flops | bytes accessed | tf_op | source)
XLA Modules:
  0.0 455.5 jit_solution(16902188156000784887)
XLA Ops:
  13.9 39.0 %collective-permute-done.7.refs_3_ = bf16[1792,512]{1,0:T(8,128)(2,1)} collective-permute-done((bf16[1792,512]{1,0:T(8,128)(2,1)}, bf16[1792,512]{1,0:T(8,128)(2,1)}, u32[]{:S(2)}, u32[]{:S(2)}) %collective-permute-start.7) | collective-permute-done | bytes 1835040 | tf_op jit(solution)/shard_map/ppermute | solution.py:20
  55.1 37.1 %collective-permute-done.refs_1_ = bf16[1792,512]{1,0:T(8,128)(2,1)} collective-permute-done((bf16[1792,512]{1,0:T(8,128)(2,1)}, bf16[1792,512]{1,0:T(8,128)(2,1)}, u32[]{:S(2)}, u32[]{:S(2)}) %collective-permute-start) | collective-permute-done | bytes 1835040 | tf_op jit(solution)/shard_map/ppermute | solution.py:20
  96.8 8.9 %all-gather.4.cloned.1.call-done.refs_3_.refs_4_.refs_5_ = bf16[1792,4096]{1,0:T(8,128)(2,1)} async-done(((bf16[1792,1024]{1,0:T(8,128)(2,1)}), bf16[1792,4096]{1,0:T(8,128)(2,1)}) %all-gather.4.cloned.1.call-update) | async-done | bytes 14680080 | tf_op jit(solution)/shard_map/all_gather | solution.py:124
  105.7 15.2 %shard_map.73 = (f32[1792,1792]{1,0:T(8,128)S(1)}, f32[8,128]{1,0:T(8,128)}) custom-call(s32[8]{0:T(128)} %dynamic-slice_bitcast_fusion.blocks_ref, bf16[1792,512]{1,0:T(8,128)(2,1)} %refs_0_.2, bf16[1792,512]{1,0:T(8,128)(2,1)} %collective-permute-done.refs_1_, bf16[1792,512]{1,0:T(8,128)(2,1)} %collective-permute-done.2.refs_2_, ...), custom_call_target="tpu_custom_call" | custom-call | flops 9865003008 | bytes 11010048 | tf_op jit(solution)/shard_map/pallas_call | solution.py:95
  120.9 5.4 %copy-done = f32[1792,1792]{1,0:T(8,128)} copy-done((f32[1792,1792]{1,0:T(8,128)}, f32[1792,1792]{1,0:T(8,128)S(1)}, u32[]{:S(2)}) %copy-start) | copy-done | bytes 12845080
  126.3 5.2 %collective-permute-done.8.refs_1_ = bf16[1792,512]{1,0:T(8,128)(2,1)} collective-permute-done((bf16[1792,512]{1,0:T(8,128)(2,1)}, bf16[1792,512]{1,0:T(8,128)(2,1)}, u32[]{:S(2)}, u32[]{:S(2)}) %collective-permute-start.8) | collective-permute-done | bytes 1835040 | tf_op jit(solution)/shard_map/ppermute | solution.py:20
  135.8 35.1 %collective-permute-done.1.refs_0_ = bf16[1792,512]{1,0:T(8,128)(2,1)} collective-permute-done((bf16[1792,512]{1,0:T(8,128)(2,1)}, bf16[1792,512]{1,0:T(8,128)(2,1)}, u32[]{:S(2)}, u32[]{:S(2)}) %collective-permute-start.1) | collective-permute-done | bytes 1835040 | tf_op jit(solution)/shard_map/ppermute | solution.py:20
  175.1 26.2 %all-gather.6.cloned.1.call-done.refs_6_.refs_7_.refs_3_.refs_4_.refs_5_ = bf16[1792,4096]{1,0:T(8,128)(2,1)} async-done(((bf16[1792,1024]{1,0:T(8,128)(2,1)}), bf16[1792,4096]{1,0:T(8,128)(2,1)}) %all-gather.6.cloned.1.call-update) | async-done | bytes 14680080 | tf_op jit(solution)/shard_map/all_gather | solution.py:124
  201.3 4.6 %copy-done.1 = f32[1792,1792]{1,0:T(8,128)S(1)} copy-done((f32[1792,1792]{1,0:T(8,128)S(1)}, f32[1792,1792]{1,0:T(8,128)}, u32[]{:S(2)}) %copy-start.1) | copy-done | bytes 12845080
  205.9 20.6 %shard_map.74 = (f32[1792,1792]{1,0:T(8,128)S(1)}, f32[8,128]{1,0:T(8,128)}) custom-call(s32[8]{0:T(128)} %dynamic-slice_bitcast_fusion.blocks_ref, bf16[1792,512]{1,0:T(8,128)(2,1)} %collective-permute-done.1.refs_0_, bf16[1792,512]{1,0:T(8,128)(2,1)} %collective-permute-done.3.refs_1_, bf16[1792,512]{1,0:T(8,128)(2,1)} %refs_2_.1, ...), custom_call_target="tpu_custom_call", output_to_operand_aliasing={{0}: (9, {})} | custom-call | flops 13153337344 | bytes 14680064 | tf_op jit(solution)/shard_map/pallas_call | solution.py:95
  226.6 15.9 %shard_map.75 = (f32[1792,1792]{1,0:T(8,128)S(1)}, f32[8,128]{1,0:T(8,128)}) custom-call(s32[8]{0:T(128)} %dynamic-slice_bitcast_fusion.blocks_ref, bf16[1792,512]{1,0:T(8,128)(2,1)} %collective-permute-done.6.refs_0_, bf16[1792,512]{1,0:T(8,128)(2,1)} %collective-permute-done.8.refs_1_, ...), custom_call_target="tpu_custom_call", output_to_operand_aliasing={{0}: (7, {})} | custom-call | flops 9865003008 | bytes 11010048 | tf_op jit(solution)/shard_map/pallas_call | solution.py:95
  256.8 19.9 %shard_map.76 = (f32[1792,1792]{1,0:T(8,128)S(1)}, f32[8,128]{1,0:T(8,128)}) custom-call(s32[8]{0:T(128)} %dynamic-slice_bitcast_fusion.blocks_ref, bf16[1792,512]{1,0:T(8,128)(2,1)} %collective-permute-done.4.refs_0_, bf16[1792,512]{1,0:T(8,128)(2,1)} %collective-permute-done.5.refs_1_, ...), custom_call_target="tpu_custom_call", output_to_operand_aliasing={{0}: (9, {})} | custom-call | flops 13153337344 | bytes 14680064 | tf_op jit(solution)/shard_map/pallas_call | solution.py:95
  278.8 10.0 %collective-permute-done.10.refs_0_ = bf16[1792,256]{1,0:T(8,128)(2,1)S(1)} collective-permute-done((bf16[1792,256]{1,0:T(8,128)(2,1)}, bf16[1792,256]{1,0:T(8,128)(2,1)S(1)}, u32[]{:S(2)}, u32[]{:S(2)}) %collective-permute-start.10) | collective-permute-done | bytes 917536 | tf_op jit(solution)/shard_map/ppermute | solution.py:20
  292.3 12.1 %shard_map.77 = (f32[1792,1792]{1,0:T(8,128)S(1)}, f32[8,128]{1,0:T(8,128)}) custom-call(s32[8]{0:T(128)} %dynamic-slice_bitcast_fusion.blocks_ref, bf16[1792,256]{1,0:T(8,128)(2,1)} %copy-done.13, bf16[1792,256]{1,0:T(8,128)(2,1)} %copy-done.14, bf16[1792,256]{1,0:T(8,128)(2,1)} %copy-done.11, ...), custom_call_target="tpu_custom_call", output_to_operand_aliasing={{0}: (9, {})} | custom-call | flops 6576668672 | bytes 7340032 | tf_op jit(solution)/shard_map/pallas_call | solution.py:95
  304.4 4.9 %copy-done.2 = f32[1792,1792]{1,0:T(8,128)} copy-done((f32[1792,1792]{1,0:T(8,128)}, f32[1792,1792]{1,0:T(8,128)S(1)}, u32[]{:S(2)}) %copy-start.2) | copy-done | bytes 12845080
  312.1 16.1 %collective-permute-done.14.refs_1_ = bf16[1792,256]{1,0:T(8,128)(2,1)} collective-permute-done((bf16[1792,256]{1,0:T(8,128)(2,1)}, bf16[1792,256]{1,0:T(8,128)(2,1)}, u32[]{:S(2)}, u32[]{:S(2)}) %collective-permute-start.14) | collective-permute-done | bytes 917536 | tf_op jit(solution)/shard_map/ppermute | solution.py:20
  331.7 4.6 %copy-done.3 = f32[1792,1792]{1,0:T(8,128)S(1)} copy-done((f32[1792,1792]{1,0:T(8,128)S(1)}, f32[1792,1792]{1,0:T(8,128)}, u32[]{:S(2)}) %copy-start.3) | copy-done | bytes 12845080
  336.4 16.2 %shard_map.78 = (f32[1792,1792]{1,0:T(8,128)S(1)}, f32[8,128]{1,0:T(8,128)}) custom-call(s32[8]{0:T(128)} %dynamic-slice_bitcast_fusion.blocks_ref, bf16[1792,512]{1,0:T(8,128)(2,1)} %refs_0_.3, bf16[1792,256]{1,0:T(8,128)(2,1)} %collective-permute-done.14.refs_1_, ...), custom_call_target="tpu_custom_call", output_to_operand_aliasing={{0}: (11, {})} | custom-call | flops 9865003008 | bytes 11010048 | tf_op jit(solution)/shard_map/pallas_call | solution.py:95
  354.2 13.2 %collective-permute-done.18.refs_0_ = bf16[1792,256]{1,0:T(8,128)(2,1)S(1)} collective-permute-done((bf16[1792,256]{1,0:T(8,128)(2,1)}, bf16[1792,256]{1,0:T(8,128)(2,1)S(1)}, u32[]{:S(2)}, u32[]{:S(2)}) %collective-permute-start.18) | collective-permute-done | bytes 917536 | tf_op jit(solution)/shard_map/ppermute | solution.py:20
  374.2 22.4 %collective-permute-done.30.refs_7_ = bf16[448,256]{1,0:T(8,128)(2,1)S(1)} collective-permute-done((bf16[448,256]{1,0:T(8,128)(2,1)S(1)}, bf16[448,256]{1,0:T(8,128)(2,1)S(1)}, u32[]{:S(2)}, u32[]{:S(2)}) %collective-permute-start.30) | collective-permute-done | bytes 229408 | tf_op jit(solution)/shard_map/ppermute | solution.py:20
  398.2 12.1 %shard_map.79 = (f32[1792,1792]{1,0:T(8,128)S(1)}, f32[8,128]{1,0:T(8,128)}) custom-call(s32[8]{0:T(128)} %dynamic-slice_bitcast_fusion.blocks_ref, bf16[1792,256]{1,0:T(8,128)(2,1)} %copy-done.7, bf16[1792,256]{1,0:T(8,128)(2,1)} %collective-permute-done.19.refs_1_, bf16[1792,256]{1,0:T(8,128)(2,1)} %copy-done.10, ...), custom_call_target="tpu_custom_call", output_to_operand_aliasing={{0}: (9, {})} | custom-call | flops 6576668672 | bytes 7340032 | tf_op jit(solution)/shard_map/pallas_call | solution.py:95
  415.2 16.5 %shard_map.80 = (f32[1792,1792]{1,0:T(8,128)S(1)}, f32[8,128]{1,0:T(8,128)}) custom-call(s32[8]{0:T(128)} %dynamic-slice_bitcast_fusion.blocks_ref, bf16[1344,256]{1,0:T(8,128)(2,1)} %copy-done.16, bf16[1792,256]{1,0:T(8,128)(2,1)} %copy-done.9, bf16[1792,256]{1,0:T(8,128)(2,1)} %copy-done.8, ...), custom_call_target="tpu_custom_call", output_to_operand_aliasing={{0}: (17, {})} | custom-call | flops 6576668672 | bytes 7340032 | tf_op jit(solution)/shard_map/pallas_call | solution.py:95
  432.8 9.8 %shard_map.81 = (f32[1792,1792]{1,0:T(8,128)}, f32[8,128]{1,0:T(8,128)}) custom-call(s32[8]{0:T(128)} %dynamic-slice_bitcast_fusion.blocks_ref, bf16[1344,256]{1,0:T(8,128)(2,1)} %copy-done.18, bf16[1344,256]{1,0:T(8,128)(2,1)} %copy-done.17, ...), custom_call_target="tpu_custom_call" | custom-call | flops 2466250752 | bytes 2752512 | tf_op jit(solution)/shard_map/pallas_call | solution.py:95
  443.4 5.5 %shard_map.82 = (f32[1792,1792]{1,0:T(8,128)}, f32[8,128]{1,0:T(8,128)}) custom-call(s32[8]{0:T(128)} %dynamic-slice_bitcast_fusion.blocks_ref, bf16[448,256]{1,0:T(8,128)(2,1)} %copy-done.22, bf16[448,256]{1,0:T(8,128)(2,1)} %copy-done.21, ...), custom_call_target="tpu_custom_call", output_to_operand_aliasing={{0}: (6, {})} | custom-call | flops 822083584 | bytes 917504 | tf_op jit(solution)/shard_map/pallas_call | solution.py:95
  (119 shorter events, 65.2 us)
Async XLA Ops:
  6.5 99.1 %all-gather.4.cloned.1.call-start = ((), (), s32[]{:S(2)}) async-start(), calls=%async_computation | async-start | bytes 18350080 | tf_op jit(solution)/shard_map/all_gather | solution.py:124
  7.3 194.0 %all-gather.6.cloned.1.call-start = ((), (), s32[]{:S(2)}) async-start(), calls=%async_computation.1 | async-start | bytes 18350080 | tf_op jit(solution)/shard_map/all_gather | solution.py:124
  8.0 323.7 %all-gather.8.cloned.1.call-start = ((), (), s32[]{:S(2)}) async-start(), calls=%async_computation.2 | async-start | bytes 18350080 | tf_op jit(solution)/shard_map/all_gather | solution.py:124
  8.8 44.1 %collective-permute-start.7 = (bf16[1792,512]{1,0:T(8,128)(2,1)}, bf16[1792,512]{1,0:T(8,128)(2,1)}, u32[]{:S(2)}, u32[]{:S(2)}) collective-permute-start(bf16[1792,512]{1,0:T(8,128)(2,1)} %refs_2_.1), channel_id=1, source_target_pairs={{0,1},{1,2},{2,3},{3,19},{19,18},{18,17},{17,16},{16,0},{4,5},{5,6... | collective-permute-start | bytes 5505032 | tf_op jit(solution)/shard_map/ppermute | solution.py:20
  11.8 43.3 %collective-permute-start.6 = (bf16[1792,512]{1,0:T(8,128)(2,1)}, bf16[1792,512]{1,0:T(8,128)(2,1)}, u32[]{:S(2)}, u32[]{:S(2)}) collective-permute-start(bf16[1792,512]{1,0:T(8,128)(2,1)} %refs_2_.1), channel_id=1, source_target_pairs={{0,16},{1,0},{2,1},{3,2},{19,3},{18,19},{17,18},{16,17},{4,20},{5,... | collective-permute-start | bytes 5505032 | tf_op jit(solution)/shard_map/ppermute | solution.py:20
  11.8 80.4 %collective-permute-start = (bf16[1792,512]{1,0:T(8,128)(2,1)}, bf16[1792,512]{1,0:T(8,128)(2,1)}, u32[]{:S(2)}, u32[]{:S(2)}) collective-permute-start(bf16[1792,512]{1,0:T(8,128)(2,1)} %refs_0_.2), channel_id=1, source_target_pairs={{0,1},{1,2},{2,3},{3,19},{19,18},{18,17},{17,16},{16,0},{4,5},{5,6... | collective-permute-start | bytes 5505032 | tf_op jit(solution)/shard_map/ppermute | solution.py:20
  13.9 80.5 %collective-permute-start.2 = (bf16[1792,512]{1,0:T(8,128)(2,1)}, bf16[1792,512]{1,0:T(8,128)(2,1)}, u32[]{:S(2)}, u32[]{:S(2)}) collective-permute-start(bf16[1792,512]{1,0:T(8,128)(2,1)} %refs_0_.2), channel_id=1, source_target_pairs={{0,16},{1,0},{2,1},{3,2},{19,3},{18,19},{17,18},{16,17},{4,20},{5,... | collective-permute-start | bytes 5505032 | tf_op jit(solution)/shard_map/ppermute | solution.py:20
  52.9 78.6 %collective-permute-start.8 = (bf16[1792,512]{1,0:T(8,128)(2,1)}, bf16[1792,512]{1,0:T(8,128)(2,1)}, u32[]{:S(2)}, u32[]{:S(2)}) collective-permute-start(bf16[1792,512]{1,0:T(8,128)(2,1)} %collective-permute-done.7.refs_3_), channel_id=1, source_target_pairs={{0,1},{1,2},{2,3},{3,19},{19,18},{18,17},{17,16},{16,0},{4,5},{5,6... | collective-permute-start | bytes 5505032 | tf_op jit(solution)/shard_map/ppermute | solution.py:20
  55.1 78.6 %collective-permute-start.9 = (bf16[1792,512]{1,0:T(8,128)(2,1)}, bf16[1792,512]{1,0:T(8,128)(2,1)}, u32[]{:S(2)}, u32[]{:S(2)}) collective-permute-start(bf16[1792,512]{1,0:T(8,128)(2,1)} %collective-permute-done.6.refs_0_), channel_id=1, source_target_pairs={{0,16},{1,0},{2,1},{3,2},{19,3},{18,19},{17,18},{16,17},{4,20},{5,... | collective-permute-start | bytes 5505032 | tf_op jit(solution)/shard_map/ppermute | solution.py:20
  92.2 78.6 %collective-permute-start.1 = (bf16[1792,512]{1,0:T(8,128)(2,1)}, bf16[1792,512]{1,0:T(8,128)(2,1)}, u32[]{:S(2)}, u32[]{:S(2)}) collective-permute-start(bf16[1792,512]{1,0:T(8,128)(2,1)} %collective-permute-done.refs_1_), channel_id=1, source_target_pairs={{0,1},{1,2},{2,3},{3,19},{19,18},{18,17},{17,16},{16,0},{4,5},{5,6... | collective-permute-start | bytes 5505032 | tf_op jit(solution)/shard_map/ppermute | solution.py:20
  94.4 78.6 %collective-permute-start.3 = (bf16[1792,512]{1,0:T(8,128)(2,1)}, bf16[1792,512]{1,0:T(8,128)(2,1)}, u32[]{:S(2)}, u32[]{:S(2)}) collective-permute-start(bf16[1792,512]{1,0:T(8,128)(2,1)} %collective-permute-done.2.refs_2_), channel_id=1, source_target_pairs={{0,16},{1,0},{2,1},{3,2},{19,3},{18,19},{17,18},{16,17},{4,20},{5,... | collective-permute-start | bytes 5505032 | tf_op jit(solution)/shard_map/ppermute | solution.py:20
  133.7 108.8 %collective-permute-start.12 = (bf16[1792,512]{1,0:T(8,128)(2,1)}, bf16[1792,512]{1,0:T(8,128)(2,1)S(1)}, u32[]{:S(2)}, u32[]{:S(2)}) collective-permute-start(bf16[1792,512]{1,0:T(8,128)(2,1)} %collective-permute-done.8.refs_1_), channel_id=1, source_target_pairs={{0,1},{1,2},{2,3},{3,19},{19,18},{18,17},{17,16},{16,0},{4,5},{5,6... | collective-permute-start | bytes 5505032 | tf_op jit(solution)/shard_map/ppermute | solution.py:20
  135.3 107.2 %collective-permute-start.13 = (bf16[1792,512]{1,0:T(8,128)(2,1)}, bf16[1792,512]{1,0:T(8,128)(2,1)}, u32[]{:S(2)}, u32[]{:S(2)}) collective-permute-start(bf16[1792,512]{1,0:T(8,128)(2,1)} %collective-permute-done.9.refs_2_), channel_id=1, source_target_pairs={{0,16},{1,0},{2,1},{3,2},{19,3},{18,19},{17,18},{16,17},{4,20},{5,... | collective-permute-start | bytes 5505032 | tf_op jit(solution)/shard_map/ppermute | solution.py:20
  173.1 76.5 %collective-permute-start.4 = (bf16[1792,512]{1,0:T(8,128)(2,1)}, bf16[1792,512]{1,0:T(8,128)(2,1)}, u32[]{:S(2)}, u32[]{:S(2)}) collective-permute-start(bf16[1792,512]{1,0:T(8,128)(2,1)} %collective-permute-done.1.refs_0_), channel_id=1, source_target_pairs={{0,1},{1,2},{2,3},{3,19},{19,18},{18,17},{17,16},{16,0},{4,5},{5,6... | collective-permute-start | bytes 5505032 | tf_op jit(solution)/shard_map/ppermute | solution.py:20
  174.6 75.7 %collective-permute-start.5 = (bf16[1792,512]{1,0:T(8,128)(2,1)}, bf16[1792,512]{1,0:T(8,128)(2,1)}, u32[]{:S(2)}, u32[]{:S(2)}) collective-permute-start(bf16[1792,512]{1,0:T(8,128)(2,1)} %collective-permute-done.3.refs_1_), channel_id=1, source_target_pairs={{0,16},{1,0},{2,1},{3,2},{19,3},{18,19},{17,18},{16,17},{4,20},{5,... | collective-permute-start | bytes 5505032 | tf_op jit(solution)/shard_map/ppermute | solution.py:20
  290.3 37.9 %collective-permute-start.14 = (bf16[1792,256]{1,0:T(8,128)(2,1)}, bf16[1792,256]{1,0:T(8,128)(2,1)}, u32[]{:S(2)}, u32[]{:S(2)}) collective-permute-start(bf16[1792,256]{1,0:T(8,128)(2,1)} %get-tuple-element.64), channel_id=1, source_target_pairs={{0,1},{1,2},{2,3},{3,19},{19,18},{18,17},{17,16},{16,0},{4,5},{5,6... | collective-permute-start | bytes 2752520 | tf_op jit(solution)/shard_map/ppermute | solution.py:20
  291.8 37.9 %collective-permute-start.15 = (bf16[1792,256]{1,0:T(8,128)(2,1)}, bf16[1792,256]{1,0:T(8,128)(2,1)}, u32[]{:S(2)}, u32[]{:S(2)}) collective-permute-start(bf16[1792,256]{1,0:T(8,128)(2,1)} %get-tuple-element.64), channel_id=1, source_target_pairs={{0,16},{1,0},{2,1},{3,2},{19,3},{18,19},{17,18},{16,17},{4,20},{5,... | collective-permute-start | bytes 2752520 | tf_op jit(solution)/shard_map/ppermute | solution.py:20
  310.0 42.6 %collective-permute-start.25 = (bf16[1792,256]{1,0:T(8,128)(2,1)}, bf16[1792,256]{1,0:T(8,128)(2,1)S(1)}, u32[]{:S(2)}, u32[]{:S(2)}) collective-permute-start(bf16[1792,256]{1,0:T(8,128)(2,1)} %collective-permute-done.20.refs_3_), channel_id=1, source_target_pairs={{0,1},{1,2},{2,3},{3,19},{19,18},{18,17},{17,16},{16,0},{4,5},{5,6... | collective-permute-start | bytes 2752520 | tf_op jit(solution)/shard_map/ppermute | solution.py:20
  311.5 41.1 %collective-permute-start.26 = (bf16[1792,256]{1,0:T(8,128)(2,1)}, bf16[1792,256]{1,0:T(8,128)(2,1)S(1)}, u32[]{:S(2)}, u32[]{:S(2)}) collective-permute-start(bf16[1792,256]{1,0:T(8,128)(2,1)} %collective-permute-done.21.refs_4_), channel_id=1, source_target_pairs={{0,16},{1,0},{2,1},{3,2},{19,3},{18,19},{17,18},{16,17},{4,20},{5,... | collective-permute-start | bytes 2752520 | tf_op jit(solution)/shard_map/ppermute | solution.py:20
  329.7 37.7 %collective-permute-start.18 = (bf16[1792,256]{1,0:T(8,128)(2,1)}, bf16[1792,256]{1,0:T(8,128)(2,1)S(1)}, u32[]{:S(2)}, u32[]{:S(2)}) collective-permute-start(bf16[1792,256]{1,0:T(8,128)(2,1)} %collective-permute-done.14.refs_1_), channel_id=1, source_target_pairs={{0,1},{1,2},{2,3},{3,19},{19,18},{18,17},{17,16},{16,0},{4,5},{5,6... | collective-permute-start | bytes 2752520 | tf_op jit(solution)/shard_map/ppermute | solution.py:20
  352.6 57.7 %collective-permute-start.28 = (bf16[1792,256]{1,0:T(8,128)(2,1)S(1)}, bf16[1792,256]{1,0:T(8,128)(2,1)S(1)}, u32[]{:S(2)}, u32[]{:S(2)}) collective-permute-start(bf16[1792,256]{1,0:T(8,128)(2,1)S(1)} %collective-permute-done.25.refs_2_), channel_id=1, source_target_pairs={{0,1},{1,2},{2,3},{3,19},{19,18},{18,17},{17,16},{16,0},{4,5},{5,6... | collective-permute-start | bytes 2752520 | tf_op jit(solution)/shard_map/ppermute | solution.py:20
  368.2 43.4 %collective-permute-start.24 = (bf16[1792,256]{1,0:T(8,128)(2,1)}, bf16[1792,256]{1,0:T(8,128)(2,1)S(1)}, u32[]{:S(2)}, u32[]{:S(2)}) collective-permute-start(bf16[1792,256]{1,0:T(8,128)(2,1)} %collective-permute-done.19.refs_1_), channel_id=1, source_target_pairs={{0,16},{1,0},{2,1},{3,2},{19,3},{18,19},{17,18},{16,17},{4,20},{5,... | collective-permute-start | bytes 2752520 | tf_op jit(solution)/shard_map/ppermute | solution.py:20
  371.3 39.0 %collective-permute-start.29 = (bf16[1344,256]{1,0:T(8,128)(2,1)S(1)}, bf16[1344,256]{1,0:T(8,128)(2,1)S(1)}, u32[]{:S(2)}, u32[]{:S(2)}) collective-permute-start(bf16[1344,256]{1,0:T(8,128)(2,1)S(1)} %slice.38), channel_id=1, source_target_pairs={{0,16},{1,0},{2,1},{3,2},{19,3},{18,19},{17,18},{16,17},{4,20},{5,... | collective-permute-start | bytes 2064392 | tf_op jit(solution)/shard_map/ppermute | solution.py:20
  373.0 37.9 %collective-permute-start.22 = (bf16[1344,256]{1,0:T(8,128)(2,1)S(1)}, bf16[1344,256]{1,0:T(8,128)(2,1)S(1)}, u32[]{:S(2)}, u32[]{:S(2)}) collective-permute-start(bf16[1344,256]{1,0:T(8,128)(2,1)S(1)} %slice.36), channel_id=1, source_target_pairs={{0,1},{1,2},{2,3},{3,19},{19,18},{18,17},{17,16},{16,0},{4,5},{5,6... | collective-permute-start | bytes 2064392 | tf_op jit(solution)/shard_map/ppermute | solution.py:20
  (36 other events, 690.5 us)
Sparse Core Ops, SparseCore 0:
  8.9 96.7 all-gather.3
  107.2 94.0 all-gather.5
  202.8 94.0 all-gather.7

commit v5 on v3

--- a/solution.py
+++ b/solution.py
@@ -24,22 +24,26 @@
     return max(t for t in range(128, most + 1, 128) if extent % t == 0)
 
 
-def add_terms_body(columns, first, scale, tm, blocks_ref, *refs):
-    count = len(columns)
-    sources = refs[: 2 * count]
-    total = None if first else refs[2 * count]
+def add_terms_body(units, first, scale, tm, blocks_ref, *refs):
+    many = sum(len(wides) for wides, *_ in units)
+    count = len(units)
+    lefts, rights = refs[:many], refs[many : many + count]
+    total = None if first else refs[many + count]
     out, mark = refs[-2:]
     mark[...] = jnp.zeros_like(mark)
-    rows = sources[0].shape[0]
-    across = sources[count].shape[0]
+    rows = lefts[0].shape[0]
+    across = rights[0].shape[0]
 
     def step(*tiles):
-        lefts, rights = tiles[:count], tiles[count : 2 * count]
         here = pl.ds(pl.multiple_of(pl.program_id(0) * tm, tm), tm)
         result = None if first else total[here, :]
-        for left, right in zip(lefts, rights):
+        at = 0
+        for (wides, *_), right in zip(units, tiles[many : many + count]):
+            left = [t[...] for t in tiles[at : at + len(wides)]]
+            at += len(wides)
+            left = left[0] if len(left) == 1 else jnp.concatenate(left, axis=1)
             term = lax.dot_general(
-                left[...], right[...], (((1,), (1,)), ((), ())), preferred_element_type=jnp.float32
+                left, right[...], (((1,), (1,)), ((), ())), preferred_element_type=jnp.float32
             )
             result = term if result is None else result + term
         if scale is None:
@@ -47,34 +51,47 @@
         else:
             tiles[-1][...] = result * scale
 
-    def place(wide, which, parts, part):
+    def place(wides, which, parts, part):
+        wide = sum(wides)
         return pl.BlockSpec((across, wide), lambda i: (0, blocks_ref[which] * parts + part))
 
-    specs = [pl.BlockSpec((tm, wide), lambda i: (i, 0)) for wide, *_ in columns]
-    specs += [place(*c) for c in columns]
+    specs = [pl.BlockSpec((tm, wide), lambda i: (i, 0)) for wides, *_ in units for wide in wides]
+    specs += [place(*u) for u in units]
     result_specs = [] if scale is None else [pl.BlockSpec((tm, across), lambda i: (i, 0))]
     results = [] if scale is None else [out]
     pltpu.emit_pipeline(step, grid=(rows // tm,), in_specs=specs, out_specs=result_specs)(
-        *sources, *results
+        *lefts, *rights, *results
     )
+
+
+def join_halves(pieces):
+    units = {}
+    for a, b, which, parts, part in pieces:
+        if parts == 2 and any(p[2:] == (which, 2, 1 - part) for p in pieces):
+            units.setdefault((which, 1, 0), ({}, b))[0][part] = a
+        else:
+            units[which, parts, part] = ({0: a}, b)
+    return [([m[k] for k in sorted(m)], b) + key for key, (m, b) in units.items()]
 
 
 def add_terms(total, blocks, pieces, scale=None):
     rows, across = pieces[0][0].shape[0], pieces[0][1].shape[0]
     first, last = total is None, scale is not None
-    columns = [(p[0].shape[1],) + tuple(p[2:]) for p in pieces]
-    operands = [p[0] for p in pieces] + [p[1] for p in pieces]
+    units = [u for b in dict.fromkeys(id(p[1]) for p in pieces)
+             for u in join_halves([p for p in pieces if id(p[1]) == b])]
+    plan = [([a.shape[1] for a in u[0]],) + tuple(u[2:]) for u in units]
+    operands = [a for u in units for a in u[0]] + [u[1] for u in units]
     in_specs = [pl.BlockSpec(memory_space=pl.ANY)] * len(operands)
     if not first:
         operands.append(pltpu.with_memory_space_constraint(total, pltpu.VMEM))
         in_specs.append(pl.BlockSpec(memory_space=pltpu.VMEM))
-    deep = sum(c[0] for c in columns)
+    deep = sum(p[0].shape[1] for p in pieces)
     if last:
         shape = jax.ShapeDtypeStruct((rows, across), jnp.float32)
     else:
         shape = pltpu.VMEM((rows, across), jnp.float32)
     return pl.pallas_call(
-        functools.partial(add_terms_body, columns, first, scale, tile(rows, 256)),
+        functools.partial(add_terms_body, plan, first, scale, tile(rows, 448 if last else 256)),
         in_specs=[pl.BlockSpec(memory_space=pltpu.SMEM)] + in_specs,
         out_specs=[
             pl.BlockSpec(memory_space=pl.ANY if last else pltpu.VMEM),
@@ -82,7 +99,7 @@
         ],
         out_shape=[shape, jax.ShapeDtypeStruct((8, 128), jnp.float32)],
         input_output_aliases={} if first or last else {len(operands): 0},
-        compiler_params=pltpu.CompilerParams(vmem_limit_bytes=44 * 1024 * 1024),
+        compiler_params=pltpu.CompilerParams(vmem_limit_bytes=(28 if last else 44) * 1024 * 1024),
         cost_estimate=pl.CostEstimate(
             flops=2 * rows * across * deep,
             bytes_accessed=2 * deep * (rows + across),
@@ -122,7 +139,12 @@
                 ahead, back = (a, a) if s == 1 else held[lane]
                 if s == 1 and phase:
                     ahead, back, _ = lax.optimization_barrier((ahead, back, held[lane]))
-                if stage > 1:
+                if stage == 2 * rounds - 1 and n % 2 == 0:
+                    if part:
+                        back, _ = lax.optimization_barrier((back, marks[stage - 1]))
+                    else:
+                        ahead, _ = lax.optimization_barrier((ahead, marks[stage - 1]))
+                elif stage > 1:
                     ahead, back, _ = lax.optimization_barrier((ahead, back, marks[stage - 1]))
                 b = b_full[tensor]
                 if 2 * s < n:

time: 448 us -> 446 us (level)
    unnamed x38 -> x30, local copies, waits for them, and re-layouts: 20.6 us -> 20.8 us
  transfers between devices with their start and end apart: 33 -> 33, of which waited for: 23 -> 22; matrix products, arithmetic and copies ran while one was open for 2% -> 1% of each run, Pallas kernels for 28% -> 28%
where the time goes in v5:
time: 446 us
  waiting for transfers between devices  239 us (54%)
  Pallas kernels  135 us (30%)
  starting transfers between devices  31.2 us (7%)
  local copies, waits for them, and re-layouts  27.2 us (6%)
  between operations  13.3 us (3%)
    ppermute x30, waiting for transfers between devices, pass_on(): return lax.ppermute(value, ('run', 'grp'), pairs)  202 us
    pallas_call x9, Pallas kernels, add_terms(): pl.pallas_call(functools.partial(add_terms_body, plan, first, scale, tile...  135 us
    all_gather x3, waiting for transfers between devices, local(): lax.all_gather(b, 'blk', axis=1, tiled=True)  34.8 us
    ppermute x30, starting transfers between devices, pass_on(): return lax.ppermute(value, ('run', 'grp'), pairs)  31.1 us
    unnamed x30, local copies, waits for them, and re-layouts  20.8 us
  transfers between devices with their start and end apart: 33, of which 22 were waited for; matrix products, arithmetic and copies ran while one was open for 1% of the time, Pallas kernels for 28%

profile of v5, /device:TPU:0, one launch (start us, length us, event | category | flops | bytes accessed | tf_op | source)
XLA Modules:
  0.0 445.6 jit_solution(7929301650386899697)
XLA Ops:
  13.9 39.0 %collective-permute-done.7.refs_3_ = bf16[1792,512]{1,0:T(8,128)(2,1)} collective-permute-done((bf16[1792,512]{1,0:T(8,128)(2,1)}, bf16[1792,512]{1,0:T(8,128)(2,1)}, u32[]{:S(2)}, u32[]{:S(2)}) %collective-permute-start.7) | collective-permute-done | bytes 1835040 | tf_op jit(solution)/shard_map/ppermute | solution.py:20
  55.1 37.1 %collective-permute-done.refs_1_ = bf16[1792,512]{1,0:T(8,128)(2,1)} collective-permute-done((bf16[1792,512]{1,0:T(8,128)(2,1)}, bf16[1792,512]{1,0:T(8,128)(2,1)}, u32[]{:S(2)}, u32[]{:S(2)}) %collective-permute-start) | collective-permute-done | bytes 1835040 | tf_op jit(solution)/shard_map/ppermute | solution.py:20
  97.0 8.6 %all-gather.4.cloned.1.call-done.refs_3_.refs_4_.refs_5_ = bf16[1792,4096]{1,0:T(8,128)(2,1)} async-done(((bf16[1792,1024]{1,0:T(8,128)(2,1)}), bf16[1792,4096]{1,0:T(8,128)(2,1)}) %all-gather.4.cloned.1.call-update) | async-done | bytes 14680080 | tf_op jit(solution)/shard_map/all_gather | solution.py:121
  105.7 15.2 %shard_map.73 = (f32[1792,1792]{1,0:T(8,128)S(1)}, f32[8,128]{1,0:T(8,128)}) custom-call(s32[8]{0:T(128)} %dynamic-slice_bitcast_fusion.blocks_ref, bf16[1792,512]{1,0:T(8,128)(2,1)} %refs_0_.2, bf16[1792,512]{1,0:T(8,128)(2,1)} %collective-permute-done.refs_1_, bf16[1792,512]{1,0:T(8,128)(2,1)} %collective-permute-done.2.refs_2_, ...), custom_call_target="tpu_custom_call" | custom-call | flops 9865003008 | bytes 11010048 | tf_op jit(solution)/shard_map/pallas_call | solution.py:93
  120.9 5.4 %copy-done = f32[1792,1792]{1,0:T(8,128)} copy-done((f32[1792,1792]{1,0:T(8,128)}, f32[1792,1792]{1,0:T(8,128)S(1)}, u32[]{:S(2)}) %copy-start) | copy-done | bytes 12845080
  126.3 5.2 %collective-permute-done.8.refs_1_ = bf16[1792,512]{1,0:T(8,128)(2,1)} collective-permute-done((bf16[1792,512]{1,0:T(8,128)(2,1)}, bf16[1792,512]{1,0:T(8,128)(2,1)}, u32[]{:S(2)}, u32[]{:S(2)}) %collective-permute-start.8) | collective-permute-done | bytes 1835040 | tf_op jit(solution)/shard_map/ppermute | solution.py:20
  135.8 35.1 %collective-permute-done.1.refs_0_ = bf16[1792,512]{1,0:T(8,128)(2,1)} collective-permute-done((bf16[1792,512]{1,0:T(8,128)(2,1)}, bf16[1792,512]{1,0:T(8,128)(2,1)}, u32[]{:S(2)}, u32[]{:S(2)}) %collective-permute-start.1) | collective-permute-done | bytes 1835040 | tf_op jit(solution)/shard_map/ppermute | solution.py:20
  175.1 26.2 %all-gather.6.cloned.1.call-done.refs_6_.refs_7_.refs_3_.refs_4_.refs_5_ = bf16[1792,4096]{1,0:T(8,128)(2,1)} async-done(((bf16[1792,1024]{1,0:T(8,128)(2,1)}), bf16[1792,4096]{1,0:T(8,128)(2,1)}) %all-gather.6.cloned.1.call-update) | async-done | bytes 14680080 | tf_op jit(solution)/shard_map/all_gather | solution.py:121
  201.3 4.6 %copy-done.1 = f32[1792,1792]{1,0:T(8,128)S(1)} copy-done((f32[1792,1792]{1,0:T(8,128)S(1)}, f32[1792,1792]{1,0:T(8,128)}, u32[]{:S(2)}) %copy-start.1) | copy-done | bytes 12845080
  205.9 20.6 %shard_map.74 = (f32[1792,1792]{1,0:T(8,128)S(1)}, f32[8,128]{1,0:T(8,128)}) custom-call(s32[8]{0:T(128)} %dynamic-slice_bitcast_fusion.blocks_ref, bf16[1792,512]{1,0:T(8,128)(2,1)} %collective-permute-done.1.refs_0_, bf16[1792,512]{1,0:T(8,128)(2,1)} %collective-permute-done.3.refs_1_, bf16[1792,512]{1,0:T(8,128)(2,1)} %refs_2_.1, ...), custom_call_target="tpu_custom_call", output_to_operand_aliasing={{0}: (9, {})} | custom-call | flops 13153337344 | bytes 14680064 | tf_op jit(solution)/shard_map/pallas_call | solution.py:93
  226.6 15.9 %shard_map.75 = (f32[1792,1792]{1,0:T(8,128)S(1)}, f32[8,128]{1,0:T(8,128)}) custom-call(s32[8]{0:T(128)} %dynamic-slice_bitcast_fusion.blocks_ref, bf16[1792,512]{1,0:T(8,128)(2,1)} %collective-permute-done.6.refs_0_, bf16[1792,512]{1,0:T(8,128)(2,1)} %collective-permute-done.8.refs_1_, ...), custom_call_target="tpu_custom_call", output_to_operand_aliasing={{0}: (7, {})} | custom-call | flops 9865003008 | bytes 11010048 | tf_op jit(solution)/shard_map/pallas_call | solution.py:93
  256.3 20.0 %shard_map.76 = (f32[1792,1792]{1,0:T(8,128)S(1)}, f32[8,128]{1,0:T(8,128)}) custom-call(s32[8]{0:T(128)} %dynamic-slice_bitcast_fusion.blocks_ref, bf16[1792,512]{1,0:T(8,128)(2,1)} %collective-permute-done.4.refs_0_, bf16[1792,512]{1,0:T(8,128)(2,1)} %collective-permute-done.5.refs_1_, ...), custom_call_target="tpu_custom_call", output_to_operand_aliasing={{0}: (9, {})} | custom-call | flops 13153337344 | bytes 14680064 | tf_op jit(solution)/shard_map/pallas_call | solution.py:93
  278.4 10.4 %collective-permute-done.10.refs_0_ = bf16[1792,256]{1,0:T(8,128)(2,1)} collective-permute-done((bf16[1792,256]{1,0:T(8,128)(2,1)S(1)}, bf16[1792,256]{1,0:T(8,128)(2,1)}, u32[]{:S(2)}, u32[]{:S(2)}) %collective-permute-start.10) | collective-permute-done | bytes 917536 | tf_op jit(solution)/shard_map/ppermute | solution.py:20
  293.1 12.2 %shard_map.77 = (f32[1792,1792]{1,0:T(8,128)S(1)}, f32[8,128]{1,0:T(8,128)}) custom-call(s32[8]{0:T(128)} %dynamic-slice_bitcast_fusion.blocks_ref, bf16[1792,256]{1,0:T(8,128)(2,1)} %collective-permute-done.10.refs_0_, bf16[1792,256]{1,0:T(8,128)(2,1)} %collective-permute-done.11.refs_1_, ...), custom_call_target="tpu_custom_call", output_to_operand_aliasing={{0}: (7, {})} | custom-call | flops 6576668672 | bytes 7340032 | tf_op jit(solution)/shard_map/pallas_call | solution.py:93
  305.3 4.9 %copy-done.2 = f32[1792,1792]{1,0:T(8,128)} copy-done((f32[1792,1792]{1,0:T(8,128)}, f32[1792,1792]{1,0:T(8,128)S(1)}, u32[]{:S(2)}) %copy-start.2) | copy-done | bytes 12845080
  312.6 15.5 %collective-permute-done.14.refs_1_ = bf16[1792,256]{1,0:T(8,128)(2,1)S(1)} collective-permute-done((bf16[1792,256]{1,0:T(8,128)(2,1)S(1)}, bf16[1792,256]{1,0:T(8,128)(2,1)S(1)}, u32[]{:S(2)}, u32[]{:S(2)}) %collective-permute-start.14) | collective-permute-done | bytes 917536 | tf_op jit(solution)/shard_map/ppermute | solution.py:20
  332.4 4.6 %copy-done.3 = f32[1792,1792]{1,0:T(8,128)S(1)} copy-done((f32[1792,1792]{1,0:T(8,128)S(1)}, f32[1792,1792]{1,0:T(8,128)}, u32[]{:S(2)}) %copy-start.3) | copy-done | bytes 12845080
  337.0 16.1 %shard_map.78 = (f32[1792,1792]{1,0:T(8,128)S(1)}, f32[8,128]{1,0:T(8,128)}) custom-call(s32[8]{0:T(128)} %dynamic-slice_bitcast_fusion.blocks_ref, bf16[1792,512]{1,0:T(8,128)(2,1)} %refs_0_.3, bf16[1792,256]{1,0:T(8,128)(2,1)} %copy-done.9, bf16[1792,256]{1,0:T(8,128)(2,1)} %copy-done.7, ...), custom_call_target="tpu_custom_call", output_to_operand_aliasing={{0}: (9, {})} | custom-call | flops 9865003008 | bytes 11010048 | tf_op jit(solution)/shard_map/pallas_call | solution.py:93
  353.2 13.4 %collective-permute-done.18.refs_0_ = bf16[1792,256]{1,0:T(8,128)(2,1)} collective-permute-done((bf16[1792,256]{1,0:T(8,128)(2,1)S(1)}, bf16[1792,256]{1,0:T(8,128)(2,1)}, u32[]{:S(2)}, u32[]{:S(2)}) %collective-permute-start.18) | collective-permute-done | bytes 917536 | tf_op jit(solution)/shard_map/ppermute | solution.py:20
  373.3 12.2 %shard_map.79 = (f32[1792,1792]{1,0:T(8,128)S(1)}, f32[8,128]{1,0:T(8,128)}) custom-call(s32[8]{0:T(128)} %dynamic-slice_bitcast_fusion.blocks_ref, bf16[1792,256]{1,0:T(8,128)(2,1)} %collective-permute-done.18.refs_0_, bf16[1792,256]{1,0:T(8,128)(2,1)} %collective-permute-done.23.refs_1_, ...), custom_call_target="tpu_custom_call", output_to_operand_aliasing={{0}: (7, {})} | custom-call | flops 6576668672 | bytes 7340032 | tf_op jit(solution)/shard_map/pallas_call | solution.py:93
  389.2 3.9 collective-permute-done.22.refs_0_
  394.7 18.1 %collective-permute-done.28.refs_1_ = bf16[1792,256]{1,0:T(8,128)(2,1)S(1)} collective-permute-done((bf16[1792,256]{1,0:T(8,128)(2,1)}, bf16[1792,256]{1,0:T(8,128)(2,1)S(1)}, u32[]{:S(2)}, u32[]{:S(2)}) %collective-permute-start.28) | collective-permute-done | bytes 917536 | tf_op jit(solution)/shard_map/ppermute | solution.py:20
  414.1 12.3 %shard_map.80 = (f32[1792,1792]{1,0:T(8,128)S(1)}, f32[8,128]{1,0:T(8,128)}) custom-call(s32[8]{0:T(128)} %dynamic-slice_bitcast_fusion.blocks_ref, bf16[1792,256]{1,0:T(8,128)(2,1)} %copy-done.12, bf16[1792,256]{1,0:T(8,128)(2,1)} %copy-done.13, bf16[1792,256]{1,0:T(8,128)(2,1)} %copy-done.14, ...), custom_call_target="tpu_custom_call", output_to_operand_aliasing={{0}: (7, {})} | custom-call | flops 6576668672 | bytes 7340032 | tf_op jit(solution)/shard_map/pallas_call | solution.py:93
  428.6 10.4 %shard_map.81 = (f32[1792,1792]{1,0:T(8,128)}, f32[8,128]{1,0:T(8,128)}) custom-call(s32[8]{0:T(128)S(1)} %copy-done.4, bf16[1792,256]{1,0:T(8,128)(2,1)S(1)} %collective-permute-done.25.refs_0_, bf16[1792,256]{1,0:T(8,128)(2,1)S(1)} %collective-permute-done.27.refs_1_, ...), custom_call_target="tpu_custom_call" | custom-call | flops 3288334336 | bytes 3670016 | tf_op jit(solution)/shard_map/pallas_call | solution.py:93
  (90 shorter events, 65.0 us)
Async XLA Ops:
  6.5 99.1 %all-gather.4.cloned.1.call-start = ((), (), s32[]{:S(2)}) async-start(), calls=%async_computation | async-start | bytes 18350080 | tf_op jit(solution)/shard_map/all_gather | solution.py:121
  7.3 194.0 %all-gather.6.cloned.1.call-start = ((), (), s32[]{:S(2)}) async-start(), calls=%async_computation.1 | async-start | bytes 18350080 | tf_op jit(solution)/shard_map/all_gather | solution.py:121
  8.0 324.4 %all-gather.8.cloned.1.call-start = ((), (), s32[]{:S(2)}) async-start(), calls=%async_computation.2 | async-start | bytes 18350080 | tf_op jit(solution)/shard_map/all_gather | solution.py:121
  8.8 44.1 %collective-permute-start.7 = (bf16[1792,512]{1,0:T(8,128)(2,1)}, bf16[1792,512]{1,0:T(8,128)(2,1)}, u32[]{:S(2)}, u32[]{:S(2)}) collective-permute-start(bf16[1792,512]{1,0:T(8,128)(2,1)} %refs_2_.1), channel_id=1, source_target_pairs={{0,1},{1,2},{2,3},{3,19},{19,18},{18,17},{17,16},{16,0},{4,5},{5,6... | collective-permute-start | bytes 5505032 | tf_op jit(solution)/shard_map/ppermute | solution.py:20
  11.8 43.3 %collective-permute-start.6 = (bf16[1792,512]{1,0:T(8,128)(2,1)}, bf16[1792,512]{1,0:T(8,128)(2,1)}, u32[]{:S(2)}, u32[]{:S(2)}) collective-permute-start(bf16[1792,512]{1,0:T(8,128)(2,1)} %refs_2_.1), channel_id=1, source_target_pairs={{0,16},{1,0},{2,1},{3,2},{19,3},{18,19},{17,18},{16,17},{4,20},{5,... | collective-permute-start | bytes 5505032 | tf_op jit(solution)/shard_map/ppermute | solution.py:20
  11.8 80.4 %collective-permute-start = (bf16[1792,512]{1,0:T(8,128)(2,1)}, bf16[1792,512]{1,0:T(8,128)(2,1)}, u32[]{:S(2)}, u32[]{:S(2)}) collective-permute-start(bf16[1792,512]{1,0:T(8,128)(2,1)} %refs_0_.2), channel_id=1, source_target_pairs={{0,1},{1,2},{2,3},{3,19},{19,18},{18,17},{17,16},{16,0},{4,5},{5,6... | collective-permute-start | bytes 5505032 | tf_op jit(solution)/shard_map/ppermute | solution.py:20
  13.9 80.5 %collective-permute-start.2 = (bf16[1792,512]{1,0:T(8,128)(2,1)}, bf16[1792,512]{1,0:T(8,128)(2,1)}, u32[]{:S(2)}, u32[]{:S(2)}) collective-permute-start(bf16[1792,512]{1,0:T(8,128)(2,1)} %refs_0_.2), channel_id=1, source_target_pairs={{0,16},{1,0},{2,1},{3,2},{19,3},{18,19},{17,18},{16,17},{4,20},{5,... | collective-permute-start | bytes 5505032 | tf_op jit(solution)/shard_map/ppermute | solution.py:20
  52.9 78.6 %collective-permute-start.8 = (bf16[1792,512]{1,0:T(8,128)(2,1)}, bf16[1792,512]{1,0:T(8,128)(2,1)}, u32[]{:S(2)}, u32[]{:S(2)}) collective-permute-start(bf16[1792,512]{1,0:T(8,128)(2,1)} %collective-permute-done.7.refs_3_), channel_id=1, source_target_pairs={{0,1},{1,2},{2,3},{3,19},{19,18},{18,17},{17,16},{16,0},{4,5},{5,6... | collective-permute-start | bytes 5505032 | tf_op jit(solution)/shard_map/ppermute | solution.py:20
  55.1 78.6 %collective-permute-start.9 = (bf16[1792,512]{1,0:T(8,128)(2,1)}, bf16[1792,512]{1,0:T(8,128)(2,1)}, u32[]{:S(2)}, u32[]{:S(2)}) collective-permute-start(bf16[1792,512]{1,0:T(8,128)(2,1)} %collective-permute-done.6.refs_0_), channel_id=1, source_target_pairs={{0,16},{1,0},{2,1},{3,2},{19,3},{18,19},{17,18},{16,17},{4,20},{5,... | collective-permute-start | bytes 5505032 | tf_op jit(solution)/shard_map/ppermute | solution.py:20
  92.2 78.6 %collective-permute-start.1 = (bf16[1792,512]{1,0:T(8,128)(2,1)}, bf16[1792,512]{1,0:T(8,128)(2,1)}, u32[]{:S(2)}, u32[]{:S(2)}) collective-permute-start(bf16[1792,512]{1,0:T(8,128)(2,1)} %collective-permute-done.refs_1_), channel_id=1, source_target_pairs={{0,1},{1,2},{2,3},{3,19},{19,18},{18,17},{17,16},{16,0},{4,5},{5,6... | collective-permute-start | bytes 5505032 | tf_op jit(solution)/shard_map/ppermute | solution.py:20
  94.4 78.6 %collective-permute-start.3 = (bf16[1792,512]{1,0:T(8,128)(2,1)}, bf16[1792,512]{1,0:T(8,128)(2,1)}, u32[]{:S(2)}, u32[]{:S(2)}) collective-permute-start(bf16[1792,512]{1,0:T(8,128)(2,1)} %collective-permute-done.2.refs_2_), channel_id=1, source_target_pairs={{0,16},{1,0},{2,1},{3,2},{19,3},{18,19},{17,18},{16,17},{4,20},{5,... | collective-permute-start | bytes 5505032 | tf_op jit(solution)/shard_map/ppermute | solution.py:20
  133.7 108.8 %collective-permute-start.12 = (bf16[1792,512]{1,0:T(8,128)(2,1)}, bf16[1792,512]{1,0:T(8,128)(2,1)S(1)}, u32[]{:S(2)}, u32[]{:S(2)}) collective-permute-start(bf16[1792,512]{1,0:T(8,128)(2,1)} %collective-permute-done.8.refs_1_), channel_id=1, source_target_pairs={{0,1},{1,2},{2,3},{3,19},{19,18},{18,17},{17,16},{16,0},{4,5},{5,6... | collective-permute-start | bytes 5505032 | tf_op jit(solution)/shard_map/ppermute | solution.py:20
  135.3 107.2 %collective-permute-start.13 = (bf16[1792,512]{1,0:T(8,128)(2,1)}, bf16[1792,512]{1,0:T(8,128)(2,1)}, u32[]{:S(2)}, u32[]{:S(2)}) collective-permute-start(bf16[1792,512]{1,0:T(8,128)(2,1)} %collective-permute-done.9.refs_2_), channel_id=1, source_target_pairs={{0,16},{1,0},{2,1},{3,2},{19,3},{18,19},{17,18},{16,17},{4,20},{5,... | collective-permute-start | bytes 5505032 | tf_op jit(solution)/shard_map/ppermute | solution.py:20
  173.1 76.5 %collective-permute-start.4 = (bf16[1792,512]{1,0:T(8,128)(2,1)}, bf16[1792,512]{1,0:T(8,128)(2,1)}, u32[]{:S(2)}, u32[]{:S(2)}) collective-permute-start(bf16[1792,512]{1,0:T(8,128)(2,1)} %collective-permute-done.1.refs_0_), channel_id=1, source_target_pairs={{0,1},{1,2},{2,3},{3,19},{19,18},{18,17},{17,16},{16,0},{4,5},{5,6... | collective-permute-start | bytes 5505032 | tf_op jit(solution)/shard_map/ppermute | solution.py:20
  174.6 77.1 %collective-permute-start.5 = (bf16[1792,512]{1,0:T(8,128)(2,1)}, bf16[1792,512]{1,0:T(8,128)(2,1)}, u32[]{:S(2)}, u32[]{:S(2)}) collective-permute-start(bf16[1792,512]{1,0:T(8,128)(2,1)} %collective-permute-done.3.refs_1_), channel_id=1, source_target_pairs={{0,16},{1,0},{2,1},{3,2},{19,3},{18,19},{17,18},{16,17},{4,20},{5,... | collective-permute-start | bytes 5505032 | tf_op jit(solution)/shard_map/ppermute | solution.py:20
  291.0 37.0 %collective-permute-start.14 = (bf16[1792,256]{1,0:T(8,128)(2,1)S(1)}, bf16[1792,256]{1,0:T(8,128)(2,1)S(1)}, u32[]{:S(2)}, u32[]{:S(2)}) collective-permute-start(bf16[1792,256]{1,0:T(8,128)(2,1)S(1)} %copy-done.10), channel_id=1, source_target_pairs={{0,1},{1,2},{2,3},{3,19},{19,18},{18,17},{17,16},{16,0},{4,5},{5,6... | collective-permute-start | bytes 2752520 | tf_op jit(solution)/shard_map/ppermute | solution.py:20
  292.6 37.7 %collective-permute-start.15 = (bf16[1792,256]{1,0:T(8,128)(2,1)S(1)}, bf16[1792,256]{1,0:T(8,128)(2,1)}, u32[]{:S(2)}, u32[]{:S(2)}) collective-permute-start(bf16[1792,256]{1,0:T(8,128)(2,1)S(1)} %copy-done.10), channel_id=1, source_target_pairs={{0,16},{1,0},{2,1},{3,2},{19,3},{18,19},{17,18},{16,17},{4,20},{5,... | collective-permute-start | bytes 2752520 | tf_op jit(solution)/shard_map/ppermute | solution.py:20
  310.6 42.6 %collective-permute-start.23 = (bf16[1792,256]{1,0:T(8,128)(2,1)S(1)}, bf16[1792,256]{1,0:T(8,128)(2,1)}, u32[]{:S(2)}, u32[]{:S(2)}) collective-permute-start(bf16[1792,256]{1,0:T(8,128)(2,1)S(1)} %collective-permute-done.20.refs_2_), channel_id=1, source_target_pairs={{0,1},{1,2},{2,3},{3,19},{19,18},{18,17},{17,16},{16,0},{4,5},{5,6... | collective-permute-start | bytes 2752520 | tf_op jit(solution)/shard_map/ppermute | solution.py:20
  312.2 41.0 %collective-permute-start.24 = (bf16[1792,256]{1,0:T(8,128)(2,1)S(1)}, bf16[1792,256]{1,0:T(8,128)(2,1)}, u32[]{:S(2)}, u32[]{:S(2)}) collective-permute-start(bf16[1792,256]{1,0:T(8,128)(2,1)S(1)} %collective-permute-done.21.refs_4_), channel_id=1, source_target_pairs={{0,16},{1,0},{2,1},{3,2},{19,3},{18,19},{17,18},{16,17},{4,20},{5,... | collective-permute-start | bytes 2752520 | tf_op jit(solution)/shard_map/ppermute | solution.py:20
  330.3 36.3 %collective-permute-start.18 = (bf16[1792,256]{1,0:T(8,128)(2,1)S(1)}, bf16[1792,256]{1,0:T(8,128)(2,1)}, u32[]{:S(2)}, u32[]{:S(2)}) collective-permute-start(bf16[1792,256]{1,0:T(8,128)(2,1)S(1)} %collective-permute-done.14.refs_1_), channel_id=1, source_target_pairs={{0,1},{1,2},{2,3},{3,19},{19,18},{18,17},{17,16},{16,0},{4,5},{5,6... | collective-permute-start | bytes 2752520 | tf_op jit(solution)/shard_map/ppermute | solution.py:20
  331.9 37.7 %collective-permute-start.19 = (bf16[1792,256]{1,0:T(8,128)(2,1)}, bf16[1792,256]{1,0:T(8,128)(2,1)}, u32[]{:S(2)}, u32[]{:S(2)}) collective-permute-start(bf16[1792,256]{1,0:T(8,128)(2,1)} %collective-permute-done.15.refs_3_), channel_id=1, source_target_pairs={{0,16},{1,0},{2,1},{3,2},{19,3},{18,19},{17,18},{16,17},{4,20},{5,... | collective-permute-start | bytes 2752520 | tf_op jit(solution)/shard_map/ppermute | solution.py:20
  371.2 41.6 %collective-permute-start.28 = (bf16[1792,256]{1,0:T(8,128)(2,1)}, bf16[1792,256]{1,0:T(8,128)(2,1)S(1)}, u32[]{:S(2)}, u32[]{:S(2)}) collective-permute-start(bf16[1792,256]{1,0:T(8,128)(2,1)} %collective-permute-done.23.refs_1_), channel_id=1, source_target_pairs={{0,1},{1,2},{2,3},{3,19},{19,18},{18,17},{17,16},{16,0},{4,5},{5,6... | collective-permute-start | bytes 2752520 | tf_op jit(solution)/shard_map/ppermute | solution.py:20
  372.8 40.0 %collective-permute-start.29 = (bf16[1792,256]{1,0:T(8,128)(2,1)}, bf16[1792,256]{1,0:T(8,128)(2,1)S(1)}, u32[]{:S(2)}, u32[]{:S(2)}) collective-permute-start(bf16[1792,256]{1,0:T(8,128)(2,1)} %collective-permute-done.19.refs_2_), channel_id=1, source_target_pairs={{0,16},{1,0},{2,1},{3,2},{19,3},{18,19},{17,18},{16,17},{4,20},{5,... | collective-permute-start | bytes 2752520 | tf_op jit(solution)/shard_map/ppermute | solution.py:20
  389.2 37.9 %collective-permute-start.27 = (bf16[1792,256]{1,0:T(8,128)(2,1)S(1)}, bf16[1792,256]{1,0:T(8,128)(2,1)S(1)}, u32[]{:S(2)}, u32[]{:S(2)}) collective-permute-start(bf16[1792,256]{1,0:T(8,128)(2,1)S(1)} %collective-permute-done.26.refs_3_), channel_id=1, source_target_pairs={{0,16},{1,0},{2,1},{3,2},{19,3},{18,19},{17,18},{16,17},{4,20},{5,... | collective-permute-start | bytes 2752520 | tf_op jit(solution)/shard_map/ppermute | solution.py:20
  (24 other events, 550.4 us)
Sparse Core Ops, SparseCore 0:
  8.9 96.7 all-gather.3
  107.2 94.0 all-gather.5
  202.8 94.0 all-gather.7

commit v6 on v5

--- a/solution.py
+++ b/solution.py
@@ -91,7 +91,7 @@
     else:
         shape = pltpu.VMEM((rows, across), jnp.float32)
     return pl.pallas_call(
-        functools.partial(add_terms_body, plan, first, scale, tile(rows, 448 if last else 256)),
+        functools.partial(add_terms_body, plan, first, scale, tile(rows, 256)),
         in_specs=[pl.BlockSpec(memory_space=pltpu.SMEM)] + in_specs,
         out_specs=[
             pl.BlockSpec(memory_space=pl.ANY if last else pltpu.VMEM),

time: 446 us -> 446 us (level)
  no operation moved by 1% of the time
where the time goes in v6:
time: 446 us
  waiting for transfers between devices  239 us (54%)
  Pallas kernels  135 us (30%)
  starting transfers between devices  31.2 us (7%)
  local copies, waits for them, and re-layouts  27.2 us (6%)
  between operations  13.3 us (3%)
    ppermute x30, waiting for transfers between devices, pass_on(): return lax.ppermute(value, ('run', 'grp'), pairs)  202 us
    pallas_call x9, Pallas kernels, add_terms(): pl.pallas_call(functools.partial(add_terms_body, plan, first, scale, tile...  135 us
    all_gather x3, waiting for transfers between devices, local(): lax.all_gather(b, 'blk', axis=1, tiled=True)  34.8 us
    ppermute x30, starting transfers between devices, pass_on(): return lax.ppermute(value, ('run', 'grp'), pairs)  31.1 us
    unnamed x30, local copies, waits for them, and re-layouts  20.8 us
  transfers between devices with their start and end apart: 33, of which 22 were waited for; matrix products, arithmetic and copies ran while one was open for 1% of the time, Pallas kernels for 28%

profile of v6, /device:TPU:0, one launch (start us, length us, event | category | flops | bytes accessed | tf_op | source)
XLA Modules:
  0.0 445.6 jit_solution(7929301650386899697)
XLA Ops:
  13.9 39.0 %collective-permute-done.7.refs_3_ = bf16[1792,512]{1,0:T(8,128)(2,1)} collective-permute-done((bf16[1792,512]{1,0:T(8,128)(2,1)}, bf16[1792,512]{1,0:T(8,128)(2,1)}, u32[]{:S(2)}, u32[]{:S(2)}) %collective-permute-start.7) | collective-permute-done | bytes 1835040 | tf_op jit(solution)/shard_map/ppermute | solution.py:20
  55.1 37.1 %collective-permute-done.refs_1_ = bf16[1792,512]{1,0:T(8,128)(2,1)} collective-permute-done((bf16[1792,512]{1,0:T(8,128)(2,1)}, bf16[1792,512]{1,0:T(8,128)(2,1)}, u32[]{:S(2)}, u32[]{:S(2)}) %collective-permute-start) | collective-permute-done | bytes 1835040 | tf_op jit(solution)/shard_map/ppermute | solution.py:20
  97.0 8.6 %all-gather.4.cloned.1.call-done.refs_3_.refs_4_.refs_5_ = bf16[1792,4096]{1,0:T(8,128)(2,1)} async-done(((bf16[1792,1024]{1,0:T(8,128)(2,1)}), bf16[1792,4096]{1,0:T(8,128)(2,1)}) %all-gather.4.cloned.1.call-update) | async-done | bytes 14680080 | tf_op jit(solution)/shard_map/all_gather | solution.py:121
  105.7 15.2 %shard_map.73 = (f32[1792,1792]{1,0:T(8,128)S(1)}, f32[8,128]{1,0:T(8,128)}) custom-call(s32[8]{0:T(128)} %dynamic-slice_bitcast_fusion.blocks_ref, bf16[1792,512]{1,0:T(8,128)(2,1)} %refs_0_.2, bf16[1792,512]{1,0:T(8,128)(2,1)} %collective-permute-done.refs_1_, bf16[1792,512]{1,0:T(8,128)(2,1)} %collective-permute-done.2.refs_2_, ...), custom_call_target="tpu_custom_call" | custom-call | flops 9865003008 | bytes 11010048 | tf_op jit(solution)/shard_map/pallas_call | solution.py:93
  120.9 5.4 %copy-done = f32[1792,1792]{1,0:T(8,128)} copy-done((f32[1792,1792]{1,0:T(8,128)}, f32[1792,1792]{1,0:T(8,128)S(1)}, u32[]{:S(2)}) %copy-start) | copy-done | bytes 12845080
  126.3 5.2 %collective-permute-done.8.refs_1_ = bf16[1792,512]{1,0:T(8,128)(2,1)} collective-permute-done((bf16[1792,512]{1,0:T(8,128)(2,1)}, bf16[1792,512]{1,0:T(8,128)(2,1)}, u32[]{:S(2)}, u32[]{:S(2)}) %collective-permute-start.8) | collective-permute-done | bytes 1835040 | tf_op jit(solution)/shard_map/ppermute | solution.py:20
  135.8 35.1 %collective-permute-done.1.refs_0_ = bf16[1792,512]{1,0:T(8,128)(2,1)} collective-permute-done((bf16[1792,512]{1,0:T(8,128)(2,1)}, bf16[1792,512]{1,0:T(8,128)(2,1)}, u32[]{:S(2)}, u32[]{:S(2)}) %collective-permute-start.1) | collective-permute-done | bytes 1835040 | tf_op jit(solution)/shard_map/ppermute | solution.py:20
  175.1 26.2 %all-gather.6.cloned.1.call-done.refs_6_.refs_7_.refs_3_.refs_4_.refs_5_ = bf16[1792,4096]{1,0:T(8,128)(2,1)} async-done(((bf16[1792,1024]{1,0:T(8,128)(2,1)}), bf16[1792,4096]{1,0:T(8,128)(2,1)}) %all-gather.6.cloned.1.call-update) | async-done | bytes 14680080 | tf_op jit(solution)/shard_map/all_gather | solution.py:121
  201.3 4.6 %copy-done.1 = f32[1792,1792]{1,0:T(8,128)S(1)} copy-done((f32[1792,1792]{1,0:T(8,128)S(1)}, f32[1792,1792]{1,0:T(8,128)}, u32[]{:S(2)}) %copy-start.1) | copy-done | bytes 12845080
  205.9 20.6 %shard_map.74 = (f32[1792,1792]{1,0:T(8,128)S(1)}, f32[8,128]{1,0:T(8,128)}) custom-call(s32[8]{0:T(128)} %dynamic-slice_bitcast_fusion.blocks_ref, bf16[1792,512]{1,0:T(8,128)(2,1)} %collective-permute-done.1.refs_0_, bf16[1792,512]{1,0:T(8,128)(2,1)} %collective-permute-done.3.refs_1_, bf16[1792,512]{1,0:T(8,128)(2,1)} %refs_2_.1, ...), custom_call_target="tpu_custom_call", output_to_operand_aliasing={{0}: (9, {})} | custom-call | flops 13153337344 | bytes 14680064 | tf_op jit(solution)/shard_map/pallas_call | solution.py:93
  226.6 15.9 %shard_map.75 = (f32[1792,1792]{1,0:T(8,128)S(1)}, f32[8,128]{1,0:T(8,128)}) custom-call(s32[8]{0:T(128)} %dynamic-slice_bitcast_fusion.blocks_ref, bf16[1792,512]{1,0:T(8,128)(2,1)} %collective-permute-done.6.refs_0_, bf16[1792,512]{1,0:T(8,128)(2,1)} %collective-permute-done.8.refs_1_, ...), custom_call_target="tpu_custom_call", output_to_operand_aliasing={{0}: (7, {})} | custom-call | flops 9865003008 | bytes 11010048 | tf_op jit(solution)/shard_map/pallas_call | solution.py:93
  256.3 20.0 %shard_map.76 = (f32[1792,1792]{1,0:T(8,128)S(1)}, f32[8,128]{1,0:T(8,128)}) custom-call(s32[8]{0:T(128)} %dynamic-slice_bitcast_fusion.blocks_ref, bf16[1792,512]{1,0:T(8,128)(2,1)} %collective-permute-done.4.refs_0_, bf16[1792,512]{1,0:T(8,128)(2,1)} %collective-permute-done.5.refs_1_, ...), custom_call_target="tpu_custom_call", output_to_operand_aliasing={{0}: (9, {})} | custom-call | flops 13153337344 | bytes 14680064 | tf_op jit(solution)/shard_map/pallas_call | solution.py:93
  278.4 10.4 %collective-permute-done.10.refs_0_ = bf16[1792,256]{1,0:T(8,128)(2,1)} collective-permute-done((bf16[1792,256]{1,0:T(8,128)(2,1)S(1)}, bf16[1792,256]{1,0:T(8,128)(2,1)}, u32[]{:S(2)}, u32[]{:S(2)}) %collective-permute-start.10) | collective-permute-done | bytes 917536 | tf_op jit(solution)/shard_map/ppermute | solution.py:20
  293.1 12.2 %shard_map.77 = (f32[1792,1792]{1,0:T(8,128)S(1)}, f32[8,128]{1,0:T(8,128)}) custom-call(s32[8]{0:T(128)} %dynamic-slice_bitcast_fusion.blocks_ref, bf16[1792,256]{1,0:T(8,128)(2,1)} %collective-permute-done.10.refs_0_, bf16[1792,256]{1,0:T(8,128)(2,1)} %collective-permute-done.11.refs_1_, ...), custom_call_target="tpu_custom_call", output_to_operand_aliasing={{0}: (7, {})} | custom-call | flops 6576668672 | bytes 7340032 | tf_op jit(solution)/shard_map/pallas_call | solution.py:93
  305.3 4.9 %copy-done.2 = f32[1792,1792]{1,0:T(8,128)} copy-done((f32[1792,1792]{1,0:T(8,128)}, f32[1792,1792]{1,0:T(8,128)S(1)}, u32[]{:S(2)}) %copy-start.2) | copy-done | bytes 12845080
  312.6 15.5 %collective-permute-done.14.refs_1_ = bf16[1792,256]{1,0:T(8,128)(2,1)S(1)} collective-permute-done((bf16[1792,256]{1,0:T(8,128)(2,1)S(1)}, bf16[1792,256]{1,0:T(8,128)(2,1)S(1)}, u32[]{:S(2)}, u32[]{:S(2)}) %collective-permute-start.14) | collective-permute-done | bytes 917536 | tf_op jit(solution)/shard_map/ppermute | solution.py:20
  332.4 4.6 %copy-done.3 = f32[1792,1792]{1,0:T(8,128)S(1)} copy-done((f32[1792,1792]{1,0:T(8,128)S(1)}, f32[1792,1792]{1,0:T(8,128)}, u32[]{:S(2)}) %copy-start.3) | copy-done | bytes 12845080
  337.0 16.1 %shard_map.78 = (f32[1792,1792]{1,0:T(8,128)S(1)}, f32[8,128]{1,0:T(8,128)}) custom-call(s32[8]{0:T(128)} %dynamic-slice_bitcast_fusion.blocks_ref, bf16[1792,512]{1,0:T(8,128)(2,1)} %refs_0_.3, bf16[1792,256]{1,0:T(8,128)(2,1)} %copy-done.9, bf16[1792,256]{1,0:T(8,128)(2,1)} %copy-done.7, ...), custom_call_target="tpu_custom_call", output_to_operand_aliasing={{0}: (9, {})} | custom-call | flops 9865003008 | bytes 11010048 | tf_op jit(solution)/shard_map/pallas_call | solution.py:93
  353.2 13.4 %collective-permute-done.18.refs_0_ = bf16[1792,256]{1,0:T(8,128)(2,1)} collective-permute-done((bf16[1792,256]{1,0:T(8,128)(2,1)S(1)}, bf16[1792,256]{1,0:T(8,128)(2,1)}, u32[]{:S(2)}, u32[]{:S(2)}) %collective-permute-start.18) | collective-permute-done | bytes 917536 | tf_op jit(solution)/shard_map/ppermute | solution.py:20
  373.3 12.2 %shard_map.79 = (f32[1792,1792]{1,0:T(8,128)S(1)}, f32[8,128]{1,0:T(8,128)}) custom-call(s32[8]{0:T(128)} %dynamic-slice_bitcast_fusion.blocks_ref, bf16[1792,256]{1,0:T(8,128)(2,1)} %collective-permute-done.18.refs_0_, bf16[1792,256]{1,0:T(8,128)(2,1)} %collective-permute-done.23.refs_1_, ...), custom_call_target="tpu_custom_call", output_to_operand_aliasing={{0}: (7, {})} | custom-call | flops 6576668672 | bytes 7340032 | tf_op jit(solution)/shard_map/pallas_call | solution.py:93
  389.2 3.9 collective-permute-done.22.refs_0_
  394.7 18.1 %collective-permute-done.28.refs_1_ = bf16[1792,256]{1,0:T(8,128)(2,1)S(1)} collective-permute-done((bf16[1792,256]{1,0:T(8,128)(2,1)}, bf16[1792,256]{1,0:T(8,128)(2,1)S(1)}, u32[]{:S(2)}, u32[]{:S(2)}) %collective-permute-start.28) | collective-permute-done | bytes 917536 | tf_op jit(solution)/shard_map/ppermute | solution.py:20
  414.1 12.3 %shard_map.80 = (f32[1792,1792]{1,0:T(8,128)S(1)}, f32[8,128]{1,0:T(8,128)}) custom-call(s32[8]{0:T(128)} %dynamic-slice_bitcast_fusion.blocks_ref, bf16[1792,256]{1,0:T(8,128)(2,1)} %copy-done.12, bf16[1792,256]{1,0:T(8,128)(2,1)} %copy-done.13, bf16[1792,256]{1,0:T(8,128)(2,1)} %copy-done.14, ...), custom_call_target="tpu_custom_call", output_to_operand_aliasing={{0}: (7, {})} | custom-call | flops 6576668672 | bytes 7340032 | tf_op jit(solution)/shard_map/pallas_call | solution.py:93
  428.6 10.4 %shard_map.81 = (f32[1792,1792]{1,0:T(8,128)}, f32[8,128]{1,0:T(8,128)}) custom-call(s32[8]{0:T(128)S(1)} %copy-done.4, bf16[1792,256]{1,0:T(8,128)(2,1)S(1)} %collective-permute-done.25.refs_0_, bf16[1792,256]{1,0:T(8,128)(2,1)S(1)} %collective-permute-done.27.refs_1_, ...), custom_call_target="tpu_custom_call" | custom-call | flops 3288334336 | bytes 3670016 | tf_op jit(solution)/shard_map/pallas_call | solution.py:93
  (90 shorter events, 65.0 us)
Async XLA Ops:
  6.5 99.1 %all-gather.4.cloned.1.call-start = ((), (), s32[]{:S(2)}) async-start(), calls=%async_computation | async-start | bytes 18350080 | tf_op jit(solution)/shard_map/all_gather | solution.py:121
  7.3 194.0 %all-gather.6.cloned.1.call-start = ((), (), s32[]{:S(2)}) async-start(), calls=%async_computation.1 | async-start | bytes 18350080 | tf_op jit(solution)/shard_map/all_gather | solution.py:121
  8.0 324.4 %all-gather.8.cloned.1.call-start = ((), (), s32[]{:S(2)}) async-start(), calls=%async_computation.2 | async-start | bytes 18350080 | tf_op jit(solution)/shard_map/all_gather | solution.py:121
  8.8 44.1 %collective-permute-start.7 = (bf16[1792,512]{1,0:T(8,128)(2,1)}, bf16[1792,512]{1,0:T(8,128)(2,1)}, u32[]{:S(2)}, u32[]{:S(2)}) collective-permute-start(bf16[1792,512]{1,0:T(8,128)(2,1)} %refs_2_.1), channel_id=1, source_target_pairs={{0,1},{1,2},{2,3},{3,19},{19,18},{18,17},{17,16},{16,0},{4,5},{5,6... | collective-permute-start | bytes 5505032 | tf_op jit(solution)/shard_map/ppermute | solution.py:20
  11.8 43.3 %collective-permute-start.6 = (bf16[1792,512]{1,0:T(8,128)(2,1)}, bf16[1792,512]{1,0:T(8,128)(2,1)}, u32[]{:S(2)}, u32[]{:S(2)}) collective-permute-start(bf16[1792,512]{1,0:T(8,128)(2,1)} %refs_2_.1), channel_id=1, source_target_pairs={{0,16},{1,0},{2,1},{3,2},{19,3},{18,19},{17,18},{16,17},{4,20},{5,... | collective-permute-start | bytes 5505032 | tf_op jit(solution)/shard_map/ppermute | solution.py:20
  11.8 80.4 %collective-permute-start = (bf16[1792,512]{1,0:T(8,128)(2,1)}, bf16[1792,512]{1,0:T(8,128)(2,1)}, u32[]{:S(2)}, u32[]{:S(2)}) collective-permute-start(bf16[1792,512]{1,0:T(8,128)(2,1)} %refs_0_.2), channel_id=1, source_target_pairs={{0,1},{1,2},{2,3},{3,19},{19,18},{18,17},{17,16},{16,0},{4,5},{5,6... | collective-permute-start | bytes 5505032 | tf_op jit(solution)/shard_map/ppermute | solution.py:20
  13.9 80.5 %collective-permute-start.2 = (bf16[1792,512]{1,0:T(8,128)(2,1)}, bf16[1792,512]{1,0:T(8,128)(2,1)}, u32[]{:S(2)}, u32[]{:S(2)}) collective-permute-start(bf16[1792,512]{1,0:T(8,128)(2,1)} %refs_0_.2), channel_id=1, source_target_pairs={{0,16},{1,0},{2,1},{3,2},{19,3},{18,19},{17,18},{16,17},{4,20},{5,... | collective-permute-start | bytes 5505032 | tf_op jit(solution)/shard_map/ppermute | solution.py:20
  52.9 78.6 %collective-permute-start.8 = (bf16[1792,512]{1,0:T(8,128)(2,1)}, bf16[1792,512]{1,0:T(8,128)(2,1)}, u32[]{:S(2)}, u32[]{:S(2)}) collective-permute-start(bf16[1792,512]{1,0:T(8,128)(2,1)} %collective-permute-done.7.refs_3_), channel_id=1, source_target_pairs={{0,1},{1,2},{2,3},{3,19},{19,18},{18,17},{17,16},{16,0},{4,5},{5,6... | collective-permute-start | bytes 5505032 | tf_op jit(solution)/shard_map/ppermute | solution.py:20
  55.1 78.6 %collective-permute-start.9 = (bf16[1792,512]{1,0:T(8,128)(2,1)}, bf16[1792,512]{1,0:T(8,128)(2,1)}, u32[]{:S(2)}, u32[]{:S(2)}) collective-permute-start(bf16[1792,512]{1,0:T(8,128)(2,1)} %collective-permute-done.6.refs_0_), channel_id=1, source_target_pairs={{0,16},{1,0},{2,1},{3,2},{19,3},{18,19},{17,18},{16,17},{4,20},{5,... | collective-permute-start | bytes 5505032 | tf_op jit(solution)/shard_map/ppermute | solution.py:20
  92.2 78.6 %collective-permute-start.1 = (bf16[1792,512]{1,0:T(8,128)(2,1)}, bf16[1792,512]{1,0:T(8,128)(2,1)}, u32[]{:S(2)}, u32[]{:S(2)}) collective-permute-start(bf16[1792,512]{1,0:T(8,128)(2,1)} %collective-permute-done.refs_1_), channel_id=1, source_target_pairs={{0,1},{1,2},{2,3},{3,19},{19,18},{18,17},{17,16},{16,0},{4,5},{5,6... | collective-permute-start | bytes 5505032 | tf_op jit(solution)/shard_map/ppermute | solution.py:20
  94.4 78.6 %collective-permute-start.3 = (bf16[1792,512]{1,0:T(8,128)(2,1)}, bf16[1792,512]{1,0:T(8,128)(2,1)}, u32[]{:S(2)}, u32[]{:S(2)}) collective-permute-start(bf16[1792,512]{1,0:T(8,128)(2,1)} %collective-permute-done.2.refs_2_), channel_id=1, source_target_pairs={{0,16},{1,0},{2,1},{3,2},{19,3},{18,19},{17,18},{16,17},{4,20},{5,... | collective-permute-start | bytes 5505032 | tf_op jit(solution)/shard_map/ppermute | solution.py:20
  133.7 108.8 %collective-permute-start.12 = (bf16[1792,512]{1,0:T(8,128)(2,1)}, bf16[1792,512]{1,0:T(8,128)(2,1)S(1)}, u32[]{:S(2)}, u32[]{:S(2)}) collective-permute-start(bf16[1792,512]{1,0:T(8,128)(2,1)} %collective-permute-done.8.refs_1_), channel_id=1, source_target_pairs={{0,1},{1,2},{2,3},{3,19},{19,18},{18,17},{17,16},{16,0},{4,5},{5,6... | collective-permute-start | bytes 5505032 | tf_op jit(solution)/shard_map/ppermute | solution.py:20
  135.3 107.2 %collective-permute-start.13 = (bf16[1792,512]{1,0:T(8,128)(2,1)}, bf16[1792,512]{1,0:T(8,128)(2,1)}, u32[]{:S(2)}, u32[]{:S(2)}) collective-permute-start(bf16[1792,512]{1,0:T(8,128)(2,1)} %collective-permute-done.9.refs_2_), channel_id=1, source_target_pairs={{0,16},{1,0},{2,1},{3,2},{19,3},{18,19},{17,18},{16,17},{4,20},{5,... | collective-permute-start | bytes 5505032 | tf_op jit(solution)/shard_map/ppermute | solution.py:20
  173.1 76.5 %collective-permute-start.4 = (bf16[1792,512]{1,0:T(8,128)(2,1)}, bf16[1792,512]{1,0:T(8,128)(2,1)}, u32[]{:S(2)}, u32[]{:S(2)}) collective-permute-start(bf16[1792,512]{1,0:T(8,128)(2,1)} %collective-permute-done.1.refs_0_), channel_id=1, source_target_pairs={{0,1},{1,2},{2,3},{3,19},{19,18},{18,17},{17,16},{16,0},{4,5},{5,6... | collective-permute-start | bytes 5505032 | tf_op jit(solution)/shard_map/ppermute | solution.py:20
  174.6 77.1 %collective-permute-start.5 = (bf16[1792,512]{1,0:T(8,128)(2,1)}, bf16[1792,512]{1,0:T(8,128)(2,1)}, u32[]{:S(2)}, u32[]{:S(2)}) collective-permute-start(bf16[1792,512]{1,0:T(8,128)(2,1)} %collective-permute-done.3.refs_1_), channel_id=1, source_target_pairs={{0,16},{1,0},{2,1},{3,2},{19,3},{18,19},{17,18},{16,17},{4,20},{5,... | collective-permute-start | bytes 5505032 | tf_op jit(solution)/shard_map/ppermute | solution.py:20
  291.0 37.0 %collective-permute-start.14 = (bf16[1792,256]{1,0:T(8,128)(2,1)S(1)}, bf16[1792,256]{1,0:T(8,128)(2,1)S(1)}, u32[]{:S(2)}, u32[]{:S(2)}) collective-permute-start(bf16[1792,256]{1,0:T(8,128)(2,1)S(1)} %copy-done.10), channel_id=1, source_target_pairs={{0,1},{1,2},{2,3},{3,19},{19,18},{18,17},{17,16},{16,0},{4,5},{5,6... | collective-permute-start | bytes 2752520 | tf_op jit(solution)/shard_map/ppermute | solution.py:20
  292.6 37.7 %collective-permute-start.15 = (bf16[1792,256]{1,0:T(8,128)(2,1)S(1)}, bf16[1792,256]{1,0:T(8,128)(2,1)}, u32[]{:S(2)}, u32[]{:S(2)}) collective-permute-start(bf16[1792,256]{1,0:T(8,128)(2,1)S(1)} %copy-done.10), channel_id=1, source_target_pairs={{0,16},{1,0},{2,1},{3,2},{19,3},{18,19},{17,18},{16,17},{4,20},{5,... | collective-permute-start | bytes 2752520 | tf_op jit(solution)/shard_map/ppermute | solution.py:20
  310.6 42.6 %collective-permute-start.23 = (bf16[1792,256]{1,0:T(8,128)(2,1)S(1)}, bf16[1792,256]{1,0:T(8,128)(2,1)}, u32[]{:S(2)}, u32[]{:S(2)}) collective-permute-start(bf16[1792,256]{1,0:T(8,128)(2,1)S(1)} %collective-permute-done.20.refs_2_), channel_id=1, source_target_pairs={{0,1},{1,2},{2,3},{3,19},{19,18},{18,17},{17,16},{16,0},{4,5},{5,6... | collective-permute-start | bytes 2752520 | tf_op jit(solution)/shard_map/ppermute | solution.py:20
  312.2 41.0 %collective-permute-start.24 = (bf16[1792,256]{1,0:T(8,128)(2,1)S(1)}, bf16[1792,256]{1,0:T(8,128)(2,1)}, u32[]{:S(2)}, u32[]{:S(2)}) collective-permute-start(bf16[1792,256]{1,0:T(8,128)(2,1)S(1)} %collective-permute-done.21.refs_4_), channel_id=1, source_target_pairs={{0,16},{1,0},{2,1},{3,2},{19,3},{18,19},{17,18},{16,17},{4,20},{5,... | collective-permute-start | bytes 2752520 | tf_op jit(solution)/shard_map/ppermute | solution.py:20
  330.3 36.3 %collective-permute-start.18 = (bf16[1792,256]{1,0:T(8,128)(2,1)S(1)}, bf16[1792,256]{1,0:T(8,128)(2,1)}, u32[]{:S(2)}, u32[]{:S(2)}) collective-permute-start(bf16[1792,256]{1,0:T(8,128)(2,1)S(1)} %collective-permute-done.14.refs_1_), channel_id=1, source_target_pairs={{0,1},{1,2},{2,3},{3,19},{19,18},{18,17},{17,16},{16,0},{4,5},{5,6... | collective-permute-start | bytes 2752520 | tf_op jit(solution)/shard_map/ppermute | solution.py:20
  331.9 37.7 %collective-permute-start.19 = (bf16[1792,256]{1,0:T(8,128)(2,1)}, bf16[1792,256]{1,0:T(8,128)(2,1)}, u32[]{:S(2)}, u32[]{:S(2)}) collective-permute-start(bf16[1792,256]{1,0:T(8,128)(2,1)} %collective-permute-done.15.refs_3_), channel_id=1, source_target_pairs={{0,16},{1,0},{2,1},{3,2},{19,3},{18,19},{17,18},{16,17},{4,20},{5,... | collective-permute-start | bytes 2752520 | tf_op jit(solution)/shard_map/ppermute | solution.py:20
  371.2 41.6 %collective-permute-start.28 = (bf16[1792,256]{1,0:T(8,128)(2,1)}, bf16[1792,256]{1,0:T(8,128)(2,1)S(1)}, u32[]{:S(2)}, u32[]{:S(2)}) collective-permute-start(bf16[1792,256]{1,0:T(8,128)(2,1)} %collective-permute-done.23.refs_1_), channel_id=1, source_target_pairs={{0,1},{1,2},{2,3},{3,19},{19,18},{18,17},{17,16},{16,0},{4,5},{5,6... | collective-permute-start | bytes 2752520 | tf_op jit(solution)/shard_map/ppermute | solution.py:20
  372.8 40.0 %collective-permute-start.29 = (bf16[1792,256]{1,0:T(8,128)(2,1)}, bf16[1792,256]{1,0:T(8,128)(2,1)S(1)}, u32[]{:S(2)}, u32[]{:S(2)}) collective-permute-start(bf16[1792,256]{1,0:T(8,128)(2,1)} %collective-permute-done.19.refs_2_), channel_id=1, source_target_pairs={{0,16},{1,0},{2,1},{3,2},{19,3},{18,19},{17,18},{16,17},{4,20},{5,... | collective-permute-start | bytes 2752520 | tf_op jit(solution)/shard_map/ppermute | solution.py:20
  389.2 37.9 %collective-permute-start.27 = (bf16[1792,256]{1,0:T(8,128)(2,1)S(1)}, bf16[1792,256]{1,0:T(8,128)(2,1)S(1)}, u32[]{:S(2)}, u32[]{:S(2)}) collective-permute-start(bf16[1792,256]{1,0:T(8,128)(2,1)S(1)} %collective-permute-done.26.refs_3_), channel_id=1, source_target_pairs={{0,16},{1,0},{2,1},{3,2},{19,3},{18,19},{17,18},{16,17},{4,20},{5,... | collective-permute-start | bytes 2752520 | tf_op jit(solution)/shard_map/ppermute | solution.py:20
  (24 other events, 550.4 us)
Sparse Core Ops, SparseCore 0:
  8.9 96.7 all-gather.3
  107.2 94.0 all-gather.5
  202.8 94.0 all-gather.7

commit v7 on v6

--- a/solution.py
+++ b/solution.py
@@ -36,7 +36,10 @@
 
     def step(*tiles):
         here = pl.ds(pl.multiple_of(pl.program_id(0) * tm, tm), tm)
-        result = None if first else total[here, :]
+        if scale is None:
+            result = None if first else total[here, :]
+        else:
+            result = total[:, here]
         at = 0
         for (wides, *_), right in zip(units, tiles[many : many + count]):
             left = [t[...] for t in tiles[at : at + len(wides)]]
@@ -53,13 +56,21 @@
 
     def place(wides, which, parts, part):
         wide = sum(wides)
+        if scale is not None:
+            return pl.BlockSpec((tm, wide), lambda i: (i, blocks_ref[which] * parts + part))
         return pl.BlockSpec((across, wide), lambda i: (0, blocks_ref[which] * parts + part))
 
-    specs = [pl.BlockSpec((tm, wide), lambda i: (i, 0)) for wides, *_ in units for wide in wides]
+    all_wides = [wide for wides, *_ in units for wide in wides]
+    if scale is None:
+        specs = [pl.BlockSpec((tm, wide), lambda i: (i, 0)) for wide in all_wides]
+        steps = rows // tm
+    else:
+        specs = [pl.BlockSpec((rows, wide), lambda i: (0, 0)) for wide in all_wides]
+        steps = across // tm
     specs += [place(*u) for u in units]
-    result_specs = [] if scale is None else [pl.BlockSpec((tm, across), lambda i: (i, 0))]
+    result_specs = [] if scale is None else [pl.BlockSpec((rows, tm), lambda i: (0, i))]
     results = [] if scale is None else [out]
-    pltpu.emit_pipeline(step, grid=(rows // tm,), in_specs=specs, out_specs=result_specs)(
+    pltpu.emit_pipeline(step, grid=(steps,), in_specs=specs, out_specs=result_specs)(
         *lefts, *rights, *results
     )
 
@@ -91,7 +102,7 @@
     else:
         shape = pltpu.VMEM((rows, across), jnp.float32)
     return pl.pallas_call(
-        functools.partial(add_terms_body, plan, first, scale, tile(rows, 256)),
+        functools.partial(add_terms_body, plan, first, scale, tile(across if last else rows, 256)),
         in_specs=[pl.BlockSpec(memory_space=pltpu.SMEM)] + in_specs,
         out_specs=[
             pl.BlockSpec(memory_space=pl.ANY if last else pltpu.VMEM),

time: 446 us -> 446 us (level)
  no operation moved by 1% of the time
where the time goes in v7:
time: 446 us; the launch traced here: 445 us
  waiting for transfers between devices  239 us (54%)
  Pallas kernels  135 us (30%)
  starting transfers between devices  31.2 us (7%)
  local copies, waits for them, and re-layouts  27.2 us (6%)
  between operations  13.3 us (3%)
    ppermute x30, waiting for transfers between devices, pass_on(): return lax.ppermute(value, ('run', 'grp'), pairs)  202 us
    pallas_call x9, Pallas kernels, add_terms(): pl.pallas_call(functools.partial(add_terms_body, plan, first, scale, tile...  135 us
    all_gather x3, waiting for transfers between devices, local(): lax.all_gather(b, 'blk', axis=1, tiled=True)  34.8 us
    ppermute x30, starting transfers between devices, pass_on(): return lax.ppermute(value, ('run', 'grp'), pairs)  31.1 us
    unnamed x30, local copies, waits for them, and re-layouts  20.8 us
  transfers between devices with their start and end apart: 33, of which 22 were waited for; matrix products, arithmetic and copies ran while one was open for 1% of the time, Pallas kernels for 28%

profile of v7, /device:TPU:0, one launch (start us, length us, event | category | flops | bytes accessed | tf_op | source)
XLA Modules:
  0.0 445.4 jit_solution(7711714255052219661)
XLA Ops:
  13.9 39.0 %collective-permute-done.7.refs_3_ = bf16[1792,512]{1,0:T(8,128)(2,1)} collective-permute-done((bf16[1792,512]{1,0:T(8,128)(2,1)}, bf16[1792,512]{1,0:T(8,128)(2,1)}, u32[]{:S(2)}, u32[]{:S(2)}) %collective-permute-start.7) | collective-permute-done | bytes 1835040 | tf_op jit(solution)/shard_map/ppermute | solution.py:20
  55.1 37.1 %collective-permute-done.refs_1_ = bf16[1792,512]{1,0:T(8,128)(2,1)} collective-permute-done((bf16[1792,512]{1,0:T(8,128)(2,1)}, bf16[1792,512]{1,0:T(8,128)(2,1)}, u32[]{:S(2)}, u32[]{:S(2)}) %collective-permute-start) | collective-permute-done | bytes 1835040 | tf_op jit(solution)/shard_map/ppermute | solution.py:20
  97.0 8.6 %all-gather.4.cloned.1.call-done.refs_3_.refs_4_.refs_5_ = bf16[1792,4096]{1,0:T(8,128)(2,1)} async-done(((bf16[1792,1024]{1,0:T(8,128)(2,1)}), bf16[1792,4096]{1,0:T(8,128)(2,1)}) %all-gather.4.cloned.1.call-update) | async-done | bytes 14680080 | tf_op jit(solution)/shard_map/all_gather | solution.py:132
  105.7 15.2 %shard_map.73 = (f32[1792,1792]{1,0:T(8,128)S(1)}, f32[8,128]{1,0:T(8,128)}) custom-call(s32[8]{0:T(128)} %dynamic-slice_bitcast_fusion.blocks_ref, bf16[1792,512]{1,0:T(8,128)(2,1)} %refs_0_.2, bf16[1792,512]{1,0:T(8,128)(2,1)} %collective-permute-done.refs_1_, bf16[1792,512]{1,0:T(8,128)(2,1)} %collective-permute-done.2.refs_2_, ...), custom_call_target="tpu_custom_call" | custom-call | flops 9865003008 | bytes 11010048 | tf_op jit(solution)/shard_map/pallas_call | solution.py:104
  120.9 5.4 %copy-done = f32[1792,1792]{1,0:T(8,128)} copy-done((f32[1792,1792]{1,0:T(8,128)}, f32[1792,1792]{1,0:T(8,128)S(1)}, u32[]{:S(2)}) %copy-start) | copy-done | bytes 12845080
  126.3 5.2 %collective-permute-done.8.refs_1_ = bf16[1792,512]{1,0:T(8,128)(2,1)} collective-permute-done((bf16[1792,512]{1,0:T(8,128)(2,1)}, bf16[1792,512]{1,0:T(8,128)(2,1)}, u32[]{:S(2)}, u32[]{:S(2)}) %collective-permute-start.8) | collective-permute-done | bytes 1835040 | tf_op jit(solution)/shard_map/ppermute | solution.py:20
  135.8 35.1 %collective-permute-done.1.refs_0_ = bf16[1792,512]{1,0:T(8,128)(2,1)} collective-permute-done((bf16[1792,512]{1,0:T(8,128)(2,1)}, bf16[1792,512]{1,0:T(8,128)(2,1)}, u32[]{:S(2)}, u32[]{:S(2)}) %collective-permute-start.1) | collective-permute-done | bytes 1835040 | tf_op jit(solution)/shard_map/ppermute | solution.py:20
  175.1 26.2 %all-gather.6.cloned.1.call-done.refs_6_.refs_7_.refs_3_.refs_4_.refs_5_ = bf16[1792,4096]{1,0:T(8,128)(2,1)} async-done(((bf16[1792,1024]{1,0:T(8,128)(2,1)}), bf16[1792,4096]{1,0:T(8,128)(2,1)}) %all-gather.6.cloned.1.call-update) | async-done | bytes 14680080 | tf_op jit(solution)/shard_map/all_gather | solution.py:132
  201.3 4.6 %copy-done.1 = f32[1792,1792]{1,0:T(8,128)S(1)} copy-done((f32[1792,1792]{1,0:T(8,128)S(1)}, f32[1792,1792]{1,0:T(8,128)}, u32[]{:S(2)}) %copy-start.1) | copy-done | bytes 12845080
  205.9 20.6 %shard_map.74 = (f32[1792,1792]{1,0:T(8,128)S(1)}, f32[8,128]{1,0:T(8,128)}) custom-call(s32[8]{0:T(128)} %dynamic-slice_bitcast_fusion.blocks_ref, bf16[1792,512]{1,0:T(8,128)(2,1)} %collective-permute-done.1.refs_0_, bf16[1792,512]{1,0:T(8,128)(2,1)} %collective-permute-done.3.refs_1_, bf16[1792,512]{1,0:T(8,128)(2,1)} %refs_2_.1, ...), custom_call_target="tpu_custom_call", output_to_operand_aliasing={{0}: (9, {})} | custom-call | flops 13153337344 | bytes 14680064 | tf_op jit(solution)/shard_map/pallas_call | solution.py:104
  226.6 15.9 %shard_map.75 = (f32[1792,1792]{1,0:T(8,128)S(1)}, f32[8,128]{1,0:T(8,128)}) custom-call(s32[8]{0:T(128)} %dynamic-slice_bitcast_fusion.blocks_ref, bf16[1792,512]{1,0:T(8,128)(2,1)} %collective-permute-done.6.refs_0_, bf16[1792,512]{1,0:T(8,128)(2,1)} %collective-permute-done.8.refs_1_, ...), custom_call_target="tpu_custom_call", output_to_operand_aliasing={{0}: (7, {})} | custom-call | flops 9865003008 | bytes 11010048 | tf_op jit(solution)/shard_map/pallas_call | solution.py:104
  256.3 20.0 %shard_map.76 = (f32[1792,1792]{1,0:T(8,128)S(1)}, f32[8,128]{1,0:T(8,128)}) custom-call(s32[8]{0:T(128)} %dynamic-slice_bitcast_fusion.blocks_ref, bf16[1792,512]{1,0:T(8,128)(2,1)} %collective-permute-done.4.refs_0_, bf16[1792,512]{1,0:T(8,128)(2,1)} %collective-permute-done.5.refs_1_, ...), custom_call_target="tpu_custom_call", output_to_operand_aliasing={{0}: (9, {})} | custom-call | flops 13153337344 | bytes 14680064 | tf_op jit(solution)/shard_map/pallas_call | solution.py:104
  278.4 10.4 %collective-permute-done.10.refs_0_ = bf16[1792,256]{1,0:T(8,128)(2,1)} collective-permute-done((bf16[1792,256]{1,0:T(8,128)(2,1)S(1)}, bf16[1792,256]{1,0:T(8,128)(2,1)}, u32[]{:S(2)}, u32[]{:S(2)}) %collective-permute-start.10) | collective-permute-done | bytes 917536 | tf_op jit(solution)/shard_map/ppermute | solution.py:20
  293.1 12.2 %shard_map.77 = (f32[1792,1792]{1,0:T(8,128)S(1)}, f32[8,128]{1,0:T(8,128)}) custom-call(s32[8]{0:T(128)} %dynamic-slice_bitcast_fusion.blocks_ref, bf16[1792,256]{1,0:T(8,128)(2,1)} %collective-permute-done.10.refs_0_, bf16[1792,256]{1,0:T(8,128)(2,1)} %collective-permute-done.11.refs_1_, ...), custom_call_target="tpu_custom_call", output_to_operand_aliasing={{0}: (7, {})} | custom-call | flops 6576668672 | bytes 7340032 | tf_op jit(solution)/shard_map/pallas_call | solution.py:104
  305.3 4.9 %copy-done.2 = f32[1792,1792]{1,0:T(8,128)} copy-done((f32[1792,1792]{1,0:T(8,128)}, f32[1792,1792]{1,0:T(8,128)S(1)}, u32[]{:S(2)}) %copy-start.2) | copy-done | bytes 12845080
  312.6 15.5 %collective-permute-done.14.refs_1_ = bf16[1792,256]{1,0:T(8,128)(2,1)S(1)} collective-permute-done((bf16[1792,256]{1,0:T(8,128)(2,1)S(1)}, bf16[1792,256]{1,0:T(8,128)(2,1)S(1)}, u32[]{:S(2)}, u32[]{:S(2)}) %collective-permute-start.14) | collective-permute-done | bytes 917536 | tf_op jit(solution)/shard_map/ppermute | solution.py:20
  332.4 4.6 %copy-done.3 = f32[1792,1792]{1,0:T(8,128)S(1)} copy-done((f32[1792,1792]{1,0:T(8,128)S(1)}, f32[1792,1792]{1,0:T(8,128)}, u32[]{:S(2)}) %copy-start.3) | copy-done | bytes 12845080
  337.0 16.1 %shard_map.78 = (f32[1792,1792]{1,0:T(8,128)S(1)}, f32[8,128]{1,0:T(8,128)}) custom-call(s32[8]{0:T(128)} %dynamic-slice_bitcast_fusion.blocks_ref, bf16[1792,512]{1,0:T(8,128)(2,1)} %refs_0_.3, bf16[1792,256]{1,0:T(8,128)(2,1)} %copy-done.9, bf16[1792,256]{1,0:T(8,128)(2,1)} %copy-done.7, ...), custom_call_target="tpu_custom_call", output_to_operand_aliasing={{0}: (9, {})} | custom-call | flops 9865003008 | bytes 11010048 | tf_op jit(solution)/shard_map/pallas_call | solution.py:104
  353.2 13.4 %collective-permute-done.18.refs_0_ = bf16[1792,256]{1,0:T(8,128)(2,1)} collective-permute-done((bf16[1792,256]{1,0:T(8,128)(2,1)S(1)}, bf16[1792,256]{1,0:T(8,128)(2,1)}, u32[]{:S(2)}, u32[]{:S(2)}) %collective-permute-start.18) | collective-permute-done | bytes 917536 | tf_op jit(solution)/shard_map/ppermute | solution.py:20
  373.3 12.2 %shard_map.79 = (f32[1792,1792]{1,0:T(8,128)S(1)}, f32[8,128]{1,0:T(8,128)}) custom-call(s32[8]{0:T(128)} %dynamic-slice_bitcast_fusion.blocks_ref, bf16[1792,256]{1,0:T(8,128)(2,1)} %collective-permute-done.18.refs_0_, bf16[1792,256]{1,0:T(8,128)(2,1)} %collective-permute-done.23.refs_1_, ...), custom_call_target="tpu_custom_call", output_to_operand_aliasing={{0}: (7, {})} | custom-call | flops 6576668672 | bytes 7340032 | tf_op jit(solution)/shard_map/pallas_call | solution.py:104
  389.2 3.9 collective-permute-done.22.refs_0_
  394.7 18.1 %collective-permute-done.28.refs_1_ = bf16[1792,256]{1,0:T(8,128)(2,1)S(1)} collective-permute-done((bf16[1792,256]{1,0:T(8,128)(2,1)}, bf16[1792,256]{1,0:T(8,128)(2,1)S(1)}, u32[]{:S(2)}, u32[]{:S(2)}) %collective-permute-start.28) | collective-permute-done | bytes 917536 | tf_op jit(solution)/shard_map/ppermute | solution.py:20
  414.1 12.3 %shard_map.80 = (f32[1792,1792]{1,0:T(8,128)S(1)}, f32[8,128]{1,0:T(8,128)}) custom-call(s32[8]{0:T(128)} %dynamic-slice_bitcast_fusion.blocks_ref, bf16[1792,256]{1,0:T(8,128)(2,1)} %copy-done.12, bf16[1792,256]{1,0:T(8,128)(2,1)} %copy-done.13, bf16[1792,256]{1,0:T(8,128)(2,1)} %copy-done.14, ...), custom_call_target="tpu_custom_call", output_to_operand_aliasing={{0}: (7, {})} | custom-call | flops 6576668672 | bytes 7340032 | tf_op jit(solution)/shard_map/pallas_call | solution.py:104
  428.6 10.3 %shard_map.81 = (f32[1792,1792]{1,0:T(8,128)}, f32[8,128]{1,0:T(8,128)}) custom-call(s32[8]{0:T(128)S(1)} %copy-done.4, bf16[1792,256]{1,0:T(8,128)(2,1)S(1)} %collective-permute-done.25.refs_0_, bf16[1792,256]{1,0:T(8,128)(2,1)S(1)} %collective-permute-done.27.refs_1_, ...), custom_call_target="tpu_custom_call" | custom-call | flops 3288334336 | bytes 3670016 | tf_op jit(solution)/shard_map/pallas_call | solution.py:104
  (90 shorter events, 65.0 us)
Async XLA Ops:
  6.5 99.1 %all-gather.4.cloned.1.call-start = ((), (), s32[]{:S(2)}) async-start(), calls=%async_computation | async-start | bytes 18350080 | tf_op jit(solution)/shard_map/all_gather | solution.py:132
  7.3 194.0 %all-gather.6.cloned.1.call-start = ((), (), s32[]{:S(2)}) async-start(), calls=%async_computation.1 | async-start | bytes 18350080 | tf_op jit(solution)/shard_map/all_gather | solution.py:132
  8.0 324.4 %all-gather.8.cloned.1.call-start = ((), (), s32[]{:S(2)}) async-start(), calls=%async_computation.2 | async-start | bytes 18350080 | tf_op jit(solution)/shard_map/all_gather | solution.py:132
  8.8 44.1 %collective-permute-start.7 = (bf16[1792,512]{1,0:T(8,128)(2,1)}, bf16[1792,512]{1,0:T(8,128)(2,1)}, u32[]{:S(2)}, u32[]{:S(2)}) collective-permute-start(bf16[1792,512]{1,0:T(8,128)(2,1)} %refs_2_.1), channel_id=1, source_target_pairs={{0,1},{1,2},{2,3},{3,19},{19,18},{18,17},{17,16},{16,0},{4,5},{5,6... | collective-permute-start | bytes 5505032 | tf_op jit(solution)/shard_map/ppermute | solution.py:20
  11.8 43.3 %collective-permute-start.6 = (bf16[1792,512]{1,0:T(8,128)(2,1)}, bf16[1792,512]{1,0:T(8,128)(2,1)}, u32[]{:S(2)}, u32[]{:S(2)}) collective-permute-start(bf16[1792,512]{1,0:T(8,128)(2,1)} %refs_2_.1), channel_id=1, source_target_pairs={{0,16},{1,0},{2,1},{3,2},{19,3},{18,19},{17,18},{16,17},{4,20},{5,... | collective-permute-start | bytes 5505032 | tf_op jit(solution)/shard_map/ppermute | solution.py:20
  11.8 80.4 %collective-permute-start = (bf16[1792,512]{1,0:T(8,128)(2,1)}, bf16[1792,512]{1,0:T(8,128)(2,1)}, u32[]{:S(2)}, u32[]{:S(2)}) collective-permute-start(bf16[1792,512]{1,0:T(8,128)(2,1)} %refs_0_.2), channel_id=1, source_target_pairs={{0,1},{1,2},{2,3},{3,19},{19,18},{18,17},{17,16},{16,0},{4,5},{5,6... | collective-permute-start | bytes 5505032 | tf_op jit(solution)/shard_map/ppermute | solution.py:20
  13.9 80.5 %collective-permute-start.2 = (bf16[1792,512]{1,0:T(8,128)(2,1)}, bf16[1792,512]{1,0:T(8,128)(2,1)}, u32[]{:S(2)}, u32[]{:S(2)}) collective-permute-start(bf16[1792,512]{1,0:T(8,128)(2,1)} %refs_0_.2), channel_id=1, source_target_pairs={{0,16},{1,0},{2,1},{3,2},{19,3},{18,19},{17,18},{16,17},{4,20},{5,... | collective-permute-start | bytes 5505032 | tf_op jit(solution)/shard_map/ppermute | solution.py:20
  52.9 78.6 %collective-permute-start.8 = (bf16[1792,512]{1,0:T(8,128)(2,1)}, bf16[1792,512]{1,0:T(8,128)(2,1)}, u32[]{:S(2)}, u32[]{:S(2)}) collective-permute-start(bf16[1792,512]{1,0:T(8,128)(2,1)} %collective-permute-done.7.refs_3_), channel_id=1, source_target_pairs={{0,1},{1,2},{2,3},{3,19},{19,18},{18,17},{17,16},{16,0},{4,5},{5,6... | collective-permute-start | bytes 5505032 | tf_op jit(solution)/shard_map/ppermute | solution.py:20
  55.1 78.6 %collective-permute-start.9 = (bf16[1792,512]{1,0:T(8,128)(2,1)}, bf16[1792,512]{1,0:T(8,128)(2,1)}, u32[]{:S(2)}, u32[]{:S(2)}) collective-permute-start(bf16[1792,512]{1,0:T(8,128)(2,1)} %collective-permute-done.6.refs_0_), channel_id=1, source_target_pairs={{0,16},{1,0},{2,1},{3,2},{19,3},{18,19},{17,18},{16,17},{4,20},{5,... | collective-permute-start | bytes 5505032 | tf_op jit(solution)/shard_map/ppermute | solution.py:20
  92.2 78.6 %collective-permute-start.1 = (bf16[1792,512]{1,0:T(8,128)(2,1)}, bf16[1792,512]{1,0:T(8,128)(2,1)}, u32[]{:S(2)}, u32[]{:S(2)}) collective-permute-start(bf16[1792,512]{1,0:T(8,128)(2,1)} %collective-permute-done.refs_1_), channel_id=1, source_target_pairs={{0,1},{1,2},{2,3},{3,19},{19,18},{18,17},{17,16},{16,0},{4,5},{5,6... | collective-permute-start | bytes 5505032 | tf_op jit(solution)/shard_map/ppermute | solution.py:20
  94.4 78.6 %collective-permute-start.3 = (bf16[1792,512]{1,0:T(8,128)(2,1)}, bf16[1792,512]{1,0:T(8,128)(2,1)}, u32[]{:S(2)}, u32[]{:S(2)}) collective-permute-start(bf16[1792,512]{1,0:T(8,128)(2,1)} %collective-permute-done.2.refs_2_), channel_id=1, source_target_pairs={{0,16},{1,0},{2,1},{3,2},{19,3},{18,19},{17,18},{16,17},{4,20},{5,... | collective-permute-start | bytes 5505032 | tf_op jit(solution)/shard_map/ppermute | solution.py:20
  133.7 108.8 %collective-permute-start.12 = (bf16[1792,512]{1,0:T(8,128)(2,1)}, bf16[1792,512]{1,0:T(8,128)(2,1)S(1)}, u32[]{:S(2)}, u32[]{:S(2)}) collective-permute-start(bf16[1792,512]{1,0:T(8,128)(2,1)} %collective-permute-done.8.refs_1_), channel_id=1, source_target_pairs={{0,1},{1,2},{2,3},{3,19},{19,18},{18,17},{17,16},{16,0},{4,5},{5,6... | collective-permute-start | bytes 5505032 | tf_op jit(solution)/shard_map/ppermute | solution.py:20
  135.3 107.2 %collective-permute-start.13 = (bf16[1792,512]{1,0:T(8,128)(2,1)}, bf16[1792,512]{1,0:T(8,128)(2,1)}, u32[]{:S(2)}, u32[]{:S(2)}) collective-permute-start(bf16[1792,512]{1,0:T(8,128)(2,1)} %collective-permute-done.9.refs_2_), channel_id=1, source_target_pairs={{0,16},{1,0},{2,1},{3,2},{19,3},{18,19},{17,18},{16,17},{4,20},{5,... | collective-permute-start | bytes 5505032 | tf_op jit(solution)/shard_map/ppermute | solution.py:20
  173.1 76.5 %collective-permute-start.4 = (bf16[1792,512]{1,0:T(8,128)(2,1)}, bf16[1792,512]{1,0:T(8,128)(2,1)}, u32[]{:S(2)}, u32[]{:S(2)}) collective-permute-start(bf16[1792,512]{1,0:T(8,128)(2,1)} %collective-permute-done.1.refs_0_), channel_id=1, source_target_pairs={{0,1},{1,2},{2,3},{3,19},{19,18},{18,17},{17,16},{16,0},{4,5},{5,6... | collective-permute-start | bytes 5505032 | tf_op jit(solution)/shard_map/ppermute | solution.py:20
  174.6 77.1 %collective-permute-start.5 = (bf16[1792,512]{1,0:T(8,128)(2,1)}, bf16[1792,512]{1,0:T(8,128)(2,1)}, u32[]{:S(2)}, u32[]{:S(2)}) collective-permute-start(bf16[1792,512]{1,0:T(8,128)(2,1)} %collective-permute-done.3.refs_1_), channel_id=1, source_target_pairs={{0,16},{1,0},{2,1},{3,2},{19,3},{18,19},{17,18},{16,17},{4,20},{5,... | collective-permute-start | bytes 5505032 | tf_op jit(solution)/shard_map/ppermute | solution.py:20
  291.0 37.0 %collective-permute-start.14 = (bf16[1792,256]{1,0:T(8,128)(2,1)S(1)}, bf16[1792,256]{1,0:T(8,128)(2,1)S(1)}, u32[]{:S(2)}, u32[]{:S(2)}) collective-permute-start(bf16[1792,256]{1,0:T(8,128)(2,1)S(1)} %copy-done.10), channel_id=1, source_target_pairs={{0,1},{1,2},{2,3},{3,19},{19,18},{18,17},{17,16},{16,0},{4,5},{5,6... | collective-permute-start | bytes 2752520 | tf_op jit(solution)/shard_map/ppermute | solution.py:20
  292.6 37.7 %collective-permute-start.15 = (bf16[1792,256]{1,0:T(8,128)(2,1)S(1)}, bf16[1792,256]{1,0:T(8,128)(2,1)}, u32[]{:S(2)}, u32[]{:S(2)}) collective-permute-start(bf16[1792,256]{1,0:T(8,128)(2,1)S(1)} %copy-done.10), channel_id=1, source_target_pairs={{0,16},{1,0},{2,1},{3,2},{19,3},{18,19},{17,18},{16,17},{4,20},{5,... | collective-permute-start | bytes 2752520 | tf_op jit(solution)/shard_map/ppermute | solution.py:20
  310.6 42.6 %collective-permute-start.23 = (bf16[1792,256]{1,0:T(8,128)(2,1)S(1)}, bf16[1792,256]{1,0:T(8,128)(2,1)}, u32[]{:S(2)}, u32[]{:S(2)}) collective-permute-start(bf16[1792,256]{1,0:T(8,128)(2,1)S(1)} %collective-permute-done.20.refs_2_), channel_id=1, source_target_pairs={{0,1},{1,2},{2,3},{3,19},{19,18},{18,17},{17,16},{16,0},{4,5},{5,6... | collective-permute-start | bytes 2752520 | tf_op jit(solution)/shard_map/ppermute | solution.py:20
  312.2 41.0 %collective-permute-start.24 = (bf16[1792,256]{1,0:T(8,128)(2,1)S(1)}, bf16[1792,256]{1,0:T(8,128)(2,1)}, u32[]{:S(2)}, u32[]{:S(2)}) collective-permute-start(bf16[1792,256]{1,0:T(8,128)(2,1)S(1)} %collective-permute-done.21.refs_4_), channel_id=1, source_target_pairs={{0,16},{1,0},{2,1},{3,2},{19,3},{18,19},{17,18},{16,17},{4,20},{5,... | collective-permute-start | bytes 2752520 | tf_op jit(solution)/shard_map/ppermute | solution.py:20
  330.3 36.3 %collective-permute-start.18 = (bf16[1792,256]{1,0:T(8,128)(2,1)S(1)}, bf16[1792,256]{1,0:T(8,128)(2,1)}, u32[]{:S(2)}, u32[]{:S(2)}) collective-permute-start(bf16[1792,256]{1,0:T(8,128)(2,1)S(1)} %collective-permute-done.14.refs_1_), channel_id=1, source_target_pairs={{0,1},{1,2},{2,3},{3,19},{19,18},{18,17},{17,16},{16,0},{4,5},{5,6... | collective-permute-start | bytes 2752520 | tf_op jit(solution)/shard_map/ppermute | solution.py:20
  331.9 37.7 %collective-permute-start.19 = (bf16[1792,256]{1,0:T(8,128)(2,1)}, bf16[1792,256]{1,0:T(8,128)(2,1)}, u32[]{:S(2)}, u32[]{:S(2)}) collective-permute-start(bf16[1792,256]{1,0:T(8,128)(2,1)} %collective-permute-done.15.refs_3_), channel_id=1, source_target_pairs={{0,16},{1,0},{2,1},{3,2},{19,3},{18,19},{17,18},{16,17},{4,20},{5,... | collective-permute-start | bytes 2752520 | tf_op jit(solution)/shard_map/ppermute | solution.py:20
  371.2 41.6 %collective-permute-start.28 = (bf16[1792,256]{1,0:T(8,128)(2,1)}, bf16[1792,256]{1,0:T(8,128)(2,1)S(1)}, u32[]{:S(2)}, u32[]{:S(2)}) collective-permute-start(bf16[1792,256]{1,0:T(8,128)(2,1)} %collective-permute-done.23.refs_1_), channel_id=1, source_target_pairs={{0,1},{1,2},{2,3},{3,19},{19,18},{18,17},{17,16},{16,0},{4,5},{5,6... | collective-permute-start | bytes 2752520 | tf_op jit(solution)/shard_map/ppermute | solution.py:20
  372.8 40.0 %collective-permute-start.29 = (bf16[1792,256]{1,0:T(8,128)(2,1)}, bf16[1792,256]{1,0:T(8,128)(2,1)S(1)}, u32[]{:S(2)}, u32[]{:S(2)}) collective-permute-start(bf16[1792,256]{1,0:T(8,128)(2,1)} %collective-permute-done.19.refs_2_), channel_id=1, source_target_pairs={{0,16},{1,0},{2,1},{3,2},{19,3},{18,19},{17,18},{16,17},{4,20},{5,... | collective-permute-start | bytes 2752520 | tf_op jit(solution)/shard_map/ppermute | solution.py:20
  389.2 37.9 %collective-permute-start.27 = (bf16[1792,256]{1,0:T(8,128)(2,1)S(1)}, bf16[1792,256]{1,0:T(8,128)(2,1)S(1)}, u32[]{:S(2)}, u32[]{:S(2)}) collective-permute-start(bf16[1792,256]{1,0:T(8,128)(2,1)S(1)} %collective-permute-done.26.refs_3_), channel_id=1, source_target_pairs={{0,16},{1,0},{2,1},{3,2},{19,3},{18,19},{17,18},{16,17},{4,20},{5,... | collective-permute-start | bytes 2752520 | tf_op jit(solution)/shard_map/ppermute | solution.py:20
  (24 other events, 550.4 us)
Sparse Core Ops, SparseCore 0:
  8.9 96.7 all-gather.3
  107.2 94.0 all-gather.5
  202.8 94.0 all-gather.7
